TPU v7x, 512 devices: a whole 4x4x16 slice. The times are simulated.
512 devices in a mesh: row: 16 (over x, y), col: 32 (over z, core).
Axes of the slice: x: 4, y: 4, z: 16, core: 2. Of those that a mesh axis runs over, the one named last changes fastest.
Arguments:
- object_field: float32 [2, 4096, 8192], P(None, 'row', 'col')
- probe_field: float32 [2, 256, 256], replicated, may hold values from -6 to 6
- object_dir_prev: float32 [2, 4096, 8192], P(None, 'row', 'col')
- probe_dir_prev: float32 [2, 256, 256], replicated, may hold values from -6 to 6
- prev_norm: float32 [], replicated, may hold values from 33554432 to 134217728
- intensities: bfloat16 [16, 32, 4, 256, 256], P('row', 'col'), may hold values from 0 to 1.5
- positions: int32 [16, 32, 4, 2], P('row', 'col'), may hold values from 0 to 8191, as said below
- counts: int32 [16, 32], P('row'), may hold values from 0 to 4, as said below
Outputs:
- object_new: float32 [2, 4096, 8192], P(None, 'row', 'col')
- probe_new: float32 [2, 256, 256], replicated
- object_direction: float32 [2, 4096, 8192], P(None, 'row', 'col')
- probe_direction: float32 [2, 256, 256], replicated
- grad_norm: float32 [], replicated
- frame_curvature: float32 [16, 32, 4], P('row', 'col')
Inputs may be any that keep to these rules, and one draw needn't show every extreme that they name: positions[i, j] lie in tile (i, j): rows i * 256 to (i + 1) * 256 - 1 and columns j * 256 to (j + 1) * 256 - 1. The devices of column indices 2 k and 2 k + 1 of one row hold at most 4 live frames together; a device's live slots are its first counts[i, j].
All inputs are finite; a program needn't handle non-finite values.
Results may differ from a plain program's by a relative error of at most 0.0003.
Values sent between devices are 32-bit elements; how exact they have to be, the bound alone decides.
No kernel may reach another device: no remote copies, remote signals or barrier semaphores. Data moves between devices by JAX's collectives and lax.ppermute only.
A program may use at most 64 MiB of HBM per device.

v0:
```python
import math

import jax
import jax.numpy as jnp
from jax import lax
from jax.sharding import PartitionSpec as P


def passed_along(shard, axis, by):
    count = lax.axis_size(axis)
    pairs = [(i, i + by) for i in range(count) if 0 <= i + by < count]
    return lax.ppermute(shard, axis, pairs)


def dft_tables(frame_width):
    rows_i = lax.broadcasted_iota(jnp.int32, (frame_width, frame_width), 0)
    cols_i = lax.broadcasted_iota(jnp.int32, (frame_width, frame_width), 1)
    phases = (rows_i * cols_i % frame_width).astype(jnp.float32) * (2.0 * math.pi / frame_width)
    factor = 1.0 / math.sqrt(frame_width)
    return (jnp.cos(phases) * factor, jnp.sin(phases) * factor)


def unitary_dft(frames, cosine, sine_table, orient):
    precise = lax.Precision.HIGHEST
    left_c = jnp.einsum("jk,bckl->bcjl", cosine, frames, precision=precise)
    left_s = jnp.einsum("jk,bckl->bcjl", sine_table, frames, precision=precise)
    middle = jnp.stack(
        [left_c[:, 0] + orient * left_s[:, 1], left_c[:, 1] - orient * left_s[:, 0]], axis=1
    )
    right_c = jnp.einsum("bcjk,kl->bcjl", middle, cosine, precision=precise)
    right_s = jnp.einsum("bcjk,kl->bcjl", middle, sine_table, precision=precise)
    return jnp.stack(
        [right_c[:, 0] + orient * right_s[:, 1], right_c[:, 1] - orient * right_s[:, 0]], axis=1
    )


def complex_times(left, right):
    real_out = left[..., 0, :, :] * right[..., 0, :, :] - left[..., 1, :, :] * right[..., 1, :, :]
    imag_out = left[..., 0, :, :] * right[..., 1, :, :] + left[..., 1, :, :] * right[..., 0, :, :]
    return jnp.stack([real_out, imag_out], axis=-3)


def conj_times(left, right):
    real_out = left[..., 0, :, :] * right[..., 0, :, :] + left[..., 1, :, :] * right[..., 1, :, :]
    imag_out = left[..., 0, :, :] * right[..., 1, :, :] - left[..., 1, :, :] * right[..., 0, :, :]
    return jnp.stack([real_out, imag_out], axis=-3)


def extend_object(tile_vals):
    lower_rim = passed_along(tile_vals, "row", -1)
    stacked = jnp.concatenate([tile_vals, lower_rim], axis=1)
    right_rim = passed_along(stacked, "col", -1)
    return jnp.concatenate([stacked, right_rim], axis=2)


def extend_direction(tile_vals):
    lower_rim = passed_along(tile_vals, "row", -1)
    stacked = jnp.concatenate([tile_vals, lower_rim], axis=1)
    right_rim = passed_along(stacked, "col", -1)
    return jnp.concatenate([stacked, right_rim], axis=2)


def fold_back(spread, tile_rows, tile_cols, frame_width):
    from_left = passed_along(spread[:, :, tile_cols:], "col", 1)
    owned = spread[:, :, :tile_cols].at[:, :, :frame_width].add(from_left)
    from_above = passed_along(owned[:, tile_rows:, :], "row", 1)
    return owned[:, :tile_rows, :].at[:, :frame_width, :].add(from_above)


def cut_patches(extended, offsets_r, offsets_c, frame_width):

    def one_patch(row_off, col_off):
        return lax.dynamic_slice(extended, (0, row_off, col_off), (2, frame_width, frame_width))

    return jax.vmap(one_patch)(offsets_r, offsets_c)


def accumulate(contrib, offsets_r, offsets_c, grid_shape):

    def add_one(slot_at, grid):
        piece = contrib[slot_at]
        anchor = (0, offsets_r[slot_at], offsets_c[slot_at])
        current = lax.dynamic_slice(grid, anchor, piece.shape)
        return lax.dynamic_update_slice(grid, current + piece, anchor)

    return lax.fori_loop(0, contrib.shape[0], add_one, jnp.zeros(grid_shape, jnp.float32))


def gradient_frames(waves, measure, cosine, sine_table):
    far_field = unitary_dft(waves, cosine, sine_table, 1.0)
    residue = far_field[:, 0] * far_field[:, 0] + far_field[:, 1] * far_field[:, 1] - measure
    backward = unitary_dft(far_field * residue[:, None], cosine, sine_table, -1.0)
    return (backward, far_field)


def per_device(
    object_field,
    probe_field,
    object_dir_prev,
    probe_dir_prev,
    prev_norm,
    intensities,
    positions,
    counts,
):
    tile_rows = object_field.shape[1]
    tile_cols = object_field.shape[2]
    frame_width = probe_field.shape[-1]
    slot_count = positions.shape[2]
    row_at = lax.axis_index("row")
    col_at = lax.axis_index("col")
    cosine, sine_table = dft_tables(frame_width)
    offsets_r = positions[0, 0, :, 0] - row_at * tile_rows
    offsets_c = positions[0, 0, :, 1] - col_at * tile_cols
    row_counts = counts[0]
    own_count = lax.dynamic_index_in_dim(row_counts, col_at, 0, keepdims=False)
    slot_ids = jnp.arange(slot_count, dtype=jnp.int32)
    live_mask = (slot_ids < own_count).astype(jnp.float32)
    extended = extend_object(object_field)
    patches = cut_patches(extended, offsets_r, offsets_c, frame_width)
    waves = complex_times(probe_field, patches) * live_mask[:, None, None, None]
    measure = intensities[0, 0].astype(jnp.float32) * live_mask[:, None, None]
    backward, far_kept = gradient_frames(waves, measure, cosine, sine_table)
    grid_shape = (2, tile_rows + frame_width, tile_cols + frame_width)
    spread = accumulate(conj_times(probe_field, backward), offsets_r, offsets_c, grid_shape)
    object_grad = fold_back(spread, tile_rows, tile_cols, frame_width)
    probe_part = jnp.sum(conj_times(patches, backward), axis=0)
    scale_probe = 1.0 / math.sqrt(slot_count * lax.axis_size("row") * lax.axis_size("col"))
    obj_square = jnp.sum(object_grad * object_grad)
    obj_along = jnp.sum(object_grad * object_dir_prev)
    probe_total, products = lax.psum(
        (probe_part, jnp.stack([obj_square, obj_along])), ("row", "col")
    )
    probe_grad = probe_total * scale_probe
    grad_norm = products[0] + jnp.sum(probe_grad * probe_grad)
    along_prev = products[1] + jnp.sum(probe_grad * probe_dir_prev)
    conj_ratio = grad_norm / prev_norm
    probe_direction = -probe_grad + conj_ratio * probe_dir_prev
    object_direction = -object_grad + conj_ratio * object_dir_prev
    descent = grad_norm - conj_ratio * along_prev
    dir_extended = extend_direction(object_direction)
    dir_patches = cut_patches(dir_extended, offsets_r, offsets_c, frame_width)
    step_waves = (
        complex_times(probe_field, dir_patches) + complex_times(probe_direction, patches)
    ) * live_mask[:, None, None, None]
    step_far = unitary_dft(step_waves, cosine, sine_table, 1.0)
    quad_term = 2.0 * (far_kept[:, 0] * step_far[:, 0] + far_kept[:, 1] * step_far[:, 1])
    frame_sums = jnp.sum(quad_term * quad_term, axis=(1, 2))
    curvature = lax.psum(jnp.sum(frame_sums), ("row", "col"))
    step_size = descent / (0.5 * curvature + 1e-06)
    frame_curvature = (frame_sums / (frame_width * frame_width)).reshape(1, 1, slot_count)
    return (
        object_field + step_size * object_direction,
        probe_field + step_size * probe_direction,
        object_direction,
        probe_direction,
        grad_norm,
        frame_curvature,
    )


def solution(mesh):
    return jax.shard_map(
        per_device,
        mesh=mesh,
        in_specs=(
            P(None, "row", "col"),
            P(),
            P(None, "row", "col"),
            P(),
            P(),
            P("row", "col", None, None, None),
            P("row", "col", None, None),
            P("row", None),
        ),
        out_specs=(
            P(None, "row", "col"),
            P(),
            P(None, "row", "col"),
            P(),
            P(),
            P("row", "col", None),
        ),
        check_vma=False,
    )
```

profile of v0, /device:TPU:1, one launch (start us, length us, event | category | flops | bytes accessed | tf_op | source)
XLA Modules:
  0.0 952.4 jit_solution(3851261916546173028)
XLA Ops:
  9.8 8.4 collective-permute-done
  18.2 9.3 collective-permute-start.1
  29.9 10.7 %collective-permute-done.1 = f32[2,512,256]{2,1,0:T(8,128)S(1)} collective-permute-done((f32[2,512,256]{2,1,0:T(8,128)S(1)}, f32[2,512,256]{2,1,0:T(8,128)S(1)}, u32[]{:S(2)}, u32[]{:S(2)}) %collective-permute-start.1) | collective-permute-done | bytes 1048608 | tf_op jit(solution)/shard_map/ppermute | solution.py:12
  42.4 14.1 %while.20 = (s32[]{:T(128)}, f32[2,512,512]{2,1,0:T(8,128)}, s32[4,3]{1,0:T(4,128)S(1)}, f32[4,2,256,256]{2,3,1,0:T(8,128)S(1)}, s32[]{:T(128)}) while((s32[]{:T(128)}, f32[2,512,512]{2,1,0:T(8,128)}, s32[4,3]{1,0:T(4,128)S(1)}, f32[4,2,256,256]{2,3,1,0:T(8,128)S(1)}, s32[]{:T(128)}) %tuple.103), condition=%wide.while_cond.2, body=%wide.while_body.2.sunk | while | flops 2 | bytes 3145845 | solution.py:73
  43.0 2.7 dynamic-slice_bitcast_fusion.2
  58.0 2.8 convolution_bitcast_fusion.5
  60.8 2.9 convolution_bitcast_fusion.4
  64.0 4.5 fusion.6
  68.6 4.8 fusion.5
  73.8 4.4 convolution_bitcast_fusion.3
  78.3 14.3 %convolution_bitcast_fusion.2 = f32[4,2,256,256]{2,3,1,0:T(8,128)S(1)} fusion(f32[4,1,256,256]{3,2,1,0:T(8,128)S(1)} %get-tuple-element.226, f32[4,1,256,256]{3,2,1,0:T(8,128)S(1)} %get-tuple-element.225, f32[4,256,256]{2,1,0:T(8,128)S(1)} %get-tuple-element.224), kind=kOutput, calls=%fused_computation.28 | convolution fusion | flops 1612644352 | bytes 5242880 | tf_op jit(solution)/shard_map/jk,bckl->bcjl/dot_general | solution.py:26
  92.9 3.0 fusion.4
  95.9 3.0 fusion.3
  104.9 58.5 %while.19 = (s32[]{:T(128)}, f32[2,512,512]{1,2,0:T(8,128)}, s32[4]{0:T(128)S(1)}, s32[4]{0:T(128)S(1)}, f32[4,2,256,256]{2,3,1,0:T(8,128)}, /*index=5*/s32[]{:T(128)}, s32[]{:T(128)}, s32[]{:T(128)}) while((s32[]{:T(128)}, f32[2,512,512]{1,2,0:T(8,128)}, s32[4]{0:T(128)S(1)}, s32[4]{0:T(128)S(1)}, f32[4,2,256,256]{2,3,1,0:T(8,128)}, ...), condition=%wide.region_1.2_spmd, body=%wide.region_0.1_spmd.sunk | while | flops 131080 | bytes 7864513 | solution.py:86
  113.1 6.1 dynamic_update_slice.8
  127.5 6.5 dynamic_update_slice.8
  142.2 6.5 dynamic_update_slice.8
  156.9 6.5 dynamic_update_slice.8
  166.8 11.7 %collective-permute-done.2 = f32[2,512,256]{1,2,0:T(8,128)S(1)} collective-permute-done((f32[2,512,256]{1,2,0:T(8,128)S(1)}, f32[2,512,256]{1,2,0:T(8,128)S(1)}, u32[]{:S(2)}, u32[]{:S(2)}) %collective-permute-start.2) | collective-permute-done | bytes 1048608 | tf_op jit(solution)/shard_map/ppermute | solution.py:12
  180.9 2.9 collective-permute-start.3
  192.3 463.4 %all-reduce.2.cloned.1.call-done = f32[2,256,256]{1,2,0:T(8,128)} async-done(((f32[2,256,256]{1,2,0:T(8,128)}), f32[2,256,256]{1,2,0:T(8,128)}) %all-reduce.2.cloned.1.call-update) | async-done | bytes 524304 | tf_op jit(solution)/shard_map/psum | solution.py:131
  657.5 103.0 %psum.21 = f32[2]{0:T(128)S(1)} all-reduce(f32[2]{0:T(128)S(1)} %pad_maximum_fusion.13), channel_id=1, replica_groups=mesh['row'=16,'col'=32] {'row','col'}, use_global_device_ids=true, to_apply=%region_4.5 | all-reduce | flops 2 | bytes 16 | tf_op jit(solution)/shard_map/psum | solution.py:131
  765.2 13.4 %collective-permute-done.4 = f32[2,256,256]{1,2,0:T(8,128)S(1)} collective-permute-done((f32[2,256,256]{1,2,0:T(8,128)S(1)}, f32[2,256,256]{1,2,0:T(8,128)S(1)}, u32[]{:S(2)}, u32[]{:S(2)}) %collective-permute-start.4) | collective-permute-done | bytes 524320 | tf_op jit(solution)/shard_map/ppermute | solution.py:12
  779.7 3.6 collective-permute-start.5
  789.5 7.2 collective-permute-done.5
  796.6 2.8 pad_maximum_fusion.4
  801.0 18.4 %while.21 = (s32[]{:T(128)}, f32[2,512,512]{1,2,0:T(8,128)}, s32[4,3]{1,0:T(4,128)S(1)}, f32[4,2,256,256]{2,3,1,0:T(8,128)}, s32[]{:T(128)}) while((s32[]{:T(128)}, f32[2,512,512]{1,2,0:T(8,128)}, s32[4,3]{1,0:T(4,128)S(1)}, f32[4,2,256,256]{2,3,1,0:T(8,128)}, s32[]{:T(128)}) %tuple.114), condition=%wide.while_cond.3, body=%wide.while_body.3.sunk | while | flops 2 | bytes 4194929 | solution.py:73
  821.8 2.9 convolution_bitcast_fusion.1
  824.7 2.8 convolution_bitcast_fusion
  827.8 4.5 fusion.2
  832.3 4.7 fusion.1
  838.3 102.2 %psum.23 = f32[]{:T(128)} all-reduce(f32[]{:T(128)} %get-tuple-element.192), channel_id=1, replica_groups=mesh['row'=16,'col'=32] {'row','col'}, use_global_device_ids=true, to_apply=%region_10.11 | all-reduce | flops 1 | bytes 8 | tf_op jit(solution)/shard_map/psum | solution.py:149
  (176 shorter events, 94.7 us)
Async XLA Ops:
  7.2 21.5 %copy-start = (s32[1,32]{1,0:T(1,128)S(1)}, s32[1,32]{1,0:T(1,128)}, u32[]{:S(2)}) copy-start(s32[1,32]{1,0:T(1,128)} %param.25) | copy-start | bytes 388
  7.2 20.3 %copy-start.22 = (s32[1,1,4,2]{2,3,1,0:T(2,128)S(1)}, s32[1,1,4,2]{2,3,1,0:T(2,128)}, u32[]{:S(2)}) copy-start(s32[1,1,4,2]{2,3,1,0:T(2,128)} %param.24) | copy-start | bytes 100
  7.2 20.5 %copy-start.14 = (f32[2,256,256]{2,1,0:T(8,128)S(1)}, f32[2,256,256]{2,1,0:T(8,128)}, u32[]{:S(2)}) copy-start(f32[2,256,256]{2,1,0:T(8,128)} %param.19) | copy-start | bytes 1572868
  7.2 648.5 %all-reduce.2.cloned.1.call-start = ((), (), s32[]{:S(2)}) async-start(), calls=%async_computation | async-start | bytes 1048576 | tf_op jit(solution)/shard_map/psum | solution.py:131
  7.2 10.9 %collective-permute-start = (f32[2,256,256]{2,1,0:T(8,128)}, f32[2,256,256]{2,1,0:T(8,128)S(1)}, u32[]{:S(2)}, u32[]{:S(2)}) collective-permute-start(f32[2,256,256]{2,1,0:T(8,128)} %param.18), channel_id=1, source_target_pairs={{32,0},{64,32},{96,64},{128,96},{160,128},{192,160},{224,192},{256... | collective-permute-start | bytes 1572872 | tf_op jit(solution)/shard_map/ppermute | solution.py:12
  18.2 22.4 %collective-permute-start.1 = (f32[2,512,256]{2,1,0:T(8,128)S(1)}, f32[2,512,256]{2,1,0:T(8,128)S(1)}, u32[]{:S(2)}, u32[]{:S(2)}) collective-permute-start(f32[2,512,256]{2,1,0:T(8,128)S(1)} %constant_dynamic-update-slice_fusion.2), channel_id=1, source_target_pairs={{1,0},{2,1},{3,2},{4,3},{5,4},{6,5},{7,6},{8,7},{9,8},{10,9},{11,1... | collective-permute-start | bytes 3145736 | tf_op jit(solution)/shard_map/ppermute | solution.py:12
  56.6 43.8 %copy-start.2 = (f32[4,2,256,256]{2,3,1,0:T(8,128)}, f32[4,2,256,256]{2,3,1,0:T(8,128)S(1)}, u32[]{:S(2)}) copy-start(f32[4,2,256,256]{2,3,1,0:T(8,128)S(1)} %get-tuple-element.148) | copy-start | bytes 6291460
  68.6 4.8 copy-start.20
  73.8 4.5 copy-start.4
  73.8 4.5 copy-start.6
  98.9 1.5 copy-start.12
  164.7 19.1 %copy-start.21 = (f32[2,256,256]{2,1,0:T(8,128)S(1)}, f32[2,256,256]{2,1,0:T(8,128)}, u32[]{:S(2)}) copy-start(f32[2,256,256]{2,1,0:T(8,128)} %param.21) | copy-start | bytes 1572868
  164.7 13.9 %collective-permute-start.2 = (f32[2,512,256]{1,2,0:T(8,128)S(1)}, f32[2,512,256]{1,2,0:T(8,128)S(1)}, u32[]{:S(2)}, u32[]{:S(2)}) collective-permute-start(f32[2,512,256]{1,2,0:T(8,128)S(1)} %slice.205), channel_id=1, source_target_pairs={{0,1},{1,2},{2,3},{3,4},{4,5},{5,6},{6,7},{7,8},{8,9},{9,10},{10,1... | collective-permute-start | bytes 3145736 | tf_op jit(solution)/shard_map/ppermute | solution.py:12
  180.9 9.3 collective-permute-start.3
  190.1 572.3 %copy-start.19 = (f32[2,256,256]{1,2,0:T(8,128)}, f32[2,256,256]{1,2,0:T(8,128)S(1)}, u32[]{:S(2)}) copy-start(f32[2,256,256]{1,2,0:T(8,128)S(1)} %collective-permute-done.3) | copy-start | bytes 1572868
  762.5 20.8 %copy-start.15 = (f32[2,256,256]{2,1,0:T(8,128)S(1)}, f32[2,256,256]{2,1,0:T(8,128)}, u32[]{:S(2)}) copy-start(f32[2,256,256]{2,1,0:T(8,128)} %param.19) | copy-start | bytes 1572868
  763.7 32.9 %copy-start.8 = (f32[2,256,256]{1,2,0:T(8,128)}, f32[2,256,256]{1,2,0:T(8,128)S(1)}, u32[]{:S(2)}) copy-start(f32[2,256,256]{1,2,0:T(8,128)S(1)} %multiply_add_fusion.8) | copy-start | bytes 1572868
  763.7 20.6 %copy-start.16 = (f32[2,256,256]{2,1,0:T(8,128)S(1)}, f32[2,256,256]{2,1,0:T(8,128)}, u32[]{:S(2)}) copy-start(f32[2,256,256]{2,1,0:T(8,128)} %param.18) | copy-start | bytes 1572868
  763.8 14.8 %collective-permute-start.4 = (f32[2,256,256]{1,2,0:T(8,128)S(1)}, f32[2,256,256]{1,2,0:T(8,128)S(1)}, u32[]{:S(2)}, u32[]{:S(2)}) collective-permute-start(f32[2,256,256]{1,2,0:T(8,128)S(1)} %multiply_add_fusion.8), channel_id=1, source_target_pairs={{32,0},{64,32},{96,64},{128,96},{160,128},{192,160},{224,192},{256... | collective-permute-start | bytes 1572872 | tf_op jit(solution)/shard_map/ppermute | solution.py:12
  779.7 7.8 copy-start.13
  779.7 16.9 %collective-permute-start.5 = (f32[2,512,256]{1,2,0:T(8,128)}, f32[2,512,256]{1,2,0:T(8,128)}, u32[]{:S(2)}, u32[]{:S(2)}) collective-permute-start(f32[2,512,256]{1,2,0:T(8,128)} %pad_maximum_fusion.12), channel_id=1, source_target_pairs={{1,0},{2,1},{3,2},{4,3},{5,4},{6,5},{7,6},{8,7},{9,8},{10,9},{11,1... | collective-permute-start | bytes 3145736 | tf_op jit(solution)/shard_map/ppermute | solution.py:12
  787.6 11.8 %copy-start.10 = (f32[2,256,256]{1,2,0:T(8,128)}, f32[2,256,256]{1,2,0:T(8,128)S(1)}, u32[]{:S(2)}) copy-start(f32[2,256,256]{1,2,0:T(8,128)S(1)} %multiply_add_fusion.7) | copy-start | bytes 1572868
  801.0 18.4 %copy-start.3 = (f32[4,2,256,256]{2,3,1,0:T(8,128)S(1)}, f32[4,2,256,256]{2,3,1,0:T(8,128)}, u32[]{:S(2)}) copy-start(f32[4,2,256,256]{2,3,1,0:T(8,128)} %copy-done.2) | copy-start | bytes 6291460
  832.3 4.7 copy-start.5
  832.3 4.7 copy-start.7
  837.1 104.2 %copy-start.11 = (f32[2,256,256]{1,2,0:T(8,128)S(1)}, f32[2,256,256]{1,2,0:T(8,128)}, u32[]{:S(2)}) copy-start(f32[2,256,256]{1,2,0:T(8,128)} %copy-done.10) | copy-start | bytes 1572868
  837.1 104.2 %copy-start.18 = (f32[2,256,256]{1,2,0:T(8,128)S(1)}, f32[2,256,256]{1,2,0:T(8,128)}, u32[]{:S(2)}) copy-start(f32[2,256,256]{1,2,0:T(8,128)} %copy.66) | copy-start | bytes 1572868
  838.3 104.1 %copy-start.9 = (f32[2,256,256]{1,2,0:T(8,128)S(1)}, f32[2,256,256]{1,2,0:T(8,128)}, u32[]{:S(2)}) copy-start(f32[2,256,256]{1,2,0:T(8,128)} %copy-done.8) | copy-start | bytes 1572868
  838.3 104.1 %copy-start.17 = (f32[2,256,256]{1,2,0:T(8,128)S(1)}, f32[2,256,256]{1,2,0:T(8,128)}, u32[]{:S(2)}) copy-start(f32[2,256,256]{1,2,0:T(8,128)} %copy.65) | copy-start | bytes 1572868
  941.3 2.7 copy-start.1
Sparse Core Ops, SparseCore 0:
  188.5 467.1 all-reduce.1
where the time goes:
time: 965 us; the launch traced here: 952 us
  waiting for transfers between devices  516 us (53%)
  blocking collectives  205 us (21%)
  local copies, waits for them, and re-layouts  91.8 us (10%)
  matrix products  54.7 us (6%)
  other arithmetic  27.2 us (3%)
  starting transfers between devices  20.7 us (2%)
  between operations  20.1 us (2%)
  loops' own time  16.1 us (2%)
    psum x1, waiting for transfers between devices, per_device(): lax.psum((probe_part, jnp.stack([obj_square, obj_along])), ('row', 'col'))  463 us
    psum x1, blocking collectives, per_device(): lax.psum((probe_part, jnp.stack([obj_square, obj_along])), ('row', 'col'))  103 us
    psum x1, blocking collectives, per_device(): curvature = lax.psum(jnp.sum(frame_sums), ('row', 'col'))  102 us
    ppermute x6, waiting for transfers between devices, passed_along(): return lax.ppermute(shard, axis, pairs)  53.1 us
    gather x44, local copies, waits for them, and re-layouts  32.1 us
    dynamic_update_slice x8, local copies, waits for them, and re-layouts, add_one(): return lax.dynamic_update_slice(grid, current + piece, anchor)  26.4 us
    ppermute x6, starting transfers between devices, passed_along(): return lax.ppermute(shard, axis, pairs)  20.7 us
    dot_general x3, matrix products, unitary_dft(): left_s = jnp.einsum('jk,bckl->bcjl', sine_table, frames, precision=precise)  20.1 us
  transfers between devices with their start and end apart: 7, of which 7 were waited for; matrix products, arithmetic and copies ran while one was open for 2% of the time, Pallas kernels for 0%

commit v1 on v0

v1 whole, which is shorter than its diff:
```python
import functools
import math

import jax
import jax.numpy as jnp
import numpy as np
from jax import lax
from jax.experimental import pallas as pl
from jax.experimental.pallas import tpu as pltpu
from jax.sharding import PartitionSpec as P

VMEM_BYTES = 48 * 1024 * 1024


def dft_blocks(width):
    at = np.arange(width)
    angle = (np.outer(at, at) % width) * (2.0 * math.pi / width)
    cosine = (np.cos(angle) / math.sqrt(width)).astype(np.float32)
    sine = (np.sin(angle) / math.sqrt(width)).astype(np.float32)

    def thrice(table):
        high = table.astype(jnp.bfloat16)
        low = (table - high.astype(np.float32)).astype(jnp.bfloat16)
        return np.concatenate([high, low, high], axis=1)

    real_rows = np.concatenate([thrice(cosine), thrice(sine)], axis=1)
    imag_rows = np.concatenate([thrice(-sine), thrice(cosine)], axis=1)
    left = np.concatenate([real_rows, imag_rows], axis=0)
    return left, np.ascontiguousarray(left.T)


def split_halves(value):
    high = value.astype(jnp.bfloat16)
    low = (value - high.astype(jnp.float32)).astype(jnp.bfloat16)
    return high, low


def dft_pair(first, second, left_ref, right_ref, tall_ref, wide_ref):
    width = first.shape[0]
    for at, part in enumerate((first, second)):
        high, low = split_halves(part)
        base = 3 * at * width
        tall_ref[base : base + width, :] = high
        tall_ref[base + width : base + 2 * width, :] = high
        tall_ref[base + 2 * width : base + 3 * width, :] = low
    middle = jnp.dot(left_ref[...], tall_ref[...], preferred_element_type=jnp.float32)
    for at in range(2):
        high, low = split_halves(middle[at * width : (at + 1) * width])
        base = 3 * at * width
        wide_ref[:, base : base + width] = high
        wide_ref[:, base + width : base + 2 * width] = high
        wide_ref[:, base + 2 * width : base + 3 * width] = low
    done = jnp.dot(wide_ref[...], right_ref[...], preferred_element_type=jnp.float32)
    return done[:, :width], done[:, width:]


def rolled(value, row, col):
    return pltpu.roll(pltpu.roll(value, row, 0), col, 1)


def wrapped(own, below, right, diag, upper, nearer):
    return jnp.where(nearer, jnp.where(upper, own, below), jnp.where(upper, right, diag))


def masks(row, col, width):
    upper = lax.broadcasted_iota(jnp.int32, (width, width), 0) >= row
    nearer = lax.broadcasted_iota(jnp.int32, (width, width), 1) >= col
    return upper, nearer


def gradient_kernel(
    positions_ref,
    counts_ref,
    own_ref,
    below_ref,
    right_ref,
    diag_ref,
    probe_ref,
    measured_ref,
    dft_left_ref,
    dft_right_ref,
    near_ref,
    side_ref,
    probe_part_ref,
    patch_ref,
    moved_ref,
    far_ref,
    tall_ref,
    wide_ref,
):
    width = probe_ref.shape[-1]
    near_ref[...] = jnp.zeros_like(near_ref)
    side_ref[...] = jnp.zeros_like(side_ref)
    probe_part_ref[...] = jnp.zeros_like(probe_part_ref)

    def frame(slot, carry):
        row = lax.rem(positions_ref[0, 0, slot, 0], width)
        col = lax.rem(positions_ref[0, 0, slot, 1], width)
        upper, nearer = masks(row, col, width)
        for part in range(2):
            patch_ref[slot, part] = wrapped(
                own_ref[part], below_ref[part], right_ref[part], diag_ref[part], upper, nearer
            )
            moved_ref[slot, part] = rolled(probe_ref[part], row, col)
        patch_r, patch_i = patch_ref[slot, 0], patch_ref[slot, 1]
        probe_r, probe_i = moved_ref[slot, 0], moved_ref[slot, 1]
        wave_r = probe_r * patch_r - probe_i * patch_i
        wave_i = probe_r * patch_i + probe_i * patch_r
        far_r, far_i = dft_pair(wave_r, wave_i, dft_left_ref, dft_right_ref, tall_ref, wide_ref)
        far_ref[slot, 0] = far_r
        far_ref[slot, 1] = far_i
        residue = far_r * far_r + far_i * far_i - measured_ref[0, 0, slot].astype(jnp.float32)
        back_i, back_r = dft_pair(
            residue * far_i, residue * far_r, dft_left_ref, dft_right_ref, tall_ref, wide_ref
        )
        patch_r, patch_i = patch_ref[slot, 0], patch_ref[slot, 1]
        probe_r, probe_i = moved_ref[slot, 0], moved_ref[slot, 1]
        back_row = lax.rem(width - row, width)
        back_col = lax.rem(width - col, width)
        probe_part_ref[0] += rolled(patch_r * back_r + patch_i * back_i, back_row, back_col)
        probe_part_ref[1] += rolled(patch_r * back_i - patch_i * back_r, back_row, back_col)
        terms = (probe_r * back_r + probe_i * back_i, probe_r * back_i - probe_i * back_r)
        for part, term in enumerate(terms):
            close = jnp.where(nearer, term, 0.0)
            beyond = term - close
            near_ref[part, :width, :] += jnp.where(upper, close, 0.0)
            near_ref[part, width:, :] += jnp.where(upper, 0.0, close)
            side_ref[part, :width, :] += jnp.where(upper, beyond, 0.0)
            side_ref[part, width:, :] += jnp.where(upper, 0.0, beyond)
        return carry

    lax.fori_loop(0, counts_ref[0, lax.axis_index("col")], frame, 0)


def curvature_kernel(
    positions_ref,
    counts_ref,
    prev_norm_ref,
    gathered_ref,
    g_own_ref,
    g_below_ref,
    g_right_ref,
    d_own_ref,
    d_below_ref,
    d_right_ref,
    probe_prev_ref,
    patch_ref,
    moved_ref,
    far_ref,
    dft_left_ref,
    dft_right_ref,
    direction_ref,
    probe_direction_ref,
    row_ref,
    below_ref,
    right_ref,
    tall_ref,
    wide_ref,
    *,
    probe_scale,
):
    width = gathered_ref.shape[-1]
    depth = gathered_ref.shape[1] - 1
    probe_grad = gathered_ref[:, :depth, :].reshape(probe_prev_ref.shape) * probe_scale
    probe_prev = probe_prev_ref[...]
    products = jnp.sum(gathered_ref[:, depth:, :], axis=0)
    at = lax.broadcasted_iota(jnp.int32, products.shape, 1)
    grad_norm = jnp.sum(jnp.where(at == 0, products, 0.0)) + jnp.sum(probe_grad * probe_grad)
    along_prev = jnp.sum(jnp.where(at == 1, products, 0.0)) + jnp.sum(probe_grad * probe_prev)
    ratio = grad_norm / prev_norm_ref[0]
    descent = grad_norm - ratio * along_prev
    probe_direction_ref[...] = ratio * probe_prev - probe_grad
    direction_ref[...] = ratio * d_own_ref[...] - g_own_ref[...]
    below_ref[...] = ratio * d_below_ref[...] - g_below_ref[...]
    right_ref[...] = ratio * d_right_ref[...] - g_right_ref[...]
    lane = lax.broadcasted_iota(jnp.int32, (1, 128), 1)

    def frame(slot, carry):
        row = lax.rem(positions_ref[0, 0, slot, 0], width)
        col = lax.rem(positions_ref[0, 0, slot, 1], width)
        upper, nearer = masks(row, col, width)
        step_r, step_i = [
            wrapped(
                direction_ref[part],
                below_ref[part],
                right_ref[part, :width],
                right_ref[part, width:],
                upper,
                nearer,
            )
            for part in range(2)
        ]
        patch_r, patch_i = patch_ref[slot, 0], patch_ref[slot, 1]
        probe_r, probe_i = moved_ref[slot, 0], moved_ref[slot, 1]
        change_r = rolled(probe_direction_ref[0], row, col)
        change_i = rolled(probe_direction_ref[1], row, col)
        wave_r = probe_r * step_r - probe_i * step_i + change_r * patch_r - change_i * patch_i
        wave_i = probe_r * step_i + probe_i * step_r + change_r * patch_i + change_i * patch_r
        far_r, far_i = dft_pair(wave_r, wave_i, dft_left_ref, dft_right_ref, tall_ref, wide_ref)
        quad = 2.0 * (far_ref[slot, 0] * far_r + far_ref[slot, 1] * far_i)
        frame_sum = jnp.sum(quad * quad)
        return carry + jnp.where((lane == 0) | (lane == slot + 1), frame_sum, 0.0)

    row = lax.fori_loop(0, counts_ref[0, lax.axis_index("col")], frame, jnp.zeros((1, 128), jnp.float32))
    row_ref[...] = jnp.where(lane == 5, grad_norm, jnp.where(lane == 6, descent, row))


def shaped(*dims):
    return jax.ShapeDtypeStruct(dims, jnp.float32)


def in_vmem(count):
    return [pl.BlockSpec(memory_space=pltpu.VMEM)] * count


def in_smem(count):
    return [pl.BlockSpec(memory_space=pltpu.SMEM)] * count


def scratch_for(width):
    return [
        pltpu.VMEM((6 * width, width), jnp.bfloat16),
        pltpu.VMEM((width, 6 * width), jnp.bfloat16),
    ]


def gradient_call(positions, counts, tiles, probe, measured, tables):
    width = probe.shape[-1]
    slots = measured.shape[2]
    return pl.pallas_call(
        gradient_kernel,
        out_shape=(
            shaped(2, 2 * width, width),
            shaped(2, 2 * width, width),
            shaped(2, width, width),
            shaped(slots, 2, width, width),
            shaped(slots, 2, width, width),
            shaped(slots, 2, width, width),
        ),
        in_specs=in_smem(2) + in_vmem(8),
        out_specs=tuple(in_vmem(6)),
        scratch_shapes=scratch_for(width),
        compiler_params=pltpu.CompilerParams(vmem_limit_bytes=VMEM_BYTES),
        cost_estimate=pl.CostEstimate(flops=10**10, bytes_accessed=10**7, transcendentals=0),
        name="gradient_frames",
    )(positions, counts, *tiles, probe, measured, *tables)


def curvature_call(positions, counts, prev_norm, gathered, tiles, probe_prev, kept, tables, probe_scale):
    width = gathered.shape[-1]
    return pl.pallas_call(
        functools.partial(curvature_kernel, probe_scale=probe_scale),
        out_shape=(shaped(2, width, width), shaped(2, width, width), shaped(1, 128)),
        in_specs=in_smem(3) + in_vmem(13),
        out_specs=tuple(in_vmem(3)),
        scratch_shapes=[
            pltpu.VMEM((2, width, width), jnp.float32),
            pltpu.VMEM((2, 2 * width, width), jnp.float32),
        ]
        + scratch_for(width),
        compiler_params=pltpu.CompilerParams(vmem_limit_bytes=VMEM_BYTES),
        cost_estimate=pl.CostEstimate(flops=5 * 10**9, bytes_accessed=10**7, transcendentals=0),
        name="curvature_frames",
    )(positions, counts, prev_norm, gathered, *tiles, probe_prev, *kept, *tables)


def passed_along(shard, axis, by):
    count = lax.axis_size(axis)
    pairs = [(i, i + by) for i in range(count) if 0 <= i + by < count]
    return lax.ppermute(shard, axis, pairs)


def summed_pieces(whole, axis):
    count = lax.axis_size(axis)
    pieces = whole.reshape((count, whole.shape[0] // count) + whole.shape[1:])
    return jnp.sum(lax.all_to_all(pieces, axis, 0, 0), axis=0)


def gathered_pieces(piece, axis):
    count = lax.axis_size(axis)
    copies = jnp.broadcast_to(piece[None], (count,) + piece.shape)
    return lax.all_to_all(copies, axis, 0, 0)


def held(value, *others):
    return lax.optimization_barrier((value,) + others)[0]


def stacked_rows(upper, lower):
    return jnp.concatenate([upper, lower], axis=1)


def per_device(
    object_field,
    probe_field,
    object_dir_prev,
    probe_dir_prev,
    prev_norm,
    intensities,
    positions,
    counts,
):
    width = probe_field.shape[-1]
    slots = positions.shape[2]
    tables = dft_blocks(width)
    probe_scale = 1.0 / math.sqrt(slots * lax.axis_size("row") * lax.axis_size("col"))

    below = passed_along(object_field, "row", -1)
    right = passed_along(object_field, "col", -1)
    below = held(below, right)
    diag = passed_along(below, "col", -1)
    prev_below = passed_along(held(object_dir_prev, below), "row", -1)
    diag = held(diag, prev_below)
    prev_right = passed_along(stacked_rows(object_dir_prev, prev_below), "col", -1)

    near, side, probe_part, *kept = gradient_call(
        positions, counts, (object_field, below, right, diag), probe_field, intensities, tables
    )
    probe_part = held(probe_part, prev_right)
    from_left = passed_along(side, "col", 1)
    piece = summed_pieces(probe_part.reshape(-1, width), "row")
    owned = near + held(from_left, piece)
    from_above = passed_along(owned[:, width:], "row", 1)
    piece = summed_pieces(held(piece, owned), "col")
    object_grad = owned[:, :width] + held(from_above, piece)
    grad_below = passed_along(object_grad, "row", -1)
    lane = lax.broadcasted_iota(jnp.int32, (1, width), 1)
    square = jnp.sum(object_grad * object_grad)
    along = jnp.sum(object_grad * object_dir_prev)
    products = jnp.where(lane == 0, square, jnp.where(lane == 1, along, 0.0))
    pieces = gathered_pieces(jnp.concatenate([piece, products], axis=0), "col")
    products = jnp.sum(pieces[:, 1], axis=0)[None]
    grad_column = stacked_rows(object_grad, held(grad_below, pieces))
    grad_right = passed_along(grad_column, "col", -1)
    piece = jnp.concatenate([pieces[:, 0], products], axis=0)
    gathered = gathered_pieces(held(piece, grad_column), "row")
    grad_right = held(grad_right, gathered)

    object_direction, probe_direction, row = curvature_call(
        positions,
        counts,
        prev_norm.reshape(1),
        gathered,
        (object_grad, grad_below, grad_right, object_dir_prev, prev_below, prev_right),
        probe_dir_prev,
        kept,
        tables,
        probe_scale,
    )
    across = jnp.sum(gathered_pieces(row, "row"), axis=0)
    across = jnp.sum(gathered_pieces(across, "col"), axis=0)
    step_size = row[0, 6] / (0.5 * across[0, 0] + 1e-06)
    frame_curvature = (row[0, 1 : 1 + slots] / (width * width)).reshape(1, 1, slots)
    return (
        object_field + step_size * object_direction,
        probe_field + step_size * probe_direction,
        object_direction,
        probe_direction,
        row[0, 5],
        frame_curvature,
    )


def solution(mesh):
    return jax.shard_map(
        per_device,
        mesh=mesh,
        in_specs=(
            P(None, "row", "col"),
            P(),
            P(None, "row", "col"),
            P(),
            P(),
            P("row", "col", None, None, None),
            P("row", "col", None, None),
            P("row", None),
        ),
        out_specs=(
            P(None, "row", "col"),
            P(),
            P(None, "row", "col"),
            P(),
            P(),
            P("row", "col", None),
        ),
        check_vma=False,
    )
```

time: 965 us -> 219 us (0.23); the launches traced: 952 us -> 218 us
  waiting for transfers between devices: 516 us -> 54.9 us
  blocking collectives: 205 us -> 65.8 us
  local copies, waits for them, and re-layouts: 91.8 us -> 11 us
  matrix products: 54.7 us -> 0 us
  Pallas kernels: 0 us -> 31.2 us
  starting transfers between devices: 20.7 us -> 43.1 us
  between operations: 20.1 us -> 2.28 us
  other arithmetic: 27.2 us -> 10.1 us
  loops' own time: 16.1 us -> 0 us
    psum x1 -> x0, waiting for transfers between devices: 463 us -> none  [per_device(): lax.psum((probe_part, jnp.stack([obj_square, obj_along])), ('row', 'col'))]
    psum x2 -> x0, blocking collectives: 205 us -> none  [the longest x1 103 us: per_device(): lax.psum((probe_part, jnp.stack([obj_square, obj_along])), ('row', 'col'))]
    all_to_all x0 -> x3, blocking collectives: none -> 65.8 us  [the longest x2 49 us: summed_pieces(): return jnp.sum(lax.all_to_all(pieces, axis, 0, 0), axis=0)]
    dot_general x12 -> x0, matrix products: 54.7 us -> none  [the longest x3 20.1 us: unitary_dft(): left_s = jnp.einsum('jk,bckl->bcjl', sine_table, frames, precision=precise)]
    gather x44 -> x0, local copies, waits for them, and re-layouts: 32.1 us -> none
    pallas_call x0 -> x2, Pallas kernels: none -> 31.2 us  [the longest x1 18.6 us: gradient_call(): pl.pallas_call(gradient_kernel, out_shape=(shaped(2, 2 * width, width), s...]
    all_to_all x0 -> x3, waiting for transfers between devices: none -> 29.6 us  [gathered_pieces(): return lax.all_to_all(copies, axis, 0, 0)]
    ppermute x6 -> x9, waiting for transfers between devices: 53.1 us -> 25.3 us  [passed_along(): return lax.ppermute(shard, axis, pairs)]
  transfers between devices with their start and end apart: 7 -> 12, of which waited for: 7 -> 6; matrix products, arithmetic and copies ran while one was open for 2% -> 2% of each run, Pallas kernels for 0% -> 9%
where the time goes in v1:
time: 219 us; the launch traced here: 218 us
  blocking collectives  65.8 us (30%)
  waiting for transfers between devices  54.9 us (25%)
  starting transfers between devices  43.1 us (20%)
  Pallas kernels  31.2 us (14%)
  local copies, waits for them, and re-layouts  11 us (5%)
  other arithmetic  10.1 us (5%)
  between operations  2.28 us (1%)
    all_to_all x2, blocking collectives, summed_pieces(): return jnp.sum(lax.all_to_all(pieces, axis, 0, 0), axis=0)  49 us
    all_to_all x3, waiting for transfers between devices, gathered_pieces(): return lax.all_to_all(copies, axis, 0, 0)  29.6 us
    ppermute x9, starting transfers between devices, passed_along(): return lax.ppermute(shard, axis, pairs)  26.4 us
    ppermute x9, waiting for transfers between devices, passed_along(): return lax.ppermute(shard, axis, pairs)  25.3 us
    pallas_call x1, Pallas kernels, gradient_call(): pl.pallas_call(gradient_kernel, out_shape=(shaped(2, 2 * width, width), s...  18.6 us
    all_to_all x1, blocking collectives, gathered_pieces(): return lax.all_to_all(copies, axis, 0, 0)  16.8 us
    all_to_all x3, starting transfers between devices, gathered_pieces(): return lax.all_to_all(copies, axis, 0, 0)  16.7 us
    pallas_call x1, Pallas kernels, curvature_call(): pl.pallas_call(functools.partial(curvature_kernel, probe_scale=probe_scal...  12.6 us
  transfers between devices with their start and end apart: 12, of which 6 were waited for; matrix products, arithmetic and copies ran while one was open for 2% of the time, Pallas kernels for 9%

profile of v1, /device:TPU:1, one launch (start us, length us, event | category | flops | bytes accessed | tf_op | source)
XLA Modules:
  0.0 218.2 jit_solution(7285351064703854258)
XLA Ops:
  0.7 8.9 %collective-permute-start.1 = (f32[2,256,256]{2,1,0:T(8,128)}, f32[2,256,256]{2,1,0:T(8,128)S(1)}, u32[]{:S(2)}, u32[]{:S(2)}) collective-permute-start(f32[2,256,256]{2,1,0:T(8,128)} %own_ref.1), channel_id=1, source_target_pairs={{1,0},{2,1},{3,2},{4,3},{5,4},{6,5},{7,6},{8,7},{9,8},{10,9},{11,1... | collective-permute-start | bytes 1572872 | tf_op jit(solution)/shard_map/ppermute | solution.py:270
  9.6 1.3 collective-permute-start
  10.9 1.9 collective-permute-done.1.right_ref
  12.8 12.5 %collective-permute-done.below_ref = f32[2,256,256]{2,1,0:T(8,128)S(1)} collective-permute-done((f32[2,256,256]{2,1,0:T(8,128)}, f32[2,256,256]{2,1,0:T(8,128)S(1)}, u32[]{:S(2)}, u32[]{:S(2)}) %collective-permute-start) | collective-permute-done | bytes 524320 | tf_op jit(solution)/shard_map/ppermute | solution.py:270
  25.3 1.3 collective-permute-start.3
  26.6 2.3 %collective-permute-start.2 = (f32[2,256,256]{2,1,0:T(8,128)S(1)}, f32[2,256,256]{2,1,0:T(8,128)}, u32[]{:S(2)}, u32[]{:S(2)}) collective-permute-start(f32[2,256,256]{2,1,0:T(8,128)S(1)} %collective-permute-done.below_ref), channel_id=1, source_target_pairs={{1,0},{2,1},{3,2},{4,3},{5,4},{6,5},{7,6},{8,7},{9,8},{10,9},{11,1... | collective-permute-start | bytes 1572872 | tf_op jit(solution)/shard_map/ppermute | solution.py:270
  29.7 10.8 %collective-permute-done.3.d_below_ref = f32[2,256,256]{2,1,0:T(8,128)S(1)} collective-permute-done((f32[2,256,256]{2,1,0:T(8,128)}, f32[2,256,256]{2,1,0:T(8,128)S(1)}, u32[]{:S(2)}, u32[]{:S(2)}) %collective-permute-start.3) | collective-permute-done | bytes 524320 | tf_op jit(solution)/shard_map/ppermute | solution.py:270
  40.5 1.1 pad_maximum_fusion
  41.7 3.1 %collective-permute-start.4 = (f32[2,512,256]{2,1,0:T(8,128)S(1)}, f32[2,512,256]{2,1,0:T(8,128)S(1)}, u32[]{:S(2)}, u32[]{:S(2)}) collective-permute-start(f32[2,512,256]{2,1,0:T(8,128)S(1)} %pad_maximum_fusion), channel_id=1, source_target_pairs={{1,0},{2,1},{3,2},{4,3},{5,4},{6,5},{7,6},{8,7},{9,8},{10,9},{11,1... | collective-permute-start | bytes 3145736 | tf_op jit(solution)/shard_map/ppermute | solution.py:270
  45.9 1.0 copy-done.12
  46.9 18.6 %gradient_frames.1 = (f32[2,512,256]{2,1,0:T(8,128)S(1)}, f32[2,512,256]{2,1,0:T(8,128)}, f32[2,256,256]{2,1,0:T(8,128)S(1)}, f32[4,2,256,256]{3,2,1,0:T(8,128)}...) custom-call(s32[1,1,4,2]{3,2,1,0:T(4,128)S(1)} %copy.23.positions_ref, s32[1,32]{1,0:T(1,128)S(1)} %copy-done.13, ...), custom_call_target="tpu_custom_call" | custom-call | flops 10000000000 | bytes 10000000 | tf_op jit(solution)/shard_map/gradient_frames/pallas_call | solution.py:230
  65.5 2.4 %collective-permute-start.5 = (f32[2,512,256]{2,1,0:T(8,128)}, f32[2,512,256]{2,1,0:T(8,128)}, u32[]{:S(2)}, u32[]{:S(2)}) collective-permute-start(f32[2,512,256]{2,1,0:T(8,128)} %get-tuple-element.31), channel_id=1, source_target_pairs={{0,1},{1,2},{2,3},{3,4},{4,5},{5,6},{6,7},{7,8},{8,9},{9,10},{10,1... | collective-permute-start | bytes 3145736 | tf_op jit(solution)/shard_map/ppermute | solution.py:270
  69.0 17.2 %all_to_all.30 = f32[16,32,256]{2,1,0:T(8,128)S(1)} all-to-all(f32[16,32,256]{2,1,0:T(8,128)S(1)} %bitcast.17), channel_id=1, replica_groups=mesh['row'=16,'col'=32] {'row'}, dimensions={0} | all-to-all | bytes 1048576 | tf_op jit(solution)/shard_map/all_to_all | solution.py:276
  86.2 1.5 add.16
  88.8 2.2 %collective-permute-start.6 = (f32[2,256,256]{2,1,0:T(8,128)S(1)}, f32[2,256,256]{2,1,0:T(8,128)S(1)}, u32[]{:S(2)}, u32[]{:S(2)}) collective-permute-start(f32[2,256,256]{2,1,0:T(8,128)S(1)} %slice.33), channel_id=1, source_target_pairs={{0,32},{32,64},{64,96},{96,128},{128,160},{160,192},{192,224},{224... | collective-permute-start | bytes 1572872 | tf_op jit(solution)/shard_map/ppermute | solution.py:270
  91.1 31.7 %all_to_all.31 = f32[32,1,256]{2,1,0:T(1,128)S(1)} all-to-all(f32[32,1,256]{2,1,0:T(1,128)S(1)} %reshape.73), channel_id=1, replica_groups=mesh['row'=16,'col'=32] {'col'}, dimensions={0} | all-to-all | bytes 65536 | tf_op jit(solution)/shard_map/all_to_all | solution.py:276
  122.9 1.8 multiply_reduce_fusion.1
  124.7 1.3 collective-permute-start.7
  126.0 1.3 compare_select_fusion.1
  127.4 16.8 %all_to_all.32 = f32[32,2,256]{2,1,0:T(2,128)S(1)} all-to-all(f32[32,2,256]{2,1,0:T(2,128)S(1)} %broadcast_in_dim.44), channel_id=1, replica_groups=mesh['row'=16,'col'=32] {'col'}, dimensions={0} | all-to-all | bytes 131072 | tf_op jit(solution)/shard_map/all_to_all | solution.py:282
  144.2 1.2 pad_maximum_fusion.1
  145.4 3.5 %collective-permute-start.8 = (f32[2,512,256]{2,1,0:T(8,128)}, f32[2,512,256]{2,1,0:T(8,128)}, u32[]{:S(2)}, u32[]{:S(2)}) collective-permute-start(f32[2,512,256]{2,1,0:T(8,128)} %pad_maximum_fusion.1), channel_id=1, source_target_pairs={{1,0},{2,1},{3,2},{4,3},{5,4},{6,5},{7,6},{8,7},{9,8},{10,9},{11,1... | collective-permute-start | bytes 3145736 | tf_op jit(solution)/shard_map/ppermute | solution.py:270
  149.9 6.4 %all-to-all-start.3 = ((f32[16,33,256]{2,1,0:T(8,128)}), f32[16,33,256]{2,1,0:T(8,128)S(1)}, u32[]{:S(2)}, u32[]{:S(2)}) async-start(f32[16,33,256]{2,1,0:T(8,128)} %broadcast_in_dim.46), calls=%async_computation.3 | async-start | bytes 1310720 | tf_op jit(solution)/shard_map/all_to_all | solution.py:282
  156.9 12.7 %all-to-all-done.3.gathered_ref = f32[16,33,256]{2,1,0:T(8,128)S(1)} async-done(((f32[16,33,256]{2,1,0:T(8,128)}), f32[16,33,256]{2,1,0:T(8,128)S(1)}, u32[]{:S(2)}, u32[]{:S(2)}) %all-to-all-start.3) | async-done | bytes 540704 | tf_op jit(solution)/shard_map/all_to_all | solution.py:282
  169.6 1.0 copy-done.4
  170.7 1.2 copy-done.6
  172.9 12.6 %curvature_frames.1 = (f32[2,256,256]{2,1,0:T(8,128)}, f32[2,256,256]{2,1,0:T(8,128)}, f32[1,128]{1,0:T(1,128)S(1)}) custom-call(s32[1,1,4,2]{3,2,1,0:T(4,128)S(1)} %copy.23.positions_ref, s32[1,32]{1,0:T(1,128)S(1)} %copy-done.13, f32[1]{0:T(128)} %bitcast.16.prev_norm_ref, f32[16,33,256]{2,1,0:T(8,128)S(1)} %all-to-all-done.3.gathered_ref, ...), custom_call_target="tpu_custom_call" | custom-call | flops 5000000000 | bytes 10000000 | tf_op jit(solution)/shard_map/curvature_frames/pallas_call | solution.py:251
  186.1 3.5 %all-to-all-start.4 = ((f32[16,1,128]{2,1,0:T(1,128)}), f32[16,1,128]{2,1,0:T(1,128)S(1)}, u32[]{:S(2)}, u32[]{:S(2)}) async-start(f32[16,1,128]{2,1,0:T(1,128)} %broadcast_in_dim.48), calls=%async_computation.4 | async-start | bytes 16384 | tf_op jit(solution)/shard_map/all_to_all | solution.py:282
  190.2 5.7 %all-to-all-done.4 = f32[16,1,128]{2,1,0:T(1,128)S(1)} async-done(((f32[16,1,128]{2,1,0:T(1,128)}), f32[16,1,128]{2,1,0:T(1,128)S(1)}, u32[]{:S(2)}, u32[]{:S(2)}) %all-to-all-start.4) | async-done | bytes 8224 | tf_op jit(solution)/shard_map/all_to_all | solution.py:282
  196.5 6.9 %all-to-all-start.5 = ((f32[32,1,128]{2,1,0:T(1,128)}), f32[32,1,128]{2,1,0:T(1,128)S(1)}, u32[]{:S(2)}, u32[]{:S(2)}) async-start(f32[32,1,128]{2,1,0:T(1,128)} %broadcast_in_dim.49), calls=%async_computation.5 | async-start | bytes 32768 | tf_op jit(solution)/shard_map/all_to_all | solution.py:282
  204.0 11.2 %all-to-all-done.5 = f32[32,1,128]{2,1,0:T(1,128)S(1)} async-done(((f32[32,1,128]{2,1,0:T(1,128)}), f32[32,1,128]{2,1,0:T(1,128)S(1)}, u32[]{:S(2)}, u32[]{:S(2)}) %all-to-all-start.5) | async-done | bytes 16416 | tf_op jit(solution)/shard_map/all_to_all | solution.py:282
  215.9 2.3 %multiply_add_fusion = (f32[2,256,256]{2,1,0:T(8,128)}, f32[2,256,256]{2,1,0:T(8,128)}) fusion(f32[2,256,256]{2,1,0:T(8,128)S(1)} %copy-done.1, f32[2,256,256]{2,1,0:T(8,128)} %get-tuple-element.22, f32[]{:T(128)} %bitcast.8, f32[2,256,256]{2,1,0:T(8,128)S(1)} %copy-done.2, f32[2,256,256]{2,1,0:T(8,128)} %get-tuple-element.21), kind=kLoop, calls=%fused_computation.3 | loop fusion | flops 524288 | bytes 3145732 | tf_op jit(solution)/shard_map/add | solution.py:356
  (50 shorter events, 8.5 us)
Async XLA Ops:
  0.6 44.2 %copy-start.2 = (f32[2,256,256]{2,1,0:T(8,128)S(1)}, f32[2,256,256]{2,1,0:T(8,128)}, u32[]{:S(2)}) copy-start(f32[2,256,256]{2,1,0:T(8,128)} %own_ref.1) | copy-start | bytes 1572868
  0.6 44.2 %copy-start.1 = (f32[2,256,256]{2,1,0:T(8,128)S(1)}, f32[2,256,256]{2,1,0:T(8,128)}, u32[]{:S(2)}) copy-start(f32[2,256,256]{2,1,0:T(8,128)} %probe_ref.1) | copy-start | bytes 1572868
  0.7 44.2 %copy-start.7 = (bf16[1,1,4,256,256]{4,3,2,1,0:T(8,128)(2,1)S(1)}, bf16[1,1,4,256,256]{4,3,2,1,0:T(8,128)(2,1)}, u32[]{:S(2)}) copy-start(bf16[1,1,4,256,256]{4,3,2,1,0:T(8,128)(2,1)} %measured_ref.1) | copy-start | bytes 1572868
  0.7 44.2 %copy-start.13 = (s32[1,32]{1,0:T(1,128)S(1)}, s32[1,32]{1,0:T(1,128)}, u32[]{:S(2)}) copy-start(s32[1,32]{1,0:T(1,128)} %counts_ref.3) | copy-start | bytes 388
  0.7 12.1 %collective-permute-start.1 = (f32[2,256,256]{2,1,0:T(8,128)}, f32[2,256,256]{2,1,0:T(8,128)S(1)}, u32[]{:S(2)}, u32[]{:S(2)}) collective-permute-start(f32[2,256,256]{2,1,0:T(8,128)} %own_ref.1), channel_id=1, source_target_pairs={{1,0},{2,1},{3,2},{4,3},{5,4},{6,5},{7,6},{8,7},{9,8},{10,9},{11,1... | collective-permute-start | bytes 1572872 | tf_op jit(solution)/shard_map/ppermute | solution.py:270
  9.6 15.7 %collective-permute-start = (f32[2,256,256]{2,1,0:T(8,128)}, f32[2,256,256]{2,1,0:T(8,128)S(1)}, u32[]{:S(2)}, u32[]{:S(2)}) collective-permute-start(f32[2,256,256]{2,1,0:T(8,128)} %own_ref.1), channel_id=1, source_target_pairs={{32,0},{64,32},{96,64},{128,96},{160,128},{192,160},{224,192},{256... | collective-permute-start | bytes 1572872 | tf_op jit(solution)/shard_map/ppermute | solution.py:270
  12.8 28.9 %copy-start.9 = (f32[2,256,256]{2,1,0:T(8,128)}, f32[2,256,256]{2,1,0:T(8,128)S(1)}, u32[]{:S(2)}) copy-start(f32[2,256,256]{2,1,0:T(8,128)S(1)} %collective-permute-done.1.right_ref) | copy-start | bytes 1572868
  25.3 16.3 %copy-start.11 = (f32[2,256,256]{2,1,0:T(8,128)}, f32[2,256,256]{2,1,0:T(8,128)S(1)}, u32[]{:S(2)}) copy-start(f32[2,256,256]{2,1,0:T(8,128)S(1)} %collective-permute-done.below_ref) | copy-start | bytes 1572868
  25.3 15.2 %collective-permute-start.3 = (f32[2,256,256]{2,1,0:T(8,128)}, f32[2,256,256]{2,1,0:T(8,128)S(1)}, u32[]{:S(2)}, u32[]{:S(2)}) collective-permute-start(f32[2,256,256]{2,1,0:T(8,128)} %d_own_ref.1), channel_id=1, source_target_pairs={{32,0},{64,32},{96,64},{128,96},{160,128},{192,160},{224,192},{256... | collective-permute-start | bytes 1572872 | tf_op jit(solution)/shard_map/ppermute | solution.py:270
  26.6 13.9 %collective-permute-start.2 = (f32[2,256,256]{2,1,0:T(8,128)S(1)}, f32[2,256,256]{2,1,0:T(8,128)}, u32[]{:S(2)}, u32[]{:S(2)}) collective-permute-start(f32[2,256,256]{2,1,0:T(8,128)S(1)} %collective-permute-done.below_ref), channel_id=1, source_target_pairs={{1,0},{2,1},{3,2},{4,3},{5,4},{6,5},{7,6},{8,7},{9,8},{10,9},{11,1... | collective-permute-start | bytes 1572872 | tf_op jit(solution)/shard_map/ppermute | solution.py:270
  41.7 26.3 %collective-permute-start.4 = (f32[2,512,256]{2,1,0:T(8,128)S(1)}, f32[2,512,256]{2,1,0:T(8,128)S(1)}, u32[]{:S(2)}, u32[]{:S(2)}) collective-permute-start(f32[2,512,256]{2,1,0:T(8,128)S(1)} %pad_maximum_fusion), channel_id=1, source_target_pairs={{1,0},{2,1},{3,2},{4,3},{5,4},{6,5},{7,6},{8,7},{9,8},{10,9},{11,1... | collective-permute-start | bytes 3145736 | tf_op jit(solution)/shard_map/ppermute | solution.py:270
  44.9 1.0 copy-start.10
  45.9 1.0 copy-start.12
  65.5 20.7 %collective-permute-start.5 = (f32[2,512,256]{2,1,0:T(8,128)}, f32[2,512,256]{2,1,0:T(8,128)}, u32[]{:S(2)}, u32[]{:S(2)}) collective-permute-start(f32[2,512,256]{2,1,0:T(8,128)} %get-tuple-element.31), channel_id=1, source_target_pairs={{0,1},{1,2},{2,3},{3,4},{4,5},{5,6},{6,7},{7,8},{8,9},{9,10},{10,1... | collective-permute-start | bytes 3145736 | tf_op jit(solution)/shard_map/ppermute | solution.py:270
  68.0 1.0 copy-start.5
  86.2 36.7 %copy-start = (f32[2,256,256]{2,1,0:T(8,128)S(1)}, f32[2,256,256]{2,1,0:T(8,128)}, u32[]{:S(2)}) copy-start(f32[2,256,256]{2,1,0:T(8,128)} %d_own_ref.1) | copy-start | bytes 1572868
  87.7 1.0 copy-start.14
  88.8 34.1 %collective-permute-start.6 = (f32[2,256,256]{2,1,0:T(8,128)S(1)}, f32[2,256,256]{2,1,0:T(8,128)S(1)}, u32[]{:S(2)}, u32[]{:S(2)}) collective-permute-start(f32[2,256,256]{2,1,0:T(8,128)S(1)} %slice.33), channel_id=1, source_target_pairs={{0,32},{32,64},{64,96},{96,128},{128,160},{160,192},{192,224},{224... | collective-permute-start | bytes 1572872 | tf_op jit(solution)/shard_map/ppermute | solution.py:270
  124.7 19.5 %collective-permute-start.7 = (f32[2,256,256]{2,1,0:T(8,128)S(1)}, f32[2,256,256]{2,1,0:T(8,128)S(1)}, u32[]{:S(2)}, u32[]{:S(2)}) collective-permute-start(f32[2,256,256]{2,1,0:T(8,128)S(1)} %get-tuple-element.46.g_own_ref), channel_id=1, source_target_pairs={{32,0},{64,32},{96,64},{128,96},{160,128},{192,160},{224,192},{256... | collective-permute-start | bytes 1572872 | tf_op jit(solution)/shard_map/ppermute | solution.py:270
  144.2 5.7 %copy-start.3 = (f32[2,256,256]{2,1,0:T(8,128)}, f32[2,256,256]{2,1,0:T(8,128)S(1)}, u32[]{:S(2)}) copy-start(f32[2,256,256]{2,1,0:T(8,128)S(1)} %collective-permute-done.7.g_below_ref) | copy-start | bytes 1572868
  145.4 24.2 %collective-permute-start.8 = (f32[2,512,256]{2,1,0:T(8,128)}, f32[2,512,256]{2,1,0:T(8,128)}, u32[]{:S(2)}, u32[]{:S(2)}) collective-permute-start(f32[2,512,256]{2,1,0:T(8,128)} %pad_maximum_fusion.1), channel_id=1, source_target_pairs={{1,0},{2,1},{3,2},{4,3},{5,4},{6,5},{7,6},{8,7},{9,8},{10,9},{11,1... | collective-permute-start | bytes 3145736 | tf_op jit(solution)/shard_map/ppermute | solution.py:270
  149.9 19.7 %all-to-all-start.3 = ((f32[16,33,256]{2,1,0:T(8,128)}), f32[16,33,256]{2,1,0:T(8,128)S(1)}, u32[]{:S(2)}, u32[]{:S(2)}) async-start(f32[16,33,256]{2,1,0:T(8,128)} %broadcast_in_dim.46), calls=%async_computation.3 | async-start | bytes 1310720 | tf_op jit(solution)/shard_map/all_to_all | solution.py:282
  169.6 1.0 copy-start.4
  170.7 1.2 copy-start.6
  171.9 1.0 copy-start.8
  186.1 9.8 %all-to-all-start.4 = ((f32[16,1,128]{2,1,0:T(1,128)}), f32[16,1,128]{2,1,0:T(1,128)S(1)}, u32[]{:S(2)}, u32[]{:S(2)}) async-start(f32[16,1,128]{2,1,0:T(1,128)} %broadcast_in_dim.48), calls=%async_computation.4 | async-start | bytes 16384 | tf_op jit(solution)/shard_map/all_to_all | solution.py:282
  196.5 18.7 %all-to-all-start.5 = ((f32[32,1,128]{2,1,0:T(1,128)}), f32[32,1,128]{2,1,0:T(1,128)S(1)}, u32[]{:S(2)}, u32[]{:S(2)}) async-start(f32[32,1,128]{2,1,0:T(1,128)} %broadcast_in_dim.49), calls=%async_computation.5 | async-start | bytes 32768 | tf_op jit(solution)/shard_map/all_to_all | solution.py:282

commit v2 on v0

v2 whole, which is shorter than its diff:
```python
import functools
import math

import jax
import jax.numpy as jnp
import numpy as np
from jax import lax
from jax.experimental import pallas as pl
from jax.experimental.pallas import tpu as pltpu
from jax.sharding import PartitionSpec as P

VMEM_BYTES = 60 * 1024 * 1024


def dft_blocks(width):
    at = np.arange(width)
    angle = (np.outer(at, at) % width) * (2.0 * math.pi / width)
    cosine = (np.cos(angle) / math.sqrt(width)).astype(np.float32)
    sine = (np.sin(angle) / math.sqrt(width)).astype(np.float32)

    def thrice(table):
        high = table.astype(jnp.bfloat16)
        low = (table - high.astype(np.float32)).astype(jnp.bfloat16)
        return np.concatenate([high, low, high], axis=1)

    real_rows = np.concatenate([thrice(cosine), thrice(sine)], axis=1)
    imag_rows = np.concatenate([thrice(-sine), thrice(cosine)], axis=1)
    left = np.concatenate([real_rows, imag_rows], axis=0)
    return left, np.ascontiguousarray(left.T)


def split_halves(value):
    high = value.astype(jnp.bfloat16)
    low = (value - high.astype(jnp.float32)).astype(jnp.bfloat16)
    return high, low


def dft_pairs(pairs, tables, scratch):
    left_ref, right_ref = tables
    tall_ref, wide_ref = scratch
    width = pairs[0][0].shape[0]
    for which, pair in enumerate(pairs):
        for at, part in enumerate(pair):
            high, low = split_halves(part)
            base = 3 * at * width
            tall_ref[which, base : base + width, :] = high
            tall_ref[which, base + width : base + 2 * width, :] = high
            tall_ref[which, base + 2 * width : base + 3 * width, :] = low
    results = []
    left_ref = left_ref()
    for which in range(len(pairs)):
        middle = jnp.dot(left_ref[...], tall_ref[which], preferred_element_type=jnp.float32)
        for at in range(2):
            high, low = split_halves(middle[at * width : (at + 1) * width])
            base = 3 * at * width
            wide_ref[which, :, base : base + width] = high
            wide_ref[which, :, base + width : base + 2 * width] = high
            wide_ref[which, :, base + 2 * width : base + 3 * width] = low
    right_ref = right_ref()
    for which in range(len(pairs)):
        done = jnp.dot(wide_ref[which], right_ref[...], preferred_element_type=jnp.float32)
        results.append((done[:, :width], done[:, width:]))
    return results


def rolled(value, row, col):
    return pltpu.roll(pltpu.roll(value, row, 0), col, 1)


def wrapped(own, below, right, diag, upper, nearer):
    return jnp.where(nearer, jnp.where(upper, own, below), jnp.where(upper, right, diag))


def masks(row, col, width):
    upper = lax.broadcasted_iota(jnp.int32, (width, width), 0) >= row
    nearer = lax.broadcasted_iota(jnp.int32, (width, width), 1) >= col
    return upper, nearer


def corner(positions_ref, slot, width):
    row = lax.rem(positions_ref[0, 0, slot, 0], width)
    col = lax.rem(positions_ref[0, 0, slot, 1], width)
    return row, col


def live_count(counts_ref):
    return counts_ref[0, lax.axis_index("col")]


class Incoming:
    def __init__(self, source, target, semaphore):
        self.target = target
        self.copy = pltpu.make_async_copy(source, target, semaphore)
        self.copy.start()
        self.waiting = True

    def __call__(self):
        if self.waiting:
            self.copy.wait()
            self.waiting = False
        return self.target


def incoming(sources, targets, semaphores):
    return [
        Incoming(source, target, semaphores.at[at])
        for at, (source, target) in enumerate(zip(sources, targets))
    ]


def outgoing(sources, targets, semaphores, first=0):
    sent = [
        pltpu.make_async_copy(source, target, semaphores.at[first + at])
        for at, (source, target) in enumerate(zip(sources, targets))
    ]
    for copy in sent:
        copy.start()
    return sent


def gradient_kernel(
    positions_ref,
    counts_ref,
    own_any,
    below_any,
    right_any,
    diag_any,
    probe_any,
    measured_any,
    left_any,
    right_table_any,
    own_grad_any,
    below_grad_any,
    right_grad_any,
    diag_grad_any,
    probe_grad_any,
    patch_any,
    moved_any,
    far_any,
    tiles_ref,
    probe_ref,
    measured_ref,
    left_ref,
    right_ref,
    grads_ref,
    patch_ref,
    moved_ref,
    far_ref,
    tall_ref,
    wide_ref,
    in_sems,
    out_sems,
):
    width = probe_ref.shape[-1]
    live = live_count(counts_ref)
    *ready, left, measured, right = incoming(
        [own_any, below_any, right_any, diag_any, probe_any]
        + [left_any, measured_any.at[0, 0], right_table_any],
        [tiles_ref.at[at] for at in range(4)] + [probe_ref, left_ref, measured_ref, right_ref],
        in_sems,
    )
    for arrival in ready:
        arrival()

    def both(first):
        slots = (first, first + 1)
        spots = [corner(positions_ref, slot, width) for slot in slots]
        waves = []
        for slot, (row, col) in zip(slots, spots):
            upper, nearer = masks(row, col, width)
            for part in range(2):
                patch_ref[slot, part] = wrapped(
                    *[tiles_ref[at, part] for at in range(4)], upper, nearer
                )
                moved_ref[slot, part] = rolled(probe_ref[part], row, col)
            patch_r, patch_i = patch_ref[slot, 0], patch_ref[slot, 1]
            probe_r, probe_i = moved_ref[slot, 0], moved_ref[slot, 1]
            kept = slot < live
            waves.append(
                (
                    jnp.where(kept, probe_r * patch_r - probe_i * patch_i, 0.0),
                    jnp.where(kept, probe_r * patch_i + probe_i * patch_r, 0.0),
                )
            )
        span = pl.ds(first, 2)
        sent = outgoing(
            [patch_ref.at[span], moved_ref.at[span]],
            [patch_any.at[span], moved_any.at[span]],
            out_sems,
            5 + 3 * (first // 2),
        )
        fars = dft_pairs(waves, (left, right), (tall_ref, wide_ref))
        turned = []
        measured()
        for slot, (far_r, far_i) in zip(slots, fars):
            far_ref[slot, 0] = far_r
            far_ref[slot, 1] = far_i
            residue = far_r * far_r + far_i * far_i - measured_ref[slot].astype(jnp.float32)
            turned.append((residue * far_i, residue * far_r))
        sent += outgoing(
            [far_ref.at[span]], [far_any.at[span]], out_sems, 7 + 3 * (first // 2)
        )
        backs = dft_pairs(turned, (left, right), (tall_ref, wide_ref))
        pieces = []
        for slot, (row, col), (back_i, back_r) in zip(slots, spots, backs):
            patch_r, patch_i = patch_ref[slot, 0], patch_ref[slot, 1]
            back_row = lax.rem(width - row, width)
            back_col = lax.rem(width - col, width)
            pieces.append(
                (
                    rolled(patch_r * back_r + patch_i * back_i, back_row, back_col),
                    rolled(patch_r * back_i - patch_i * back_r, back_row, back_col),
                )
            )
        for part in range(2):
            total = pieces[0][part] + pieces[1][part]
            grads_ref[4, part] = total if first == 0 else grads_ref[4, part] + total
        for part in range(2):
            sums = [0.0, 0.0, 0.0, 0.0]
            for slot, (row, col), (back_i, back_r) in zip(slots, spots, backs):
                upper, nearer = masks(row, col, width)
                probe_r, probe_i = moved_ref[slot, 0], moved_ref[slot, 1]
                if part == 0:
                    term = probe_r * back_r + probe_i * back_i
                else:
                    term = probe_r * back_i - probe_i * back_r
                close = jnp.where(nearer, term, 0.0)
                beyond = term - close
                for at, side in enumerate((close, beyond)):
                    top = jnp.where(upper, side, 0.0)
                    sums[2 * at] = sums[2 * at] + top
                    sums[2 * at + 1] = sums[2 * at + 1] + (side - top)
            for at, total in enumerate(sums):
                grads_ref[at, part] = total if first == 0 else grads_ref[at, part] + total
        for copy in sent:
            copy.wait()

    both(0)
    pl.when(live > 2)(lambda: both(2))
    outs = [own_grad_any, below_grad_any, right_grad_any, diag_grad_any, probe_grad_any]
    for copy in outgoing([grads_ref.at[at] for at in range(5)], outs, out_sems):
        copy.wait()


def linear_frames(positions_ref, live, tiles, change, kept, tables, scratch, finish):
    own_ref, below_ref, right_ref, diag_ref = [tile() for tile in tiles]
    change_ref = change()
    width = own_ref.shape[-1]

    def both(first, patches, moves, fars):
        slots = (first, first + 1)
        patch_ref, moved_ref = patches(), moves()
        waves = []
        for at, slot in enumerate(slots):
            row, col = corner(positions_ref, slot, width)
            upper, nearer = masks(row, col, width)
            step_r, step_i = [
                wrapped(own_ref[part], below_ref[part], right_ref[part], diag_ref[part], upper, nearer)
                for part in range(2)
            ]
            patch_r, patch_i = patch_ref[at, 0], patch_ref[at, 1]
            probe_r, probe_i = moved_ref[at, 0], moved_ref[at, 1]
            change_r = rolled(change_ref[0], row, col)
            change_i = rolled(change_ref[1], row, col)
            waves.append(
                (
                    probe_r * step_r - probe_i * step_i + change_r * patch_r - change_i * patch_i,
                    probe_r * step_i + probe_i * step_r + change_r * patch_i + change_i * patch_r,
                )
            )
        steps = dft_pairs(waves, tables, scratch)
        far_ref = fars()
        quads = [
            2.0 * (far_ref[at, 0] * step_r + far_ref[at, 1] * step_i)
            for at, (step_r, step_i) in enumerate(steps)
        ]
        finish(slots, quads)

    both(0, *kept[0])
    for arrival in kept[1]:
        arrival()
    pl.when(live > 2)(lambda: both(2, *kept[1]))


def halves(array, ref):
    return [(array.at[pl.ds(first, 2)], ref.at[pl.ds(first, 2)]) for first in (0, 2)]


def previous_kernel(
    positions_ref,
    counts_ref,
    own_any,
    below_any,
    right_any,
    diag_any,
    change_any,
    patch_any,
    moved_any,
    far_any,
    left_any,
    right_table_any,
    quad_any,
    sums_ref,
    tiles_ref,
    change_ref,
    patch_ref,
    moved_ref,
    far_ref,
    left_ref,
    right_ref,
    quad_ref,
    tall_ref,
    wide_ref,
    in_sems,
    out_sem,
):
    live = live_count(counts_ref)
    kept = [
        halves(patch_any, patch_ref),
        halves(moved_any, moved_ref),
        halves(far_any, far_ref),
    ]
    moves = [(change_any, change_ref)]
    moves += [
        (tile, tiles_ref.at[at]) for at, tile in enumerate((own_any, below_any, right_any, diag_any))
    ]
    moves += [kept[0][0], kept[1][0], (left_any, left_ref), (right_table_any, right_ref), kept[2][0]]
    moves += [kept[0][1], kept[1][1], kept[2][1]]
    change, *arrivals = incoming(*zip(*moves), in_sems)
    tiles, (patch, moved, left, right, far), later = arrivals[:4], arrivals[4:9], arrivals[9:]
    lane = lax.broadcasted_iota(jnp.int32, (1, 128), 1)
    sums_ref[...] = jnp.zeros_like(sums_ref)

    def finish(slots, quads):
        row = sums_ref[...]
        for slot, quad in zip(slots, quads):
            quad_ref[slot] = quad
            square = jnp.sum(quad * quad)
            row = row + jnp.where((lane == 2) | (lane == 16 + slot), square, 0.0)
        sums_ref[...] = row

    linear_frames(
        positions_ref,
        live,
        tiles,
        change,
        ((patch, moved, far), later),
        (left, right),
        (tall_ref, wide_ref),
        finish,
    )
    copy = pltpu.make_async_copy(quad_ref, quad_any, out_sem)
    copy.start()
    copy.wait()


def curvature_kernel(
    positions_ref,
    counts_ref,
    own_any,
    below_any,
    right_any,
    diag_any,
    total_any,
    patch_any,
    moved_any,
    far_any,
    left_any,
    right_table_any,
    prev_any,
    quad_any,
    prev_sums_ref,
    prev_probe_any,
    sums_ref,
    change_any,
    tiles_ref,
    total_ref,
    change_ref,
    patch_ref,
    moved_ref,
    far_ref,
    left_ref,
    right_ref,
    quad_ref,
    prev_ref,
    prev_probe_ref,
    tall_ref,
    wide_ref,
    in_sems,
    out_sem,
    *,
    probe_scale,
):
    live = live_count(counts_ref)
    kept = [
        halves(patch_any, patch_ref),
        halves(moved_any, moved_ref),
        halves(far_any, far_ref),
    ]
    moves = [(total_any, total_ref)]
    moves += [
        (tile, tiles_ref.at[at]) for at, tile in enumerate((own_any, below_any, right_any, diag_any))
    ]
    moves += [kept[0][0], kept[1][0], (left_any, left_ref), (right_table_any, right_ref), kept[2][0]]
    moves += [kept[0][1], kept[1][1], kept[2][1]]
    moves += [(quad_any, quad_ref), (prev_any, prev_ref), (prev_probe_any, prev_probe_ref)]
    total, *arrivals = incoming(*zip(*moves), in_sems)
    tiles, (patch, moved, left, right, far), later = arrivals[:4], arrivals[4:9], arrivals[9:12]
    quad_in, prev, prev_probe = arrivals[12:]
    change_ref[...] = total()[...].reshape(change_ref.shape) * probe_scale
    copy = pltpu.make_async_copy(change_ref, change_any, out_sem)
    copy.start()
    lane = lax.broadcasted_iota(jnp.int32, (1, 128), 1)
    sums_ref[...] = prev_sums_ref[...]

    def finish(slots, quads):
        quad_in()
        row = sums_ref[...]
        for slot, quad in zip(slots, quads):
            square = jnp.sum(quad * quad)
            cross = jnp.sum(quad * quad_ref[slot])
            row = row + jnp.where((lane == 0) | (lane == 8 + slot), square, 0.0)
            row = row + jnp.where((lane == 1) | (lane == 12 + slot), cross, 0.0)
        sums_ref[...] = row

    linear_frames(
        positions_ref,
        live,
        tiles,
        lambda: change_ref,
        ((patch, moved, far), later),
        (left, right),
        (tall_ref, wide_ref),
        finish,
    )
    prev()
    prev_probe()
    own = tiles_ref[0]
    probe_grad = change_ref[...]
    values = [
        (3, jnp.sum(own * own)),
        (4, jnp.sum(own * prev_ref[...])),
        (20, jnp.sum(probe_grad * probe_grad)),
        (21, jnp.sum(probe_grad * prev_probe_ref[...])),
    ]
    row = sums_ref[...]
    for at, value in values:
        row = jnp.where(lane == at, value, row)
    sums_ref[...] = row
    copy.wait()


def update_kernel(
    prev_norm_ref,
    gathered_ref,
    sums_ref,
    object_any,
    object_grad_any,
    object_prev_any,
    probe_any,
    probe_grad_any,
    probe_prev_any,
    object_new_any,
    probe_new_any,
    object_direction_any,
    probe_direction_any,
    row_ref,
    held_ref,
    made_ref,
    in_sems,
    out_sems,
):
    sources = [object_prev_any, object_grad_any, object_any]
    sources += [probe_prev_any, probe_grad_any, probe_any]
    arrivals = incoming(sources, [held_ref.at[at] for at in range(6)], in_sems)
    total = jnp.sum(gathered_ref[...], axis=0)
    local = sums_ref[...]
    lane = lax.broadcasted_iota(jnp.int32, (1, 128), 1)

    def pick(row, at):
        return jnp.sum(jnp.where(lane == at, row, 0.0))

    grad_norm = pick(total, 3) + pick(local, 20)
    along_prev = pick(total, 4) + pick(local, 21)
    ratio = grad_norm / prev_norm_ref[0]
    descent = grad_norm - ratio * along_prev
    curvature = pick(total, 0) - 2.0 * ratio * pick(total, 1) + ratio * ratio * pick(total, 2)
    step_size = descent / (0.5 * curvature + 1e-06)
    outs = [object_direction_any, object_new_any, probe_direction_any, probe_new_any]
    sent = []
    for first in (0, 3):
        at = 2 * (first // 3)
        prev, grad, field = [arrival()[...] for arrival in arrivals[first : first + 3]]
        direction = ratio * prev - grad
        made_ref[at] = direction
        made_ref[at + 1] = field + step_size * direction
        span = range(at, at + 2)
        sent += outgoing([made_ref.at[i] for i in span], [outs[i] for i in span], out_sems, at)
    pixels = held_ref.shape[-1] * held_ref.shape[-2]
    row = jnp.where(lane == 4, grad_norm, 0.0)
    for slot in range(4):
        frame_sum = (
            pick(local, 8 + slot)
            - 2.0 * ratio * pick(local, 12 + slot)
            + ratio * ratio * pick(local, 16 + slot)
        )
        row = jnp.where(lane == slot, frame_sum / pixels, row)
    row_ref[...] = row
    for copy in sent:
        copy.wait()


def shaped(*dims):
    return jax.ShapeDtypeStruct(dims, jnp.float32)


def buffer(*dims, dtype=jnp.float32):
    return pltpu.VMEM(dims, dtype)


def arrivals_of(count):
    return pltpu.SemaphoreType.DMA((count,))


def anywhere(count):
    return [pl.BlockSpec(memory_space=pl.ANY)] * count


def in_hbm(count):
    return [pl.BlockSpec(memory_space=pltpu.HBM)] * count


def in_vmem(count):
    return [pl.BlockSpec(memory_space=pltpu.VMEM)] * count


def in_smem(count):
    return [pl.BlockSpec(memory_space=pltpu.SMEM)] * count


def table_buffers(width):
    return [
        buffer(2 * width, 6 * width, dtype=jnp.bfloat16),
        buffer(6 * width, 2 * width, dtype=jnp.bfloat16),
    ]


def dft_scratch(width):
    return [
        buffer(2, 6 * width, width, dtype=jnp.bfloat16),
        buffer(2, width, 6 * width, dtype=jnp.bfloat16),
    ]


def costing(flops):
    return {
        "compiler_params": pltpu.CompilerParams(vmem_limit_bytes=VMEM_BYTES),
        "cost_estimate": pl.CostEstimate(flops=flops, bytes_accessed=10**7, transcendentals=0),
    }


def gradient_call(positions, counts, tiles, probe, measured, tables):
    width = probe.shape[-1]
    slots = measured.shape[2]
    frames = buffer(slots, 2, width, width)
    return pl.pallas_call(
        gradient_kernel,
        out_shape=(shaped(2, width, width),) * 5 + (shaped(slots, 2, width, width),) * 3,
        in_specs=in_smem(2) + anywhere(4) + in_hbm(4),
        out_specs=(*anywhere(5), *in_hbm(3)),
        scratch_shapes=[
            buffer(4, 2, width, width),
            buffer(2, width, width),
            buffer(slots, width, width, dtype=measured.dtype),
            *table_buffers(width),
            buffer(5, 2, width, width),
            frames,
            frames,
            frames,
            *dft_scratch(width),
            arrivals_of(8),
            arrivals_of(11),
        ],
        name="gradient_frames",
        **costing(10**10),
    )(positions, counts, *tiles, probe, measured, *tables)


def previous_call(positions, counts, tiles, probe_prev, kept, tables):
    width = probe_prev.shape[-1]
    slots = kept[0].shape[0]
    frames = buffer(slots, 2, width, width)
    return pl.pallas_call(
        previous_kernel,
        out_shape=(shaped(slots, width, width), shaped(1, 128)),
        in_specs=in_smem(2) + anywhere(4) + in_hbm(6),
        out_specs=(*in_hbm(1), *in_vmem(1)),
        scratch_shapes=[
            buffer(4, 2, width, width),
            buffer(2, width, width),
            frames,
            frames,
            frames,
            *table_buffers(width),
            buffer(slots, width, width),
            *dft_scratch(width),
            arrivals_of(13),
            pltpu.SemaphoreType.DMA,
        ],
        name="previous_frames",
        **costing(5 * 10**9),
    )(positions, counts, *tiles, probe_prev, *kept, *tables)


def curvature_call(positions, counts, tiles, total, kept, tables, previous, probe_scale):
    width = tiles[0].shape[-1]
    slots = kept[0].shape[0]
    frames = buffer(slots, 2, width, width)
    return pl.pallas_call(
        functools.partial(curvature_kernel, probe_scale=probe_scale),
        out_shape=(shaped(1, 128), shaped(2, width, width)),
        in_specs=in_smem(2) + anywhere(5) + in_hbm(7) + in_vmem(1) + in_hbm(1),
        out_specs=(*in_vmem(1), *in_hbm(1)),
        scratch_shapes=[
            buffer(4, 2, width, width),
            buffer(*total.shape),
            buffer(2, width, width),
            frames,
            frames,
            frames,
            *table_buffers(width),
            buffer(slots, width, width),
            buffer(2, width, width),
            buffer(2, width, width),
            *dft_scratch(width),
            arrivals_of(16),
            pltpu.SemaphoreType.DMA,
        ],
        name="curvature_frames",
        **costing(5 * 10**9),
    )(positions, counts, *tiles, total, *kept, *tables, *previous)


def update_call(prev_norm, gathered, sums, arrays):
    shape = arrays[0].shape
    return pl.pallas_call(
        update_kernel,
        out_shape=(shaped(*shape),) * 4 + (shaped(1, 128),),
        in_specs=in_smem(1) + in_vmem(2) + in_hbm(6),
        out_specs=(*in_hbm(4), *in_vmem(1)),
        scratch_shapes=[buffer(6, *shape), buffer(4, *shape), arrivals_of(6), arrivals_of(4)],
        name="update",
        **costing(10**6),
    )(prev_norm, gathered, sums, *arrays)


def passed_along(shard, axis, by):
    count = lax.axis_size(axis)
    pairs = [(i, i + by) for i in range(count) if 0 <= i + by < count]
    return lax.ppermute(shard, axis, pairs)


def device_groups(block):
    rows, cols = lax.axis_size("row"), lax.axis_size("col")
    near = [
        [row * cols + first + at for row in range(rows) for at in range(block)]
        for first in range(0, cols, block)
    ]
    return near, [list(members) for members in zip(*near)]


def exchanged(pieces, groups):
    return lax.all_to_all(pieces, ("row", "col"), 0, 0, axis_index_groups=groups)


def copies(piece, groups):
    return jnp.broadcast_to(piece[None], (len(groups[0]),) + piece.shape)


def held(value, *others):
    return lax.optimization_barrier((value,) + others)[0]


def per_device(
    object_field,
    probe_field,
    object_dir_prev,
    probe_dir_prev,
    prev_norm,
    intensities,
    positions,
    counts,
):
    width = probe_field.shape[-1]
    slots = positions.shape[2]
    tables = dft_blocks(width)
    probe_scale = 1.0 / math.sqrt(slots * lax.axis_size("row") * lax.axis_size("col"))
    near, apart = device_groups(4)

    right = passed_along(object_field, "col", -1)
    below = passed_along(object_field, "row", -1)
    diag = passed_along(held(below, right), "col", -1)
    prev_below = passed_along(held(object_dir_prev, below), "row", -1)
    prev_diag = passed_along(held(prev_below, diag), "col", -1)

    own_grad, below_grad, right_grad, diag_grad, probe_part, *kept = gradient_call(
        positions,
        counts,
        (object_field, below, right, held(diag, prev_below)),
        probe_field,
        intensities,
        tables,
    )
    probe_part = held(probe_part, prev_diag)
    from_left_diag = passed_along(diag_grad, "col", 1)
    prev_right = passed_along(held(object_dir_prev, diag_grad), "col", -1)
    pieces = exchanged(probe_part.reshape((len(near[0]), -1, width)), near)
    pieces, from_left_diag = lax.optimization_barrier((pieces, from_left_diag))
    piece = copies(jnp.sum(pieces, axis=0), apart)
    piece, below_sum = lax.optimization_barrier((piece, below_grad + from_left_diag))
    from_above = passed_along(below_sum, "row", 1)
    from_left = passed_along(right_grad, "col", 1)
    pieces = exchanged(piece, apart)
    pieces, from_above, from_left = lax.optimization_barrier((pieces, from_above, from_left))
    piece = copies(jnp.sum(pieces, axis=0), near)
    object_grad = own_grad + from_left + from_above
    piece, object_grad, prev_right = lax.optimization_barrier((piece, object_grad, prev_right))
    grad_below = passed_along(object_grad, "row", -1)
    grad_right = passed_along(object_grad, "col", -1)
    grad_diag = passed_along(grad_below, "col", -1)
    total = exchanged(piece, near)
    prev_tiles = (object_dir_prev, prev_below, prev_right, prev_diag)
    previous = previous_call(positions, counts, prev_tiles, probe_dir_prev, kept, tables)
    total = held(total, grad_right, grad_diag, *previous)
    sums, probe_grad = curvature_call(
        positions,
        counts,
        (object_grad, grad_below, grad_right, grad_diag),
        total,
        kept,
        tables,
        (object_dir_prev, *previous, probe_dir_prev),
        probe_scale,
    )
    near, apart = device_groups(2)
    across = jnp.sum(exchanged(copies(sums, near), near), axis=0)
    across = exchanged(copies(across, apart), apart)
    arrays = (object_field, object_grad, object_dir_prev, probe_field, probe_grad, probe_dir_prev)
    object_new, probe_new, object_direction, probe_direction, row = update_call(
        prev_norm.reshape(1), across, sums, arrays
    )
    return (
        object_new,
        probe_new,
        object_direction,
        probe_direction,
        row[0, slots],
        row[0, :slots].reshape(1, 1, slots),
    )


def solution(mesh):
    return jax.shard_map(
        per_device,
        mesh=mesh,
        in_specs=(
            P(None, "row", "col"),
            P(),
            P(None, "row", "col"),
            P(),
            P(),
            P("row", "col", None, None, None),
            P("row", "col", None, None),
            P("row", None),
        ),
        out_specs=(
            P(None, "row", "col"),
            P(),
            P(None, "row", "col"),
            P(),
            P(),
            P("row", "col", None),
        ),
        check_vma=False,
    )
```

time: 965 us -> 208 us (0.22); the launches traced: 952 us -> 207 us
  waiting for transfers between devices: 516 us -> 62.5 us
  blocking collectives: 205 us -> 11.7 us
  local copies, waits for them, and re-layouts: 91.8 us -> 9.02 us
  starting transfers between devices: 20.7 us -> 79.7 us
  matrix products: 54.7 us -> 0 us
  Pallas kernels: 0 us -> 41 us
  other arithmetic: 27.2 us -> 1.31 us
  between operations: 20.1 us -> 1.63 us
  loops' own time: 16.1 us -> 0 us
    psum x1 -> x0, waiting for transfers between devices: 463 us -> none  [per_device(): lax.psum((probe_part, jnp.stack([obj_square, obj_along])), ('row', 'col'))]
    psum x2 -> x0, blocking collectives: 205 us -> none  [the longest x1 103 us: per_device(): lax.psum((probe_part, jnp.stack([obj_square, obj_along])), ('row', 'col'))]
    dot_general x12 -> x0, matrix products: 54.7 us -> none  [the longest x3 20.1 us: unitary_dft(): left_s = jnp.einsum('jk,bckl->bcjl', sine_table, frames, precision=precise)]
    all_to_all x0 -> x4, starting transfers between devices: none -> 42.7 us  [exchanged(): lax.all_to_all(pieces, ('row', 'col'), 0, 0, axis_index_groups=groups)]
    pallas_call x0 -> x4, Pallas kernels: none -> 41 us  [the longest x1 15.5 us: gradient_call(): pl.pallas_call(gradient_kernel, out_shape=(shaped(2, width, width),) * 5...]
    gather x44 -> x0, local copies, waits for them, and re-layouts: 32.1 us -> none
    dynamic_update_slice x8 -> x0, local copies, waits for them, and re-layouts: 26.4 us -> none  [add_one(): return lax.dynamic_update_slice(grid, current + piece, anchor)]
    all_to_all x0 -> x4, waiting for transfers between devices: none -> 23.6 us  [exchanged(): lax.all_to_all(pieces, ('row', 'col'), 0, 0, axis_index_groups=groups)]
  transfers between devices with their start and end apart: 7 -> 16, of which waited for: 7 -> 9; matrix products, arithmetic and copies ran while one was open for 2% -> 2% of each run, Pallas kernels for 0% -> 13%
where the time goes in v2:
time: 208 us; the launch traced here: 207 us
  starting transfers between devices  79.7 us (38%)
  waiting for transfers between devices  62.5 us (30%)
  Pallas kernels  41 us (20%)
  blocking collectives  11.7 us (6%)
  local copies, waits for them, and re-layouts  9.02 us (4%)
    all_to_all x4, starting transfers between devices, exchanged(): lax.all_to_all(pieces, ('row', 'col'), 0, 0, axis_index_groups=groups)  42.7 us
    ppermute x12, waiting for transfers between devices, passed_along(): return lax.ppermute(shard, axis, pairs)  38.9 us
    ppermute x12, starting transfers between devices, passed_along(): return lax.ppermute(shard, axis, pairs)  37 us
    all_to_all x4, waiting for transfers between devices, exchanged(): lax.all_to_all(pieces, ('row', 'col'), 0, 0, axis_index_groups=groups)  23.6 us
    pallas_call x1, Pallas kernels, gradient_call(): pl.pallas_call(gradient_kernel, out_shape=(shaped(2, width, width),) * 5...  15.5 us
    all_to_all x1, blocking collectives, exchanged(): lax.all_to_all(pieces, ('row', 'col'), 0, 0, axis_index_groups=groups)  11.7 us
    pallas_call x1, Pallas kernels, previous_call(): pl.pallas_call(previous_kernel, out_shape=(shaped(slots, width, width), s...  10.7 us
    pallas_call x1, Pallas kernels, curvature_call(): pl.pallas_call(functools.partial(curvature_kernel, probe_scale=probe_scal...  10.4 us
  transfers between devices with their start and end apart: 16, of which 9 were waited for; matrix products, arithmetic and copies ran while one was open for 2% of the time, Pallas kernels for 13%

profile of v2, /device:TPU:1, one launch (start us, length us, event | category | flops | bytes accessed | tf_op | source)
XLA Modules:
  0.0 206.9 jit_solution(12330138543830720691)
XLA Ops:
  0.6 1.3 collective-permute-start
  1.9 8.8 %collective-permute-start.1 = (f32[2,256,256]{2,1,0:T(8,128)}, f32[2,256,256]{2,1,0:T(8,128)S(1)}, u32[]{:S(2)}, u32[]{:S(2)}) collective-permute-start(f32[2,256,256]{2,1,0:T(8,128)} %object_any.1), channel_id=1, source_target_pairs={{1,0},{2,1},{3,2},{4,3},{5,4},{6,5},{7,6},{8,7},{9,8},{10,9},{11,1... | collective-permute-start | bytes 1572872 | tf_op jit(solution)/shard_map/ppermute | solution.py:660
  11.4 2.8 %collective-permute-done.1.right_any = f32[2,256,256]{2,1,0:T(8,128)S(1)} collective-permute-done((f32[2,256,256]{2,1,0:T(8,128)}, f32[2,256,256]{2,1,0:T(8,128)S(1)}, u32[]{:S(2)}, u32[]{:S(2)}) %collective-permute-start.1) | collective-permute-done | bytes 524320 | tf_op jit(solution)/shard_map/ppermute | solution.py:660
  14.2 6.5 %collective-permute-start.2 = (f32[2,256,256]{2,1,0:T(8,128)S(1)}, f32[2,256,256]{2,1,0:T(8,128)S(1)}, u32[]{:S(2)}, u32[]{:S(2)}) collective-permute-start(f32[2,256,256]{2,1,0:T(8,128)S(1)} %collective-permute-done.below_any), channel_id=1, source_target_pairs={{1,0},{2,1},{3,2},{4,3},{5,4},{6,5},{7,6},{8,7},{9,8},{10,9},{11,1... | collective-permute-start | bytes 1572872 | tf_op jit(solution)/shard_map/ppermute | solution.py:660
  20.7 1.3 collective-permute-start.3
  22.0 1.3 copy.24.positions_ref
  23.4 5.1 %collective-permute-done.2.diag_any = f32[2,256,256]{2,1,0:T(8,128)S(1)} collective-permute-done((f32[2,256,256]{2,1,0:T(8,128)S(1)}, f32[2,256,256]{2,1,0:T(8,128)S(1)}, u32[]{:S(2)}, u32[]{:S(2)}) %collective-permute-start.2) | collective-permute-done | bytes 524320 | tf_op jit(solution)/shard_map/ppermute | solution.py:660
  28.5 8.0 %collective-permute-done.3.below_any = f32[2,256,256]{2,1,0:T(8,128)S(1)} collective-permute-done((f32[2,256,256]{2,1,0:T(8,128)}, f32[2,256,256]{2,1,0:T(8,128)S(1)}, u32[]{:S(2)}, u32[]{:S(2)}) %collective-permute-start.3) | collective-permute-done | bytes 524320 | tf_op jit(solution)/shard_map/ppermute | solution.py:660
  36.5 2.3 %collective-permute-start.4 = (f32[2,256,256]{2,1,0:T(8,128)S(1)}, f32[2,256,256]{2,1,0:T(8,128)S(1)}, u32[]{:S(2)}, u32[]{:S(2)}) collective-permute-start(f32[2,256,256]{2,1,0:T(8,128)S(1)} %collective-permute-done.3.below_any), channel_id=1, source_target_pairs={{1,0},{2,1},{3,2},{4,3},{5,4},{6,5},{7,6},{8,7},{9,8},{10,9},{11,1... | collective-permute-start | bytes 1572872 | tf_op jit(solution)/shard_map/ppermute | solution.py:660
  38.8 15.5 %gradient_frames.1 = (f32[2,256,256]{2,1,0:T(8,128)}, f32[2,256,256]{2,1,0:T(8,128)}, f32[2,256,256]{2,1,0:T(8,128)}, f32[2,256,256]{2,1,0:T(8,128)}, f32[2,256,...) custom-call(s32[1,1,4,2]{3,2,1,0:T(4,128)} %copy.24.positions_ref, ...), custom_call_target="tpu_custom_call" | custom-call | flops 10000000000 | bytes 10000000 | tf_op jit(solution)/shard_map/gradient_frames/pallas_call | solution.py:566
  55.2 12.3 %all-to-all-start = ((f32[64,8,256]{2,1,0:T(8,128)}), f32[64,8,256]{2,1,0:T(8,128)S(1)}, u32[]{:S(2)}, u32[]{:S(2)}) async-start(f32[64,8,256]{2,1,0:T(8,128)} %bitcast.8), calls=%async_computation | async-start | bytes 1048576 | tf_op jit(solution)/shard_map/all_to_all | solution.py:673
  67.5 3.5 %collective-permute-start.5 = (f32[2,256,256]{2,1,0:T(8,128)}, f32[2,256,256]{2,1,0:T(8,128)S(1)}, u32[]{:S(2)}, u32[]{:S(2)}) collective-permute-start(f32[2,256,256]{2,1,0:T(8,128)} %get-tuple-element.46), channel_id=1, source_target_pairs={{0,1},{1,2},{2,3},{3,4},{4,5},{5,6},{6,7},{7,8},{8,9},{9,10},{10,1... | collective-permute-start | bytes 1572872 | tf_op jit(solution)/shard_map/ppermute | solution.py:660
  71.0 2.1 collective-permute-start.7
  73.1 6.1 %collective-permute-done.5 = f32[2,256,256]{2,1,0:T(8,128)S(1)} collective-permute-done((f32[2,256,256]{2,1,0:T(8,128)}, f32[2,256,256]{2,1,0:T(8,128)S(1)}, u32[]{:S(2)}, u32[]{:S(2)}) %collective-permute-start.5) | collective-permute-done | bytes 524320 | tf_op jit(solution)/shard_map/ppermute | solution.py:660
  80.3 1.1 add.9
  82.1 2.2 %collective-permute-start.6 = (f32[2,256,256]{2,1,0:T(8,128)S(1)}, f32[2,256,256]{2,1,0:T(8,128)S(1)}, u32[]{:S(2)}, u32[]{:S(2)}) collective-permute-start(f32[2,256,256]{2,1,0:T(8,128)S(1)} %add.9), channel_id=1, source_target_pairs={{0,32},{32,64},{64,96},{96,128},{128,160},{160,192},{192,224},{224... | collective-permute-start | bytes 1572872 | tf_op jit(solution)/shard_map/ppermute | solution.py:660
  84.3 2.7 %collective-permute-start.8 = (f32[2,256,256]{2,1,0:T(8,128)S(1)}, f32[2,256,256]{2,1,0:T(8,128)}, u32[]{:S(2)}, u32[]{:S(2)}) collective-permute-start(f32[2,256,256]{2,1,0:T(8,128)S(1)} %copy-done.2), channel_id=1, source_target_pairs={{1,0},{2,1},{3,2},{4,3},{5,4},{6,5},{7,6},{8,7},{9,8},{10,9},{11,1... | collective-permute-start | bytes 1572872 | tf_op jit(solution)/shard_map/ppermute | solution.py:660
  87.0 14.3 %all-to-all-start.1 = ((f32[8,8,256]{2,1,0:T(8,128)}), f32[8,8,256]{2,1,0:T(8,128)S(1)}, u32[]{:S(2)}, u32[]{:S(2)}) async-start(f32[8,8,256]{2,1,0:T(8,128)} %broadcast_in_dim.10), calls=%async_computation.1 | async-start | bytes 131072 | tf_op jit(solution)/shard_map/all_to_all | solution.py:673
  101.4 11.9 %all-to-all-done.1 = f32[8,8,256]{2,1,0:T(8,128)S(1)} async-done(((f32[8,8,256]{2,1,0:T(8,128)}), f32[8,8,256]{2,1,0:T(8,128)S(1)}, u32[]{:S(2)}, u32[]{:S(2)}) %all-to-all-start.1) | async-done | bytes 65568 | tf_op jit(solution)/shard_map/all_to_all | solution.py:673
  114.4 10.7 %all-to-all-start.2 = ((f32[64,8,256]{2,1,0:T(8,128)}), f32[64,8,256]{2,1,0:T(8,128)S(1)}, u32[]{:S(2)}, u32[]{:S(2)}) async-start(f32[64,8,256]{2,1,0:T(8,128)} %broadcast_in_dim.11), calls=%async_computation.2 | async-start | bytes 1048576 | tf_op jit(solution)/shard_map/all_to_all | solution.py:673
  125.1 1.3 collective-permute-start.9
  126.4 2.4 %collective-permute-start.10 = (f32[2,256,256]{2,1,0:T(8,128)S(1)}, f32[2,256,256]{2,1,0:T(8,128)S(1)}, u32[]{:S(2)}, u32[]{:S(2)}) collective-permute-start(f32[2,256,256]{2,1,0:T(8,128)S(1)} %add_add_fusion.own_any.object_grad_any), channel_id=1, source_target_pairs={{1,0},{2,1},{3,2},{4,3},{5,4},{6,5},{7,6},{8,7},{9,8},{10,9},{11,1... | collective-permute-start | bytes 1572872 | tf_op jit(solution)/shard_map/ppermute | solution.py:660
  128.8 16.2 %collective-permute-done.9.below_any = f32[2,256,256]{2,1,0:T(8,128)S(1)} collective-permute-done((f32[2,256,256]{2,1,0:T(8,128)S(1)}, f32[2,256,256]{2,1,0:T(8,128)S(1)}, u32[]{:S(2)}, u32[]{:S(2)}) %collective-permute-start.9) | collective-permute-done | bytes 524320 | tf_op jit(solution)/shard_map/ppermute | solution.py:660
  145.0 2.7 %collective-permute-start.11 = (f32[2,256,256]{2,1,0:T(8,128)S(1)}, f32[2,256,256]{2,1,0:T(8,128)S(1)}, u32[]{:S(2)}, u32[]{:S(2)}) collective-permute-start(f32[2,256,256]{2,1,0:T(8,128)S(1)} %collective-permute-done.9.below_any), channel_id=1, source_target_pairs={{1,0},{2,1},{3,2},{4,3},{5,4},{6,5},{7,6},{8,7},{9,8},{10,9},{11,1... | collective-permute-start | bytes 1572872 | tf_op jit(solution)/shard_map/ppermute | solution.py:660
  147.7 10.7 %previous_frames.1 = (f32[4,256,256]{2,1,0:T(8,128)}, f32[1,128]{1,0:T(1,128)}) custom-call(s32[1,1,4,2]{3,2,1,0:T(4,128)} %copy.24.positions_ref, s32[1,32]{1,0:T(1,128)} %counts_ref.5, f32[2,256,256]{2,1,0:T(8,128)} %object_prev_any.1, f32[2,256,256]{2,1,0:T(8,128)} %copy-done.5, f32[2,256,256]{2,1,0:T(8,128)} %collective-permute-done.8.right_any, ...), custom_call_target="tpu_custom_call" | custom-call | flops 5000000000 | bytes 10000000 | tf_op jit(solution)/shard_map/previous_frames/pallas_call | solution.py:593
  159.6 10.4 %curvature_frames.1 = (f32[1,128]{1,0:T(1,128)}, f32[2,256,256]{2,1,0:T(8,128)}) custom-call(s32[1,1,4,2]{3,2,1,0:T(4,128)} %copy.24.positions_ref, s32[1,32]{1,0:T(1,128)} %counts_ref.5, f32[2,256,256]{2,1,0:T(8,128)} %copy-done, f32[2,256,256]{2,1,0:T(8,128)} %copy-done.7, f32[2,256,256]{2,1,0:T(8,128)} %copy-done.9, f32[2,256,256]{2,1,0:T(8,128)} %copy-done.11, ...), custom_call_target="tpu_custom_call" | custom-call | flops 5000000000 | bytes 10000000 | tf_op jit(solution)/shard_map/curvature_frames/pallas_call | solution.py:619
  170.7 11.7 %all_to_all.25 = f32[32,1,128]{2,1,0:T(1,128)S(1)} all-to-all(f32[32,1,128]{2,1,0:T(1,128)S(1)} %broadcast_in_dim.13), channel_id=1, replica_groups={{0,1,32,33,64,65,96,97,128,129,160,161,192,193,224,225,256,257,288,289,..., dimensions={0} | all-to-all | bytes 32768 | tf_op jit(solution)/shard_map/all_to_all | solution.py:673
  183.1 5.4 %all-to-all-start.4 = ((f32[16,1,128]{2,1,0:T(1,128)}), f32[16,1,128]{2,1,0:T(1,128)S(1)}, u32[]{:S(2)}, u32[]{:S(2)}) async-start(f32[16,1,128]{2,1,0:T(1,128)} %broadcast_in_dim.14), calls=%async_computation.4 | async-start | bytes 16384 | tf_op jit(solution)/shard_map/all_to_all | solution.py:673
  189.1 10.6 %all-to-all-done.4.gathered_ref = f32[16,1,128]{2,1,0:T(1,128)S(1)} async-done(((f32[16,1,128]{2,1,0:T(1,128)}), f32[16,1,128]{2,1,0:T(1,128)S(1)}, u32[]{:S(2)}, u32[]{:S(2)}) %all-to-all-start.4) | async-done | bytes 8224 | tf_op jit(solution)/shard_map/all_to_all | solution.py:673
  200.2 4.3 %update.1 = (f32[2,256,256]{2,1,0:T(8,128)}, f32[2,256,256]{2,1,0:T(8,128)}, f32[2,256,256]{2,1,0:T(8,128)}, f32[2,256,256]{2,1,0:T(8,128)}, f32[1,128]{1,0:T(1,128)}) custom-call(f32[1]{0:T(128)} %bitcast.7.prev_norm_ref, f32[16,1,128]{2,1,0:T(1,128)} %copy-done.4, f32[1,128]{1,0:T(1,128)} %get-tuple-element.67.sums_ref, f32[2,256,256]{2,1,0:T(8,128)} %object_any.1, ...), custom_call_target="tpu_custom_call" | custom-call | flops 1000000 | bytes 10000000 | tf_op jit(solution)/shard_map/update/pallas_call | solution.py:646
  204.6 1.2 slice.6
  205.8 1.1 slice_bitcast_fusion
  (43 shorter events, 7.4 us)
Async XLA Ops:
  0.6 10.8 %collective-permute-start = (f32[2,256,256]{2,1,0:T(8,128)}, f32[2,256,256]{2,1,0:T(8,128)S(1)}, u32[]{:S(2)}, u32[]{:S(2)}) collective-permute-start(f32[2,256,256]{2,1,0:T(8,128)} %object_any.1), channel_id=1, source_target_pairs={{32,0},{64,32},{96,64},{128,96},{160,128},{192,160},{224,192},{256... | collective-permute-start | bytes 1572872 | tf_op jit(solution)/shard_map/ppermute | solution.py:660
  1.9 12.3 %collective-permute-start.1 = (f32[2,256,256]{2,1,0:T(8,128)}, f32[2,256,256]{2,1,0:T(8,128)S(1)}, u32[]{:S(2)}, u32[]{:S(2)}) collective-permute-start(f32[2,256,256]{2,1,0:T(8,128)} %object_any.1), channel_id=1, source_target_pairs={{1,0},{2,1},{3,2},{4,3},{5,4},{6,5},{7,6},{8,7},{9,8},{10,9},{11,1... | collective-permute-start | bytes 1572872 | tf_op jit(solution)/shard_map/ppermute | solution.py:660
  11.4 27.3 %copy-start.8 = (f32[2,256,256]{2,1,0:T(8,128)}, f32[2,256,256]{2,1,0:T(8,128)S(1)}, u32[]{:S(2)}) copy-start(f32[2,256,256]{2,1,0:T(8,128)S(1)} %collective-permute-done.below_any) | copy-start | bytes 1572868
  14.2 24.5 %copy-start.10 = (f32[2,256,256]{2,1,0:T(8,128)}, f32[2,256,256]{2,1,0:T(8,128)S(1)}, u32[]{:S(2)}) copy-start(f32[2,256,256]{2,1,0:T(8,128)S(1)} %collective-permute-done.1.right_any) | copy-start | bytes 1572868
  14.2 14.3 %collective-permute-start.2 = (f32[2,256,256]{2,1,0:T(8,128)S(1)}, f32[2,256,256]{2,1,0:T(8,128)S(1)}, u32[]{:S(2)}, u32[]{:S(2)}) collective-permute-start(f32[2,256,256]{2,1,0:T(8,128)S(1)} %collective-permute-done.below_any), channel_id=1, source_target_pairs={{1,0},{2,1},{3,2},{4,3},{5,4},{6,5},{7,6},{8,7},{9,8},{10,9},{11,1... | collective-permute-start | bytes 1572872 | tf_op jit(solution)/shard_map/ppermute | solution.py:660
  20.7 15.7 %collective-permute-start.3 = (f32[2,256,256]{2,1,0:T(8,128)}, f32[2,256,256]{2,1,0:T(8,128)S(1)}, u32[]{:S(2)}, u32[]{:S(2)}) collective-permute-start(f32[2,256,256]{2,1,0:T(8,128)} %object_prev_any.1), channel_id=1, source_target_pairs={{32,0},{64,32},{96,64},{128,96},{160,128},{192,160},{224,192},{256... | collective-permute-start | bytes 1572872 | tf_op jit(solution)/shard_map/ppermute | solution.py:660
  28.5 10.3 %copy-start.12 = (f32[2,256,256]{2,1,0:T(8,128)}, f32[2,256,256]{2,1,0:T(8,128)S(1)}, u32[]{:S(2)}) copy-start(f32[2,256,256]{2,1,0:T(8,128)S(1)} %collective-permute-done.2.diag_any) | copy-start | bytes 1572868
  36.5 17.9 %copy-start.5 = (f32[2,256,256]{2,1,0:T(8,128)}, f32[2,256,256]{2,1,0:T(8,128)S(1)}, u32[]{:S(2)}) copy-start(f32[2,256,256]{2,1,0:T(8,128)S(1)} %collective-permute-done.3.below_any) | copy-start | bytes 1572868
  36.5 17.9 %collective-permute-start.4 = (f32[2,256,256]{2,1,0:T(8,128)S(1)}, f32[2,256,256]{2,1,0:T(8,128)S(1)}, u32[]{:S(2)}, u32[]{:S(2)}) collective-permute-start(f32[2,256,256]{2,1,0:T(8,128)S(1)} %collective-permute-done.3.below_any), channel_id=1, source_target_pairs={{1,0},{2,1},{3,2},{4,3},{5,4},{6,5},{7,6},{8,7},{9,8},{10,9},{11,1... | collective-permute-start | bytes 1572872 | tf_op jit(solution)/shard_map/ppermute | solution.py:660
  54.3 30.0 %copy-start.2 = (f32[2,256,256]{2,1,0:T(8,128)S(1)}, f32[2,256,256]{2,1,0:T(8,128)}, u32[]{:S(2)}) copy-start(f32[2,256,256]{2,1,0:T(8,128)} %object_prev_any.1) | copy-start | bytes 1572868
  54.3 59.0 %copy-start.3 = (f32[2,256,256]{2,1,0:T(8,128)S(1)}, f32[2,256,256]{2,1,0:T(8,128)}, u32[]{:S(2)}) copy-start(f32[2,256,256]{2,1,0:T(8,128)} %get-tuple-element.54) | copy-start | bytes 1572868
  54.4 0.8 copy-start.6
  55.2 25.1 %all-to-all-start = ((f32[64,8,256]{2,1,0:T(8,128)}), f32[64,8,256]{2,1,0:T(8,128)S(1)}, u32[]{:S(2)}, u32[]{:S(2)}) async-start(f32[64,8,256]{2,1,0:T(8,128)} %bitcast.8), calls=%async_computation | async-start | bytes 1048576 | tf_op jit(solution)/shard_map/all_to_all | solution.py:673
  67.5 11.7 %collective-permute-start.5 = (f32[2,256,256]{2,1,0:T(8,128)}, f32[2,256,256]{2,1,0:T(8,128)S(1)}, u32[]{:S(2)}, u32[]{:S(2)}) collective-permute-start(f32[2,256,256]{2,1,0:T(8,128)} %get-tuple-element.46), channel_id=1, source_target_pairs={{0,1},{1,2},{2,3},{3,4},{4,5},{5,6},{6,7},{7,8},{8,9},{9,10},{10,1... | collective-permute-start | bytes 1572872 | tf_op jit(solution)/shard_map/ppermute | solution.py:660
  71.0 30.3 %collective-permute-start.7 = (f32[2,256,256]{2,1,0:T(8,128)}, f32[2,256,256]{2,1,0:T(8,128)S(1)}, u32[]{:S(2)}, u32[]{:S(2)}) collective-permute-start(f32[2,256,256]{2,1,0:T(8,128)} %get-tuple-element.52), channel_id=1, source_target_pairs={{0,1},{1,2},{2,3},{3,4},{4,5},{5,6},{6,7},{7,8},{8,9},{9,10},{10,1... | collective-permute-start | bytes 1572872 | tf_op jit(solution)/shard_map/ppermute | solution.py:660
  82.1 31.2 %collective-permute-start.6 = (f32[2,256,256]{2,1,0:T(8,128)S(1)}, f32[2,256,256]{2,1,0:T(8,128)S(1)}, u32[]{:S(2)}, u32[]{:S(2)}) collective-permute-start(f32[2,256,256]{2,1,0:T(8,128)S(1)} %add.9), channel_id=1, source_target_pairs={{0,32},{32,64},{64,96},{96,128},{128,160},{160,192},{192,224},{224... | collective-permute-start | bytes 1572872 | tf_op jit(solution)/shard_map/ppermute | solution.py:660
  84.3 29.1 %collective-permute-start.8 = (f32[2,256,256]{2,1,0:T(8,128)S(1)}, f32[2,256,256]{2,1,0:T(8,128)}, u32[]{:S(2)}, u32[]{:S(2)}) collective-permute-start(f32[2,256,256]{2,1,0:T(8,128)S(1)} %copy-done.2), channel_id=1, source_target_pairs={{1,0},{2,1},{3,2},{4,3},{5,4},{6,5},{7,6},{8,7},{9,8},{10,9},{11,1... | collective-permute-start | bytes 1572872 | tf_op jit(solution)/shard_map/ppermute | solution.py:660
  87.0 26.3 %all-to-all-start.1 = ((f32[8,8,256]{2,1,0:T(8,128)}), f32[8,8,256]{2,1,0:T(8,128)S(1)}, u32[]{:S(2)}, u32[]{:S(2)}) async-start(f32[8,8,256]{2,1,0:T(8,128)} %broadcast_in_dim.10), calls=%async_computation.1 | async-start | bytes 131072 | tf_op jit(solution)/shard_map/all_to_all | solution.py:673
  113.4 45.0 %copy-start = (f32[2,256,256]{2,1,0:T(8,128)}, f32[2,256,256]{2,1,0:T(8,128)S(1)}, u32[]{:S(2)}) copy-start(f32[2,256,256]{2,1,0:T(8,128)S(1)} %add_add_fusion.own_any.object_grad_any) | copy-start | bytes 1572868
  114.4 44.1 %all-to-all-start.2 = ((f32[64,8,256]{2,1,0:T(8,128)}), f32[64,8,256]{2,1,0:T(8,128)S(1)}, u32[]{:S(2)}, u32[]{:S(2)}) async-start(f32[64,8,256]{2,1,0:T(8,128)} %broadcast_in_dim.11), calls=%async_computation.2 | async-start | bytes 1048576 | tf_op jit(solution)/shard_map/all_to_all | solution.py:673
  125.1 19.9 %collective-permute-start.9 = (f32[2,256,256]{2,1,0:T(8,128)S(1)}, f32[2,256,256]{2,1,0:T(8,128)S(1)}, u32[]{:S(2)}, u32[]{:S(2)}) collective-permute-start(f32[2,256,256]{2,1,0:T(8,128)S(1)} %add_add_fusion.own_any.object_grad_any), channel_id=1, source_target_pairs={{32,0},{64,32},{96,64},{128,96},{160,128},{192,160},{224,192},{256... | collective-permute-start | bytes 1572872 | tf_op jit(solution)/shard_map/ppermute | solution.py:660
  126.4 32.0 %collective-permute-start.10 = (f32[2,256,256]{2,1,0:T(8,128)S(1)}, f32[2,256,256]{2,1,0:T(8,128)S(1)}, u32[]{:S(2)}, u32[]{:S(2)}) collective-permute-start(f32[2,256,256]{2,1,0:T(8,128)S(1)} %add_add_fusion.own_any.object_grad_any), channel_id=1, source_target_pairs={{1,0},{2,1},{3,2},{4,3},{5,4},{6,5},{7,6},{8,7},{9,8},{10,9},{11,1... | collective-permute-start | bytes 1572872 | tf_op jit(solution)/shard_map/ppermute | solution.py:660
  145.0 13.4 %copy-start.7 = (f32[2,256,256]{2,1,0:T(8,128)}, f32[2,256,256]{2,1,0:T(8,128)S(1)}, u32[]{:S(2)}) copy-start(f32[2,256,256]{2,1,0:T(8,128)S(1)} %collective-permute-done.9.below_any) | copy-start | bytes 1572868
  145.0 13.4 %collective-permute-start.11 = (f32[2,256,256]{2,1,0:T(8,128)S(1)}, f32[2,256,256]{2,1,0:T(8,128)S(1)}, u32[]{:S(2)}, u32[]{:S(2)}) collective-permute-start(f32[2,256,256]{2,1,0:T(8,128)S(1)} %collective-permute-done.9.below_any), channel_id=1, source_target_pairs={{1,0},{2,1},{3,2},{4,3},{5,4},{6,5},{7,6},{8,7},{9,8},{10,9},{11,1... | collective-permute-start | bytes 1572872 | tf_op jit(solution)/shard_map/ppermute | solution.py:660
  158.5 0.8 copy-start.9
  158.5 0.9 copy-start.11
  158.5 1.1 copy-start.1
  183.1 16.6 %all-to-all-start.4 = ((f32[16,1,128]{2,1,0:T(1,128)}), f32[16,1,128]{2,1,0:T(1,128)S(1)}, u32[]{:S(2)}, u32[]{:S(2)}) async-start(f32[16,1,128]{2,1,0:T(1,128)} %broadcast_in_dim.14), calls=%async_computation.4 | async-start | bytes 16384 | tf_op jit(solution)/shard_map/all_to_all | solution.py:673
  199.7 0.6 copy-start.4

commit v3 on v2

--- a/solution.py
+++ b/solution.py
@@ -143,6 +143,7 @@
     left_ref,
     right_ref,
     grads_ref,
+    probe_sum_ref,
     patch_ref,
     moved_ref,
     far_ref,
@@ -214,7 +215,10 @@
             )
         for part in range(2):
             total = pieces[0][part] + pieces[1][part]
-            grads_ref[4, part] = total if first == 0 else grads_ref[4, part] + total
+            for half in range(2):
+                rows = pl.ds((2 * part + half) * width, width)
+                side = total[:, half * (width // 2) : (half + 1) * (width // 2)]
+                probe_sum_ref[rows, :] = side if first == 0 else probe_sum_ref[rows, :] + side
         for part in range(2):
             sums = [0.0, 0.0, 0.0, 0.0]
             for slot, (row, col), (back_i, back_r) in zip(slots, spots, backs):
@@ -238,7 +242,8 @@
     both(0)
     pl.when(live > 2)(lambda: both(2))
     outs = [own_grad_any, below_grad_any, right_grad_any, diag_grad_any, probe_grad_any]
-    for copy in outgoing([grads_ref.at[at] for at in range(5)], outs, out_sems):
+    made = [grads_ref.at[at] for at in range(4)] + [probe_sum_ref]
+    for copy in outgoing(made, outs, out_sems):
         copy.wait()
 
 
@@ -286,94 +291,62 @@
     return [(array.at[pl.ds(first, 2)], ref.at[pl.ds(first, 2)]) for first in (0, 2)]
 
 
-def previous_kernel(
+def fold_kernel(
+    own_any,
+    left_any,
+    above_any,
+    prev_any,
+    pieces_any,
+    grad_any,
+    payload_ref,
+    held_ref,
+    pieces_ref,
+    grad_ref,
+    in_sems,
+    out_sem,
+):
+    sources = [own_any, left_any, above_any, prev_any, pieces_any]
+    targets = [held_ref.at[at] for at in range(4)] + [pieces_ref]
+    own, left, above, prev, pieces = incoming(sources, targets, in_sems)
+    grad_ref[...] = own()[...] + left()[...] + above()[...]
+    copy = pltpu.make_async_copy(grad_ref, grad_any, out_sem)
+    copy.start()
+    square = jnp.sum(grad_ref[...] * grad_ref[...])
+    along = jnp.sum(grad_ref[...] * prev()[...])
+    piece = jnp.sum(pieces()[...], axis=0)
+    depth = piece.shape[0]
+    lanes = lax.broadcasted_iota(jnp.int32, (1, payload_ref.shape[2]), 1)
+    extra = jnp.where(lanes == 0, square, jnp.where(lanes == 1, along, 0.0))
+    for at in range(payload_ref.shape[0]):
+        payload_ref[at, :depth] = piece
+        payload_ref[at, depth:] = extra
+    copy.wait()
+
+
+def curvature_kernel(
     positions_ref,
     counts_ref,
+    prev_norm_ref,
     own_any,
     below_any,
     right_any,
     diag_any,
-    change_any,
-    patch_any,
-    moved_any,
-    far_any,
-    left_any,
-    right_table_any,
-    quad_any,
-    sums_ref,
-    tiles_ref,
-    change_ref,
-    patch_ref,
-    moved_ref,
-    far_ref,
-    left_ref,
-    right_ref,
-    quad_ref,
-    tall_ref,
-    wide_ref,
-    in_sems,
-    out_sem,
-):
-    live = live_count(counts_ref)
-    kept = [
-        halves(patch_any, patch_ref),
-        halves(moved_any, moved_ref),
-        halves(far_any, far_ref),
-    ]
-    moves = [(change_any, change_ref)]
-    moves += [
-        (tile, tiles_ref.at[at]) for at, tile in enumerate((own_any, below_any, right_any, diag_any))
-    ]
-    moves += [kept[0][0], kept[1][0], (left_any, left_ref), (right_table_any, right_ref), kept[2][0]]
-    moves += [kept[0][1], kept[1][1], kept[2][1]]
-    change, *arrivals = incoming(*zip(*moves), in_sems)
-    tiles, (patch, moved, left, right, far), later = arrivals[:4], arrivals[4:9], arrivals[9:]
-    lane = lax.broadcasted_iota(jnp.int32, (1, 128), 1)
-    sums_ref[...] = jnp.zeros_like(sums_ref)
-
-    def finish(slots, quads):
-        row = sums_ref[...]
-        for slot, quad in zip(slots, quads):
-            quad_ref[slot] = quad
-            square = jnp.sum(quad * quad)
-            row = row + jnp.where((lane == 2) | (lane == 16 + slot), square, 0.0)
-        sums_ref[...] = row
-
-    linear_frames(
-        positions_ref,
-        live,
-        tiles,
-        change,
-        ((patch, moved, far), later),
-        (left, right),
-        (tall_ref, wide_ref),
-        finish,
-    )
-    copy = pltpu.make_async_copy(quad_ref, quad_any, out_sem)
-    copy.start()
-    copy.wait()
-
-
-def curvature_kernel(
-    positions_ref,
-    counts_ref,
-    own_any,
-    below_any,
-    right_any,
-    diag_any,
+    prev_own_any,
+    prev_below_any,
+    prev_right_any,
+    prev_diag_any,
     total_any,
     patch_any,
     moved_any,
     far_any,
     left_any,
     right_table_any,
-    prev_any,
-    quad_any,
-    prev_sums_ref,
     prev_probe_any,
+    direction_any,
+    probe_direction_any,
     sums_ref,
-    change_any,
     tiles_ref,
+    prev_tiles_ref,
     total_ref,
     change_ref,
     patch_ref,
@@ -381,98 +354,103 @@
     far_ref,
     left_ref,
     right_ref,
-    quad_ref,
-    prev_ref,
     prev_probe_ref,
     tall_ref,
     wide_ref,
     in_sems,
-    out_sem,
+    out_sems,
     *,
     probe_scale,
+    pieces,
 ):
     live = live_count(counts_ref)
+    width = change_ref.shape[-1]
     kept = [
         halves(patch_any, patch_ref),
         halves(moved_any, moved_ref),
         halves(far_any, far_ref),
     ]
-    moves = [(total_any, total_ref)]
-    moves += [
-        (tile, tiles_ref.at[at]) for at, tile in enumerate((own_any, below_any, right_any, diag_any))
-    ]
+    moves = [(total_any, total_ref), (prev_probe_any, prev_probe_ref)]
+    for group, target in (
+        ((own_any, below_any, right_any, diag_any), tiles_ref),
+        ((prev_own_any, prev_below_any, prev_right_any, prev_diag_any), prev_tiles_ref),
+    ):
+        moves += [(tile, target.at[at]) for at, tile in enumerate(group)]
     moves += [kept[0][0], kept[1][0], (left_any, left_ref), (right_table_any, right_ref), kept[2][0]]
     moves += [kept[0][1], kept[1][1], kept[2][1]]
-    moves += [(quad_any, quad_ref), (prev_any, prev_ref), (prev_probe_any, prev_probe_ref)]
-    total, *arrivals = incoming(*zip(*moves), in_sems)
-    tiles, (patch, moved, left, right, far), later = arrivals[:4], arrivals[4:9], arrivals[9:12]
-    quad_in, prev, prev_probe = arrivals[12:]
-    change_ref[...] = total()[...].reshape(change_ref.shape) * probe_scale
-    copy = pltpu.make_async_copy(change_ref, change_any, out_sem)
-    copy.start()
+    total, prev_probe, *arrivals = incoming(*zip(*moves), in_sems)
+    tiles, prev_tiles = arrivals[:4], arrivals[4:8]
+    (patch, moved, left, right, far), later = arrivals[8:13], arrivals[13:]
+
+    total()
+    depth = 4 * width // pieces
+    products = jnp.zeros((1, total_ref.shape[-1]), jnp.float32)
+    for piece in range(pieces):
+        base = piece * (depth + 1)
+        part, rest = divmod(piece * depth, 2 * width)
+        half, first = divmod(rest, width)
+        lanes = slice(half * (width // 2), (half + 1) * (width // 2))
+        change_ref[part, first : first + depth, lanes] = (
+            total_ref[base : base + depth, :] * probe_scale
+        )
+        products = products + total_ref[base + depth : base + depth + 1, :]
     lane = lax.broadcasted_iota(jnp.int32, (1, 128), 1)
-    sums_ref[...] = prev_sums_ref[...]
+    probe_grad = change_ref[...]
+    prev_probe()
+    grad_norm = jnp.sum(jnp.where(lane == 0, products, 0.0)) + jnp.sum(probe_grad * probe_grad)
+    along_prev = jnp.sum(jnp.where(lane == 1, products, 0.0))
+    along_prev = along_prev + jnp.sum(probe_grad * prev_probe_ref[...])
+    ratio = grad_norm / prev_norm_ref[0]
+    descent = grad_norm - ratio * along_prev
+    change_ref[...] = ratio * prev_probe_ref[...] - change_ref[...]
+    for at, (tile, prev) in enumerate(zip(tiles, prev_tiles)):
+        tile()
+        prev()
+        tiles_ref[at] = ratio * prev_tiles_ref[at] - tiles_ref[at]
+    sent = outgoing(
+        [tiles_ref.at[0], change_ref], [direction_any, probe_direction_any], out_sems
+    )
+    row = jnp.where(lane == 5, grad_norm, jnp.where(lane == 6, descent, 0.0))
+    sums_ref[...] = row
 
     def finish(slots, quads):
-        quad_in()
         row = sums_ref[...]
         for slot, quad in zip(slots, quads):
             square = jnp.sum(quad * quad)
-            cross = jnp.sum(quad * quad_ref[slot])
-            row = row + jnp.where((lane == 0) | (lane == 8 + slot), square, 0.0)
-            row = row + jnp.where((lane == 1) | (lane == 12 + slot), cross, 0.0)
+            row = row + jnp.where((lane == 0) | (lane == 1 + slot), square, 0.0)
         sums_ref[...] = row
 
     linear_frames(
         positions_ref,
         live,
-        tiles,
+        [(lambda at=at: tiles_ref.at[at]) for at in range(4)],
         lambda: change_ref,
         ((patch, moved, far), later),
         (left, right),
         (tall_ref, wide_ref),
         finish,
     )
-    prev()
-    prev_probe()
-    own = tiles_ref[0]
-    probe_grad = change_ref[...]
-    values = [
-        (3, jnp.sum(own * own)),
-        (4, jnp.sum(own * prev_ref[...])),
-        (20, jnp.sum(probe_grad * probe_grad)),
-        (21, jnp.sum(probe_grad * prev_probe_ref[...])),
-    ]
-    row = sums_ref[...]
-    for at, value in values:
-        row = jnp.where(lane == at, value, row)
-    sums_ref[...] = row
-    copy.wait()
+    for copy in sent:
+        copy.wait()
 
 
 def update_kernel(
-    prev_norm_ref,
     gathered_ref,
     sums_ref,
     object_any,
-    object_grad_any,
-    object_prev_any,
+    direction_any,
     probe_any,
-    probe_grad_any,
-    probe_prev_any,
+    probe_direction_any,
     object_new_any,
     probe_new_any,
-    object_direction_any,
-    probe_direction_any,
-    row_ref,
+    norm_ref,
+    frames_ref,
     held_ref,
-    made_ref,
     in_sems,
     out_sems,
 ):
-    sources = [object_prev_any, object_grad_any, object_any]
-    sources += [probe_prev_any, probe_grad_any, probe_any]
-    arrivals = incoming(sources, [held_ref.at[at] for at in range(6)], in_sems)
+    sources = [object_any, direction_any, probe_any, probe_direction_any]
+    arrivals = incoming(sources, [held_ref.at[at] for at in range(4)], in_sems)
     total = jnp.sum(gathered_ref[...], axis=0)
     local = sums_ref[...]
     lane = lax.broadcasted_iota(jnp.int32, (1, 128), 1)
@@ -480,32 +458,18 @@
     def pick(row, at):
         return jnp.sum(jnp.where(lane == at, row, 0.0))
 
-    grad_norm = pick(total, 3) + pick(local, 20)
-    along_prev = pick(total, 4) + pick(local, 21)
-    ratio = grad_norm / prev_norm_ref[0]
-    descent = grad_norm - ratio * along_prev
-    curvature = pick(total, 0) - 2.0 * ratio * pick(total, 1) + ratio * ratio * pick(total, 2)
-    step_size = descent / (0.5 * curvature + 1e-06)
-    outs = [object_direction_any, object_new_any, probe_direction_any, probe_new_any]
+    curvature = pick(total, 0)
+    step_size = pick(local, 6) / (0.5 * curvature + 1e-06)
+    outs = [object_new_any, probe_new_any]
     sent = []
-    for first in (0, 3):
-        at = 2 * (first // 3)
-        prev, grad, field = [arrival()[...] for arrival in arrivals[first : first + 3]]
-        direction = ratio * prev - grad
-        made_ref[at] = direction
-        made_ref[at + 1] = field + step_size * direction
-        span = range(at, at + 2)
-        sent += outgoing([made_ref.at[i] for i in span], [outs[i] for i in span], out_sems, at)
+    for which in range(2):
+        field, direction = [arrival() for arrival in arrivals[2 * which : 2 * which + 2]]
+        field[...] = field[...] + step_size * direction[...]
+        sent += outgoing([field], [outs[which]], out_sems, which)
+    norm_ref[0, 0] = pick(local, 5)
     pixels = held_ref.shape[-1] * held_ref.shape[-2]
-    row = jnp.where(lane == 4, grad_norm, 0.0)
-    for slot in range(4):
-        frame_sum = (
-            pick(local, 8 + slot)
-            - 2.0 * ratio * pick(local, 12 + slot)
-            + ratio * ratio * pick(local, 16 + slot)
-        )
-        row = jnp.where(lane == slot, frame_sum / pixels, row)
-    row_ref[...] = row
+    for slot in range(frames_ref.shape[-1]):
+        frames_ref[0, 0, slot] = pick(local, 1 + slot) / pixels
     for copy in sent:
         copy.wait()
 
@@ -565,7 +529,9 @@
     frames = buffer(slots, 2, width, width)
     return pl.pallas_call(
         gradient_kernel,
-        out_shape=(shaped(2, width, width),) * 5 + (shaped(slots, 2, width, width),) * 3,
+        out_shape=(shaped(2, width, width),) * 4
+        + (shaped(4 * width, width // 2),)
+        + (shaped(slots, 2, width, width),) * 3,
         in_specs=in_smem(2) + anywhere(4) + in_hbm(4),
         out_specs=(*anywhere(5), *in_hbm(3)),
         scratch_shapes=[
@@ -573,7 +539,8 @@
             buffer(2, width, width),
             buffer(slots, width, width, dtype=measured.dtype),
             *table_buffers(width),
-            buffer(5, 2, width, width),
+            buffer(4, 2, width, width),
+            buffer(4 * width, width // 2),
             frames,
             frames,
             frames,
@@ -586,42 +553,37 @@
     )(positions, counts, *tiles, probe, measured, *tables)
 
 
-def previous_call(positions, counts, tiles, probe_prev, kept, tables):
-    width = probe_prev.shape[-1]
-    slots = kept[0].shape[0]
-    frames = buffer(slots, 2, width, width)
+def fold_call(parts, prev, pieces, targets):
+    shape = prev.shape
+    depth = pieces.shape[1]
     return pl.pallas_call(
-        previous_kernel,
-        out_shape=(shaped(slots, width, width), shaped(1, 128)),
-        in_specs=in_smem(2) + anywhere(4) + in_hbm(6),
-        out_specs=(*in_hbm(1), *in_vmem(1)),
+        fold_kernel,
+        out_shape=(shaped(*shape), shaped(targets, depth + 1, pieces.shape[2])),
+        in_specs=anywhere(5),
+        out_specs=(*anywhere(1), *in_vmem(1)),
         scratch_shapes=[
-            buffer(4, 2, width, width),
-            buffer(2, width, width),
-            frames,
-            frames,
-            frames,
-            *table_buffers(width),
-            buffer(slots, width, width),
-            *dft_scratch(width),
-            arrivals_of(13),
+            buffer(4, *shape),
+            buffer(*pieces.shape),
+            buffer(*shape),
+            arrivals_of(5),
             pltpu.SemaphoreType.DMA,
         ],
-        name="previous_frames",
-        **costing(5 * 10**9),
-    )(positions, counts, *tiles, probe_prev, *kept, *tables)
-
-
-def curvature_call(positions, counts, tiles, total, kept, tables, previous, probe_scale):
+        name="fold",
+        **costing(10**6),
+    )(*parts, prev, pieces)
+
+
+def curvature_call(positions, counts, prev_norm, tiles, total, pieces, kept, tables, probe_prev, scale):
     width = tiles[0].shape[-1]
     slots = kept[0].shape[0]
     frames = buffer(slots, 2, width, width)
     return pl.pallas_call(
-        functools.partial(curvature_kernel, probe_scale=probe_scale),
-        out_shape=(shaped(1, 128), shaped(2, width, width)),
-        in_specs=in_smem(2) + anywhere(5) + in_hbm(7) + in_vmem(1) + in_hbm(1),
-        out_specs=(*in_vmem(1), *in_hbm(1)),
+        functools.partial(curvature_kernel, probe_scale=scale, pieces=pieces),
+        out_shape=(shaped(2, width, width), shaped(2, width, width), shaped(1, 128)),
+        in_specs=in_smem(3) + anywhere(9) + in_hbm(6),
+        out_specs=(*in_hbm(2), *in_vmem(1)),
         scratch_shapes=[
+            buffer(4, 2, width, width),
             buffer(4, 2, width, width),
             buffer(*total.shape),
             buffer(2, width, width),
@@ -629,29 +591,27 @@
             frames,
             frames,
             *table_buffers(width),
-            buffer(slots, width, width),
-            buffer(2, width, width),
             buffer(2, width, width),
             *dft_scratch(width),
-            arrivals_of(16),
-            pltpu.SemaphoreType.DMA,
+            arrivals_of(18),
+            arrivals_of(2),
         ],
         name="curvature_frames",
         **costing(5 * 10**9),
-    )(positions, counts, *tiles, total, *kept, *tables, *previous)
-
-
-def update_call(prev_norm, gathered, sums, arrays):
+    )(positions, counts, prev_norm, *tiles, total, *kept, *tables, probe_prev)
+
+
+def update_call(gathered, sums, arrays, slots):
     shape = arrays[0].shape
     return pl.pallas_call(
         update_kernel,
-        out_shape=(shaped(*shape),) * 4 + (shaped(1, 128),),
-        in_specs=in_smem(1) + in_vmem(2) + in_hbm(6),
-        out_specs=(*in_hbm(4), *in_vmem(1)),
-        scratch_shapes=[buffer(6, *shape), buffer(4, *shape), arrivals_of(6), arrivals_of(4)],
+        out_shape=(shaped(*shape),) * 2 + (shaped(1, 1), shaped(1, 1, slots)),
+        in_specs=in_vmem(2) + in_hbm(4),
+        out_specs=(*in_hbm(2), *in_smem(2)),
+        scratch_shapes=[buffer(4, *shape), arrivals_of(4), arrivals_of(2)],
         name="update",
         **costing(10**6),
-    )(prev_norm, gathered, sums, *arrays)
+    )(gathered, sums, *arrays)
 
 
 def passed_along(shard, axis, by):
@@ -701,61 +661,63 @@
     below = passed_along(object_field, "row", -1)
     diag = passed_along(held(below, right), "col", -1)
     prev_below = passed_along(held(object_dir_prev, below), "row", -1)
-    prev_diag = passed_along(held(prev_below, diag), "col", -1)
+    prev_right = passed_along(held(object_dir_prev, below), "col", -1)
 
     own_grad, below_grad, right_grad, diag_grad, probe_part, *kept = gradient_call(
         positions,
         counts,
-        (object_field, below, right, held(diag, prev_below)),
+        (object_field, below, right, diag),
         probe_field,
         intensities,
         tables,
     )
-    probe_part = held(probe_part, prev_diag)
+    probe_part, prev_below, prev_right = lax.optimization_barrier(
+        (probe_part, prev_below, prev_right)
+    )
     from_left_diag = passed_along(diag_grad, "col", 1)
-    prev_right = passed_along(held(object_dir_prev, diag_grad), "col", -1)
-    pieces = exchanged(probe_part.reshape((len(near[0]), -1, width)), near)
-    pieces, from_left_diag = lax.optimization_barrier((pieces, from_left_diag))
-    piece = copies(jnp.sum(pieces, axis=0), apart)
-    piece, below_sum = lax.optimization_barrier((piece, below_grad + from_left_diag))
-    from_above = passed_along(below_sum, "row", 1)
+    pieces = exchanged(probe_part.reshape((len(near[0]), -1, width // 2)), near)
+    from_above = passed_along(below_grad + from_left_diag, "row", 1)
     from_left = passed_along(right_grad, "col", 1)
-    pieces = exchanged(piece, apart)
-    pieces, from_above, from_left = lax.optimization_barrier((pieces, from_above, from_left))
-    piece = copies(jnp.sum(pieces, axis=0), near)
-    object_grad = own_grad + from_left + from_above
-    piece, object_grad, prev_right = lax.optimization_barrier((piece, object_grad, prev_right))
+    prev_diag = passed_along(held(prev_below, diag_grad), "col", -1)
+    from_above = held(from_above, prev_diag)
+    object_grad, payload = fold_call(
+        (own_grad, from_left, from_above), object_dir_prev, pieces, len(apart[0])
+    )
     grad_below = passed_along(object_grad, "row", -1)
     grad_right = passed_along(object_grad, "col", -1)
+    payload, grad_below, grad_right = lax.optimization_barrier(
+        (exchanged(payload, apart), grad_below, grad_right)
+    )
+    payload = jnp.sum(payload, axis=0)[:, None, :]
     grad_diag = passed_along(grad_below, "col", -1)
-    total = exchanged(piece, near)
-    prev_tiles = (object_dir_prev, prev_below, prev_right, prev_diag)
-    previous = previous_call(positions, counts, prev_tiles, probe_dir_prev, kept, tables)
-    total = held(total, grad_right, grad_diag, *previous)
-    sums, probe_grad = curvature_call(
+    total = exchanged(copies(payload, near), near)
+    total = held(total, grad_diag)
+    object_direction, probe_direction, sums = curvature_call(
         positions,
         counts,
-        (object_grad, grad_below, grad_right, grad_diag),
-        total,
+        prev_norm.reshape(1),
+        (object_grad, grad_below, grad_right, grad_diag)
+        + (object_dir_prev, prev_below, prev_right, prev_diag),
+        total.reshape(-1, width // 2),
+        len(near[0]),
         kept,
         tables,
-        (object_dir_prev, *previous, probe_dir_prev),
+        probe_dir_prev,
         probe_scale,
     )
     near, apart = device_groups(2)
     across = jnp.sum(exchanged(copies(sums, near), near), axis=0)
     across = exchanged(copies(across, apart), apart)
-    arrays = (object_field, object_grad, object_dir_prev, probe_field, probe_grad, probe_dir_prev)
-    object_new, probe_new, object_direction, probe_direction, row = update_call(
-        prev_norm.reshape(1), across, sums, arrays
+    object_new, probe_new, norm, frame_curvature = update_call(
+        across, sums, (object_field, object_direction, probe_field, probe_direction), slots
     )
     return (
         object_new,
         probe_new,
         object_direction,
         probe_direction,
-        row[0, slots],
-        row[0, :slots].reshape(1, 1, slots),
+        norm.reshape(()),
+        frame_curvature,
     )
 
 

time: 208 us -> 191 us (0.918)
  blocking collectives: 11.7 us -> 56.1 us
  starting transfers between devices: 79.7 us -> 50.1 us
  waiting for transfers between devices: 62.5 us -> 42 us
  Pallas kernels: 41 us -> 32.7 us
  local copies, waits for them, and re-layouts: 9.02 us -> 5.89 us
    all_to_all x1 -> x3, blocking collectives: 11.7 us -> 56.1 us  [exchanged(): lax.all_to_all(pieces, ('row', 'col'), 0, 0, axis_index_groups=groups)]
    all_to_all x4 -> x2, starting transfers between devices: 42.7 us -> 16.1 us  [exchanged(): lax.all_to_all(pieces, ('row', 'col'), 0, 0, axis_index_groups=groups)]
    all_to_all x4 -> x2, waiting for transfers between devices: 23.6 us -> 0.01 us  [exchanged(): lax.all_to_all(pieces, ('row', 'col'), 0, 0, axis_index_groups=groups)]
    pallas_call x4, Pallas kernels: 41 us -> 32.7 us  [the longest x1 15.5 us: gradient_call(): pl.pallas_call(gradient_kernel, out_shape=(shaped(2, width, width),) * 4...]
    ppermute x12, waiting for transfers between devices: 38.9 us -> 42 us  [passed_along(): return lax.ppermute(shard, axis, pairs)]
    ppermute x12, starting transfers between devices: 37 us -> 34 us  [passed_along(): return lax.ppermute(shard, axis, pairs)]
  transfers between devices with their start and end apart: 16 -> 14, of which waited for: 9 -> 7; matrix products, arithmetic and copies ran while one was open for 2% -> 1% of each run, Pallas kernels for 13% -> 8%
where the time goes in v3:
time: 191 us; the launch traced here: 190 us
  blocking collectives  56.1 us (29%)
  starting transfers between devices  50.1 us (26%)
  waiting for transfers between devices  42 us (22%)
  Pallas kernels  32.7 us (17%)
  local copies, waits for them, and re-layouts  5.89 us (3%)
    all_to_all x3, blocking collectives, exchanged(): lax.all_to_all(pieces, ('row', 'col'), 0, 0, axis_index_groups=groups)  56.1 us
    ppermute x12, waiting for transfers between devices, passed_along(): return lax.ppermute(shard, axis, pairs)  42 us
    ppermute x12, starting transfers between devices, passed_along(): return lax.ppermute(shard, axis, pairs)  34 us
    all_to_all x2, starting transfers between devices, exchanged(): lax.all_to_all(pieces, ('row', 'col'), 0, 0, axis_index_groups=groups)  16.1 us
    pallas_call x1, Pallas kernels, gradient_call(): pl.pallas_call(gradient_kernel, out_shape=(shaped(2, width, width),) * 4...  15.5 us
    pallas_call x1, Pallas kernels, curvature_call(): pl.pallas_call(functools.partial(curvature_kernel, probe_scale=scale, pie...  10.5 us
    unnamed x27, local copies, waits for them, and re-layouts  4.11 us
  transfers between devices with their start and end apart: 14, of which 7 were waited for; matrix products, arithmetic and copies ran while one was open for 1% of the time, Pallas kernels for 8%

profile of v3, /device:TPU:1, one launch (start us, length us, event | category | flops | bytes accessed | tf_op | source)
XLA Modules:
  0.0 189.6 jit_solution(7172270551271689395)
XLA Ops:
  0.6 8.8 %collective-permute-start.1 = (f32[2,256,256]{2,1,0:T(8,128)}, f32[2,256,256]{2,1,0:T(8,128)S(1)}, u32[]{:S(2)}, u32[]{:S(2)}) collective-permute-start(f32[2,256,256]{2,1,0:T(8,128)} %object_any.1), channel_id=1, source_target_pairs={{1,0},{2,1},{3,2},{4,3},{5,4},{6,5},{7,6},{8,7},{9,8},{10,9},{11,1... | collective-permute-start | bytes 1572872 | tf_op jit(solution)/shard_map/ppermute | solution.py:620
  9.4 1.3 collective-permute-start
  10.7 1.9 %collective-permute-done.1.right_any = f32[2,256,256]{2,1,0:T(8,128)S(1)} collective-permute-done((f32[2,256,256]{2,1,0:T(8,128)}, f32[2,256,256]{2,1,0:T(8,128)S(1)}, u32[]{:S(2)}, u32[]{:S(2)}) %collective-permute-start.1) | collective-permute-done | bytes 524320 | tf_op jit(solution)/shard_map/ppermute | solution.py:620
  12.6 12.5 %collective-permute-done.below_any = f32[2,256,256]{2,1,0:T(8,128)S(1)} collective-permute-done((f32[2,256,256]{2,1,0:T(8,128)}, f32[2,256,256]{2,1,0:T(8,128)S(1)}, u32[]{:S(2)}, u32[]{:S(2)}) %collective-permute-start) | collective-permute-done | bytes 524320 | tf_op jit(solution)/shard_map/ppermute | solution.py:620
  25.2 2.3 %collective-permute-start.2 = (f32[2,256,256]{2,1,0:T(8,128)S(1)}, f32[2,256,256]{2,1,0:T(8,128)S(1)}, u32[]{:S(2)}, u32[]{:S(2)}) collective-permute-start(f32[2,256,256]{2,1,0:T(8,128)S(1)} %collective-permute-done.below_any), channel_id=1, source_target_pairs={{1,0},{2,1},{3,2},{4,3},{5,4},{6,5},{7,6},{8,7},{9,8},{10,9},{11,1... | collective-permute-start | bytes 1572872 | tf_op jit(solution)/shard_map/ppermute | solution.py:620
  27.5 1.3 copy.25.positions_ref
  28.8 1.9 %collective-permute-start.7 = (f32[2,256,256]{2,1,0:T(8,128)}, f32[2,256,256]{2,1,0:T(8,128)S(1)}, u32[]{:S(2)}, u32[]{:S(2)}) collective-permute-start(f32[2,256,256]{2,1,0:T(8,128)} %prev_own_any.1), channel_id=1, source_target_pairs={{1,0},{2,1},{3,2},{4,3},{5,4},{6,5},{7,6},{8,7},{9,8},{10,9},{11,1... | collective-permute-start | bytes 1572872 | tf_op jit(solution)/shard_map/ppermute | solution.py:620
  30.7 1.3 collective-permute-start.6
  32.0 3.9 %collective-permute-done.2.diag_any = f32[2,256,256]{2,1,0:T(8,128)S(1)} collective-permute-done((f32[2,256,256]{2,1,0:T(8,128)S(1)}, f32[2,256,256]{2,1,0:T(8,128)S(1)}, u32[]{:S(2)}, u32[]{:S(2)}) %collective-permute-start.2) | collective-permute-done | bytes 524320 | tf_op jit(solution)/shard_map/ppermute | solution.py:620
  36.0 0.8 copy-done.12
  36.7 15.5 %gradient_frames.1 = (f32[2,256,256]{2,1,0:T(8,128)}, f32[2,256,256]{2,1,0:T(8,128)}, f32[2,256,256]{2,1,0:T(8,128)}, f32[2,256,256]{2,1,0:T(8,128)}, f32[1024,1...) custom-call(s32[1,1,4,2]{3,2,1,0:T(4,128)} %copy.25.positions_ref, ...), custom_call_target="tpu_custom_call" | custom-call | flops 10000000000 | bytes 10000000 | tf_op jit(solution)/shard_map/gradient_frames/pallas_call | solution.py:530
  52.3 4.2 %all-to-all-start = ((f32[64,16,128]{2,1,0:T(8,128)}), f32[64,16,128]{2,1,0:T(8,128)S(1)}, u32[]{:S(2)}, u32[]{:S(2)}) async-start(f32[64,16,128]{2,1,0:T(8,128)} %bitcast.8), calls=%async_computation | async-start | bytes 1048576 | tf_op jit(solution)/shard_map/all_to_all | solution.py:633
  56.5 3.1 %collective-permute-start.4 = (f32[2,256,256]{2,1,0:T(8,128)}, f32[2,256,256]{2,1,0:T(8,128)S(1)}, u32[]{:S(2)}, u32[]{:S(2)}) collective-permute-start(f32[2,256,256]{2,1,0:T(8,128)} %get-tuple-element.38), channel_id=1, source_target_pairs={{0,1},{1,2},{2,3},{3,4},{4,5},{5,6},{6,7},{7,8},{8,9},{9,10},{10,1... | collective-permute-start | bytes 1572872 | tf_op jit(solution)/shard_map/ppermute | solution.py:620
  59.6 1.9 %collective-permute-start.8 = (f32[2,256,256]{2,1,0:T(8,128)S(1)}, f32[2,256,256]{2,1,0:T(8,128)S(1)}, u32[]{:S(2)}, u32[]{:S(2)}) collective-permute-start(f32[2,256,256]{2,1,0:T(8,128)S(1)} %collective-permute-done.6.prev_below_any), channel_id=1, source_target_pairs={{1,0},{2,1},{3,2},{4,3},{5,4},{6,5},{7,6},{8,7},{9,8},{10,9},{11,1... | collective-permute-start | bytes 1572872 | tf_op jit(solution)/shard_map/ppermute | solution.py:620
  61.6 6.5 %collective-permute-done.4 = f32[2,256,256]{2,1,0:T(8,128)S(1)} collective-permute-done((f32[2,256,256]{2,1,0:T(8,128)}, f32[2,256,256]{2,1,0:T(8,128)S(1)}, u32[]{:S(2)}, u32[]{:S(2)}) %collective-permute-start.4) | collective-permute-done | bytes 524320 | tf_op jit(solution)/shard_map/ppermute | solution.py:620
  68.1 1.1 add.3
  69.2 3.0 %collective-permute-start.5 = (f32[2,256,256]{2,1,0:T(8,128)S(1)}, f32[2,256,256]{2,1,0:T(8,128)S(1)}, u32[]{:S(2)}, u32[]{:S(2)}) collective-permute-start(f32[2,256,256]{2,1,0:T(8,128)S(1)} %add.3), channel_id=1, source_target_pairs={{0,32},{32,64},{64,96},{96,128},{128,160},{160,192},{192,224},{224... | collective-permute-start | bytes 1572872 | tf_op jit(solution)/shard_map/ppermute | solution.py:620
  72.2 4.6 %collective-permute-start.3 = (f32[2,256,256]{2,1,0:T(8,128)}, f32[2,256,256]{2,1,0:T(8,128)S(1)}, u32[]{:S(2)}, u32[]{:S(2)}) collective-permute-start(f32[2,256,256]{2,1,0:T(8,128)} %get-tuple-element.36), channel_id=1, source_target_pairs={{0,1},{1,2},{2,3},{3,4},{4,5},{5,6},{6,7},{7,8},{8,9},{9,10},{10,1... | collective-permute-start | bytes 1572872 | tf_op jit(solution)/shard_map/ppermute | solution.py:620
  76.8 1.5 collective-permute-done.5.above_any
  78.3 4.9 %collective-permute-done.3.left_any = f32[2,256,256]{2,1,0:T(8,128)S(1)} collective-permute-done((f32[2,256,256]{2,1,0:T(8,128)}, f32[2,256,256]{2,1,0:T(8,128)S(1)}, u32[]{:S(2)}, u32[]{:S(2)}) %collective-permute-start.3) | collective-permute-done | bytes 524320 | tf_op jit(solution)/shard_map/ppermute | solution.py:620
  84.2 3.0 %fold.1 = (f32[2,256,256]{2,1,0:T(8,128)}, f32[8,17,128]{2,1,0:T(8,128)}) custom-call(f32[2,256,256]{2,1,0:T(8,128)} %get-tuple-element.35.own_any, f32[2,256,256]{2,1,0:T(8,128)} %copy-done.3, f32[2,256,256]{2,1,0:T(8,128)} %copy-done.2, f32[2,256,256]{2,1,0:T(8,128)} %prev_own_any.1, f32[64,16,128]{2,1,0:T(8,128)} %copy-done), custom_call_target="tpu_custom_call" | custom-call | flops 1000000 | bytes 10000000 | tf_op jit(solution)/shard_map/fold/pallas_call | solution.py:559
  87.2 1.9 %collective-permute-start.10 = (f32[2,256,256]{2,1,0:T(8,128)}, f32[2,256,256]{2,1,0:T(8,128)S(1)}, u32[]{:S(2)}, u32[]{:S(2)}) collective-permute-start(f32[2,256,256]{2,1,0:T(8,128)} %get-tuple-element.45.own_any), channel_id=1, source_target_pairs={{1,0},{2,1},{3,2},{4,3},{5,4},{6,5},{7,6},{8,7},{9,8},{10,9},{11,1... | collective-permute-start | bytes 1572872 | tf_op jit(solution)/shard_map/ppermute | solution.py:620
  89.1 1.5 collective-permute-start.9
  90.6 27.8 %all_to_all.25 = f32[8,17,128]{2,1,0:T(8,128)S(1)} all-to-all(f32[8,17,128]{2,1,0:T(8,128)} %get-tuple-element.46), channel_id=1, replica_groups={{0,4,8,12,16,20,24,28},{1,5,9,13,17,21,25,29},{2,6,10,14,18,22,26,30},{..., dimensions={0} | all-to-all | bytes 139264 | tf_op jit(solution)/shard_map/all_to_all | solution.py:633
  118.4 1.1 broadcast_in_dim.8
  119.5 11.9 %all-to-all-start.2 = ((f32[64,17,1,128]{3,2,1,0:T(1,128)}), f32[64,17,1,128]{3,2,1,0:T(1,128)S(1)}, u32[]{:S(2)}, u32[]{:S(2)}) async-start(f32[64,17,1,128]{3,2,1,0:T(1,128)} %broadcast_in_dim.8), calls=%async_computation.2 | async-start | bytes 1114112 | tf_op jit(solution)/shard_map/all_to_all | solution.py:633
  131.5 2.4 %collective-permute-start.11 = (f32[2,256,256]{2,1,0:T(8,128)S(1)}, f32[2,256,256]{2,1,0:T(8,128)S(1)}, u32[]{:S(2)}, u32[]{:S(2)}) collective-permute-start(f32[2,256,256]{2,1,0:T(8,128)S(1)} %collective-permute-done.9.below_any), channel_id=1, source_target_pairs={{1,0},{2,1},{3,2},{4,3},{5,4},{6,5},{7,6},{8,7},{9,8},{10,9},{11,1... | collective-permute-start | bytes 1572872 | tf_op jit(solution)/shard_map/ppermute | solution.py:620
  134.5 10.7 %collective-permute-done.11.diag_any = f32[2,256,256]{2,1,0:T(8,128)S(1)} collective-permute-done((f32[2,256,256]{2,1,0:T(8,128)S(1)}, f32[2,256,256]{2,1,0:T(8,128)S(1)}, u32[]{:S(2)}, u32[]{:S(2)}) %collective-permute-start.11) | collective-permute-done | bytes 524320 | tf_op jit(solution)/shard_map/ppermute | solution.py:620
  146.3 10.5 %curvature_frames.1 = (f32[2,256,256]{2,1,0:T(8,128)}, f32[2,256,256]{2,1,0:T(8,128)}, f32[1,128]{1,0:T(1,128)}) custom-call(s32[1,1,4,2]{3,2,1,0:T(4,128)} %copy.25.positions_ref, s32[1,32]{1,0:T(1,128)} %counts_ref.3, f32[1]{0:T(128)} %bitcast.6.prev_norm_ref, f32[2,256,256]{2,1,0:T(8,128)} %get-tuple-element.45.own_any, f32[2,256,256]{2,1,0:T(8,128)} %copy-done.8, ...), custom_call_target="tpu_custom_call" | custom-call | flops 5000000000 | bytes 10000000 | tf_op jit(solution)/shard_map/curvature_frames/pallas_call | solution.py:580
  157.4 13.8 %all_to_all.26 = f32[32,1,128]{2,1,0:T(1,128)S(1)} all-to-all(f32[32,1,128]{2,1,0:T(1,128)S(1)} %broadcast_in_dim.10), channel_id=1, replica_groups={{0,1,32,33,64,65,96,97,128,129,160,161,192,193,224,225,256,257,288,289,..., dimensions={0} | all-to-all | bytes 32768 | tf_op jit(solution)/shard_map/all_to_all | solution.py:633
  171.3 14.5 %all_to_all.27.gathered_ref = f32[16,1,128]{2,1,0:T(1,128)} all-to-all(f32[16,1,128]{2,1,0:T(1,128)S(1)} %broadcast_in_dim.22), channel_id=1, replica_groups={{0,2,4,6,8,10,12,14,16,18,20,22,24,26,28,30},{1,3,5,7,9,11,13,15,17,19,..., dimensions={0} | all-to-all | bytes 16384 | tf_op jit(solution)/shard_map/all_to_all | solution.py:633
  185.7 3.7 %update.1 = (f32[2,256,256]{2,1,0:T(8,128)}, f32[2,256,256]{2,1,0:T(8,128)}, f32[1,1]{1,0:T(1,128)}, f32[1,1,4]{2,1,0:T(1,128)}) custom-call(f32[16,1,128]{2,1,0:T(1,128)} %all_to_all.27.gathered_ref, f32[1,128]{1,0:T(1,128)} %get-tuple-element.55.sums_ref, f32[2,256,256]{2,1,0:T(8,128)} %object_any.1, f32[2,256,256]{2,1,0:T(8,128)} %get-tuple-element.30.direction_any, ...), custom_call_target="tpu_custom_call" | custom-call | flops 1000000 | bytes 10000000 | tf_op jit(solution)/shard_map/update/pallas_call | solution.py:606
  (36 shorter events, 2.7 us)
Async XLA Ops:
  0.6 12.0 %collective-permute-start.1 = (f32[2,256,256]{2,1,0:T(8,128)}, f32[2,256,256]{2,1,0:T(8,128)S(1)}, u32[]{:S(2)}, u32[]{:S(2)}) collective-permute-start(f32[2,256,256]{2,1,0:T(8,128)} %object_any.1), channel_id=1, source_target_pairs={{1,0},{2,1},{3,2},{4,3},{5,4},{6,5},{7,6},{8,7},{9,8},{10,9},{11,1... | collective-permute-start | bytes 1572872 | tf_op jit(solution)/shard_map/ppermute | solution.py:620
  9.4 15.7 %collective-permute-start = (f32[2,256,256]{2,1,0:T(8,128)}, f32[2,256,256]{2,1,0:T(8,128)S(1)}, u32[]{:S(2)}, u32[]{:S(2)}) collective-permute-start(f32[2,256,256]{2,1,0:T(8,128)} %object_any.1), channel_id=1, source_target_pairs={{32,0},{64,32},{96,64},{128,96},{160,128},{192,160},{224,192},{256... | collective-permute-start | bytes 1572872 | tf_op jit(solution)/shard_map/ppermute | solution.py:620
  12.6 23.3 %copy-start.9 = (f32[2,256,256]{2,1,0:T(8,128)}, f32[2,256,256]{2,1,0:T(8,128)S(1)}, u32[]{:S(2)}) copy-start(f32[2,256,256]{2,1,0:T(8,128)S(1)} %collective-permute-done.1.right_any) | copy-start | bytes 1572868
  25.2 10.8 %copy-start.10 = (f32[2,256,256]{2,1,0:T(8,128)}, f32[2,256,256]{2,1,0:T(8,128)S(1)}, u32[]{:S(2)}) copy-start(f32[2,256,256]{2,1,0:T(8,128)S(1)} %collective-permute-done.below_any) | copy-start | bytes 1572868
  25.2 10.8 %collective-permute-start.2 = (f32[2,256,256]{2,1,0:T(8,128)S(1)}, f32[2,256,256]{2,1,0:T(8,128)S(1)}, u32[]{:S(2)}, u32[]{:S(2)}) collective-permute-start(f32[2,256,256]{2,1,0:T(8,128)S(1)} %collective-permute-done.below_any), channel_id=1, source_target_pairs={{1,0},{2,1},{3,2},{4,3},{5,4},{6,5},{7,6},{8,7},{9,8},{10,9},{11,1... | collective-permute-start | bytes 1572872 | tf_op jit(solution)/shard_map/ppermute | solution.py:620
  28.8 23.4 %collective-permute-start.7 = (f32[2,256,256]{2,1,0:T(8,128)}, f32[2,256,256]{2,1,0:T(8,128)S(1)}, u32[]{:S(2)}, u32[]{:S(2)}) collective-permute-start(f32[2,256,256]{2,1,0:T(8,128)} %prev_own_any.1), channel_id=1, source_target_pairs={{1,0},{2,1},{3,2},{4,3},{5,4},{6,5},{7,6},{8,7},{9,8},{10,9},{11,1... | collective-permute-start | bytes 1572872 | tf_op jit(solution)/shard_map/ppermute | solution.py:620
  30.7 21.5 %collective-permute-start.6 = (f32[2,256,256]{2,1,0:T(8,128)}, f32[2,256,256]{2,1,0:T(8,128)S(1)}, u32[]{:S(2)}, u32[]{:S(2)}) collective-permute-start(f32[2,256,256]{2,1,0:T(8,128)} %prev_own_any.1), channel_id=1, source_target_pairs={{32,0},{64,32},{96,64},{128,96},{160,128},{192,160},{224,192},{256... | collective-permute-start | bytes 1572872 | tf_op jit(solution)/shard_map/ppermute | solution.py:620
  36.0 0.8 copy-start.12
  52.3 34.9 %copy-start.4 = (f32[2,256,256]{2,1,0:T(8,128)}, f32[2,256,256]{2,1,0:T(8,128)S(1)}, u32[]{:S(2)}) copy-start(f32[2,256,256]{2,1,0:T(8,128)S(1)} %collective-permute-done.7.prev_right_any) | copy-start | bytes 1572868
  52.3 34.9 %copy-start.5 = (f32[2,256,256]{2,1,0:T(8,128)}, f32[2,256,256]{2,1,0:T(8,128)S(1)}, u32[]{:S(2)}) copy-start(f32[2,256,256]{2,1,0:T(8,128)S(1)} %collective-permute-done.6.prev_below_any) | copy-start | bytes 1572868
  52.3 30.9 %all-to-all-start = ((f32[64,16,128]{2,1,0:T(8,128)}), f32[64,16,128]{2,1,0:T(8,128)S(1)}, u32[]{:S(2)}, u32[]{:S(2)}) async-start(f32[64,16,128]{2,1,0:T(8,128)} %bitcast.8), calls=%async_computation | async-start | bytes 1048576 | tf_op jit(solution)/shard_map/all_to_all | solution.py:633
  56.5 11.6 %collective-permute-start.4 = (f32[2,256,256]{2,1,0:T(8,128)}, f32[2,256,256]{2,1,0:T(8,128)S(1)}, u32[]{:S(2)}, u32[]{:S(2)}) collective-permute-start(f32[2,256,256]{2,1,0:T(8,128)} %get-tuple-element.38), channel_id=1, source_target_pairs={{0,1},{1,2},{2,3},{3,4},{4,5},{5,6},{6,7},{7,8},{8,9},{9,10},{10,1... | collective-permute-start | bytes 1572872 | tf_op jit(solution)/shard_map/ppermute | solution.py:620
  59.6 17.2 %collective-permute-start.8 = (f32[2,256,256]{2,1,0:T(8,128)S(1)}, f32[2,256,256]{2,1,0:T(8,128)S(1)}, u32[]{:S(2)}, u32[]{:S(2)}) collective-permute-start(f32[2,256,256]{2,1,0:T(8,128)S(1)} %collective-permute-done.6.prev_below_any), channel_id=1, source_target_pairs={{1,0},{2,1},{3,2},{4,3},{5,4},{6,5},{7,6},{8,7},{9,8},{10,9},{11,1... | collective-permute-start | bytes 1572872 | tf_op jit(solution)/shard_map/ppermute | solution.py:620
  69.2 9.1 %collective-permute-start.5 = (f32[2,256,256]{2,1,0:T(8,128)S(1)}, f32[2,256,256]{2,1,0:T(8,128)S(1)}, u32[]{:S(2)}, u32[]{:S(2)}) collective-permute-start(f32[2,256,256]{2,1,0:T(8,128)S(1)} %add.3), channel_id=1, source_target_pairs={{0,32},{32,64},{64,96},{96,128},{128,160},{160,192},{192,224},{224... | collective-permute-start | bytes 1572872 | tf_op jit(solution)/shard_map/ppermute | solution.py:620
  72.2 11.0 %collective-permute-start.3 = (f32[2,256,256]{2,1,0:T(8,128)}, f32[2,256,256]{2,1,0:T(8,128)S(1)}, u32[]{:S(2)}, u32[]{:S(2)}) collective-permute-start(f32[2,256,256]{2,1,0:T(8,128)} %get-tuple-element.36), channel_id=1, source_target_pairs={{0,1},{1,2},{2,3},{3,4},{4,5},{5,6},{6,7},{7,8},{8,9},{9,10},{10,1... | collective-permute-start | bytes 1572872 | tf_op jit(solution)/shard_map/ppermute | solution.py:620
  76.8 68.4 %copy-start.6 = (f32[2,256,256]{2,1,0:T(8,128)}, f32[2,256,256]{2,1,0:T(8,128)S(1)}, u32[]{:S(2)}) copy-start(f32[2,256,256]{2,1,0:T(8,128)S(1)} %collective-permute-done.8.prev_diag_any) | copy-start | bytes 1572868
  78.3 4.9 %copy-start.2 = (f32[2,256,256]{2,1,0:T(8,128)}, f32[2,256,256]{2,1,0:T(8,128)S(1)}, u32[]{:S(2)}) copy-start(f32[2,256,256]{2,1,0:T(8,128)S(1)} %collective-permute-done.5.above_any) | copy-start | bytes 1572868
  83.2 0.8 copy-start.3
  83.2 1.0 copy-start
  87.2 31.2 %collective-permute-start.10 = (f32[2,256,256]{2,1,0:T(8,128)}, f32[2,256,256]{2,1,0:T(8,128)S(1)}, u32[]{:S(2)}, u32[]{:S(2)}) collective-permute-start(f32[2,256,256]{2,1,0:T(8,128)} %get-tuple-element.45.own_any), channel_id=1, source_target_pairs={{1,0},{2,1},{3,2},{4,3},{5,4},{6,5},{7,6},{8,7},{9,8},{10,9},{11,1... | collective-permute-start | bytes 1572872 | tf_op jit(solution)/shard_map/ppermute | solution.py:620
  89.1 29.3 %collective-permute-start.9 = (f32[2,256,256]{2,1,0:T(8,128)}, f32[2,256,256]{2,1,0:T(8,128)S(1)}, u32[]{:S(2)}, u32[]{:S(2)}) collective-permute-start(f32[2,256,256]{2,1,0:T(8,128)} %get-tuple-element.45.own_any), channel_id=1, source_target_pairs={{32,0},{64,32},{96,64},{128,96},{160,128},{192,160},{224,192},{256... | collective-permute-start | bytes 1572872 | tf_op jit(solution)/shard_map/ppermute | solution.py:620
  118.4 26.9 %copy-start.7 = (f32[2,256,256]{2,1,0:T(8,128)}, f32[2,256,256]{2,1,0:T(8,128)S(1)}, u32[]{:S(2)}) copy-start(f32[2,256,256]{2,1,0:T(8,128)S(1)} %collective-permute-done.10.right_any) | copy-start | bytes 1572868
  118.4 26.9 %copy-start.8 = (f32[2,256,256]{2,1,0:T(8,128)}, f32[2,256,256]{2,1,0:T(8,128)S(1)}, u32[]{:S(2)}) copy-start(f32[2,256,256]{2,1,0:T(8,128)S(1)} %collective-permute-done.9.below_any) | copy-start | bytes 1572868
  119.5 25.7 %all-to-all-start.2 = ((f32[64,17,1,128]{3,2,1,0:T(1,128)}), f32[64,17,1,128]{3,2,1,0:T(1,128)S(1)}, u32[]{:S(2)}, u32[]{:S(2)}) async-start(f32[64,17,1,128]{3,2,1,0:T(1,128)} %broadcast_in_dim.8), calls=%async_computation.2 | async-start | bytes 1114112 | tf_op jit(solution)/shard_map/all_to_all | solution.py:633
  131.5 13.8 %collective-permute-start.11 = (f32[2,256,256]{2,1,0:T(8,128)S(1)}, f32[2,256,256]{2,1,0:T(8,128)S(1)}, u32[]{:S(2)}, u32[]{:S(2)}) collective-permute-start(f32[2,256,256]{2,1,0:T(8,128)S(1)} %collective-permute-done.9.below_any), channel_id=1, source_target_pairs={{1,0},{2,1},{3,2},{4,3},{5,4},{6,5},{7,6},{8,7},{9,8},{10,9},{11,1... | collective-permute-start | bytes 1572872 | tf_op jit(solution)/shard_map/ppermute | solution.py:620
  145.2 0.8 copy-start.11
  145.2 1.0 copy-start.1

commit v4 on v3

--- a/solution.py
+++ b/solution.py
@@ -10,6 +10,8 @@
 from jax.sharding import PartitionSpec as P
 
 VMEM_BYTES = 60 * 1024 * 1024
+
+FOLD_FLOPS = 2 * 10**10
 
 
 def dft_blocks(width):
@@ -295,32 +297,35 @@
     own_any,
     left_any,
     above_any,
+    corner_any,
     prev_any,
-    pieces_any,
     grad_any,
-    payload_ref,
+    products_ref,
     held_ref,
-    pieces_ref,
     grad_ref,
     in_sems,
     out_sem,
 ):
-    sources = [own_any, left_any, above_any, prev_any, pieces_any]
-    targets = [held_ref.at[at] for at in range(4)] + [pieces_ref]
-    own, left, above, prev, pieces = incoming(sources, targets, in_sems)
-    grad_ref[...] = own()[...] + left()[...] + above()[...]
+    sources = [own_any, left_any, above_any, corner_any, prev_any]
+    targets = [held_ref.at[at] for at in range(5)]
+    own, left, above, diag, prev = incoming(sources, targets, in_sems)
+    grad_ref[...] = own()[...] + left()[...] + above()[...] + diag()[...]
     copy = pltpu.make_async_copy(grad_ref, grad_any, out_sem)
     copy.start()
     square = jnp.sum(grad_ref[...] * grad_ref[...])
     along = jnp.sum(grad_ref[...] * prev()[...])
+    lanes = lax.broadcasted_iota(jnp.int32, products_ref.shape, 1)
+    products_ref[...] = jnp.where(lanes == 0, square, jnp.where(lanes == 1, along, 0.0))
+    copy.wait()
+
+
+def payload_kernel(pieces_any, products_ref, payload_ref, pieces_ref, in_sem):
+    (pieces,) = incoming([pieces_any], [pieces_ref], in_sem)
     piece = jnp.sum(pieces()[...], axis=0)
     depth = piece.shape[0]
-    lanes = lax.broadcasted_iota(jnp.int32, (1, payload_ref.shape[2]), 1)
-    extra = jnp.where(lanes == 0, square, jnp.where(lanes == 1, along, 0.0))
     for at in range(payload_ref.shape[0]):
         payload_ref[at, :depth] = piece
-        payload_ref[at, depth:] = extra
-    copy.wait()
+        payload_ref[at, depth:] = products_ref[...]
 
 
 def curvature_kernel(
@@ -553,24 +558,34 @@
     )(positions, counts, *tiles, probe, measured, *tables)
 
 
-def fold_call(parts, prev, pieces, targets):
+def fold_call(parts, prev):
     shape = prev.shape
-    depth = pieces.shape[1]
     return pl.pallas_call(
         fold_kernel,
-        out_shape=(shaped(*shape), shaped(targets, depth + 1, pieces.shape[2])),
+        out_shape=(shaped(*shape), shaped(1, 128)),
         in_specs=anywhere(5),
         out_specs=(*anywhere(1), *in_vmem(1)),
         scratch_shapes=[
-            buffer(4, *shape),
-            buffer(*pieces.shape),
+            buffer(5, *shape),
             buffer(*shape),
             arrivals_of(5),
             pltpu.SemaphoreType.DMA,
         ],
         name="fold",
+        **costing(FOLD_FLOPS),
+    )(*parts, prev)
+
+
+def payload_call(pieces, products, targets):
+    return pl.pallas_call(
+        payload_kernel,
+        out_shape=shaped(targets, pieces.shape[1] + 1, pieces.shape[2]),
+        in_specs=anywhere(1) + in_vmem(1),
+        out_specs=in_vmem(1)[0],
+        scratch_shapes=[buffer(*pieces.shape), arrivals_of(1)],
+        name="payload",
         **costing(10**6),
-    )(*parts, prev, pieces)
+    )(pieces, products)
 
 
 def curvature_call(positions, counts, prev_norm, tiles, total, pieces, kept, tables, probe_prev, scale):
@@ -620,6 +635,17 @@
     return lax.ppermute(shard, axis, pairs)
 
 
+def passed_across(shard, by):
+    rows, cols = lax.axis_size("row"), lax.axis_size("col")
+    pairs = [
+        (row * cols + col, (row + by) * cols + col + by)
+        for row in range(rows)
+        for col in range(cols)
+        if 0 <= row + by < rows and 0 <= col + by < cols
+    ]
+    return lax.ppermute(shard, ("row", "col"), pairs)
+
+
 def device_groups(block):
     rows, cols = lax.axis_size("row"), lax.axis_size("col")
     near = [
@@ -659,9 +685,11 @@
 
     right = passed_along(object_field, "col", -1)
     below = passed_along(object_field, "row", -1)
-    diag = passed_along(held(below, right), "col", -1)
-    prev_below = passed_along(held(object_dir_prev, below), "row", -1)
-    prev_right = passed_along(held(object_dir_prev, below), "col", -1)
+    diag = passed_along(below, "col", -1)
+    prev = held(object_dir_prev, below)
+    prev_below = passed_along(prev, "row", -1)
+    prev_right = passed_along(prev, "col", -1)
+    prev_diag = passed_across(prev, -1)
 
     own_grad, below_grad, right_grad, diag_grad, probe_part, *kept = gradient_call(
         positions,
@@ -671,27 +699,25 @@
         intensities,
         tables,
     )
-    probe_part, prev_below, prev_right = lax.optimization_barrier(
-        (probe_part, prev_below, prev_right)
-    )
-    from_left_diag = passed_along(diag_grad, "col", 1)
+    probe_part, prev_below, prev_right, prev_diag = lax.optimization_barrier(
+        (probe_part, prev_below, prev_right, prev_diag)
+    )
+    corner_part = passed_across(diag_grad, 1)
+    from_above = passed_along(below_grad, "row", 1)
+    from_left = passed_along(right_grad, "col", 1)
     pieces = exchanged(probe_part.reshape((len(near[0]), -1, width // 2)), near)
-    from_above = passed_along(below_grad + from_left_diag, "row", 1)
-    from_left = passed_along(right_grad, "col", 1)
-    prev_diag = passed_along(held(prev_below, diag_grad), "col", -1)
-    from_above = held(from_above, prev_diag)
-    object_grad, payload = fold_call(
-        (own_grad, from_left, from_above), object_dir_prev, pieces, len(apart[0])
-    )
+    object_grad, products = fold_call(
+        (own_grad, from_left, from_above, corner_part), object_dir_prev
+    )
+    payload = payload_call(pieces, products, len(apart[0]))
     grad_below = passed_along(object_grad, "row", -1)
     grad_right = passed_along(object_grad, "col", -1)
-    payload, grad_below, grad_right = lax.optimization_barrier(
-        (exchanged(payload, apart), grad_below, grad_right)
+    grad_diag = passed_across(object_grad, -1)
+    payload, grad_below, grad_right, grad_diag = lax.optimization_barrier(
+        (exchanged(payload, apart), grad_below, grad_right, grad_diag)
     )
     payload = jnp.sum(payload, axis=0)[:, None, :]
-    grad_diag = passed_along(grad_below, "col", -1)
     total = exchanged(copies(payload, near), near)
-    total = held(total, grad_diag)
     object_direction, probe_direction, sums = curvature_call(
         positions,
         counts,

time: 191 us -> 194 us (1.016)
  starting transfers between devices: 50.1 us -> 92.6 us
  blocking collectives: 56.1 us -> 24.4 us
  waiting for transfers between devices: 42 us -> 32.7 us
  Pallas kernels: 32.7 us -> 35.2 us
    ppermute x12 -> x9, waiting for transfers between devices: 42 us -> 2.63 us  [passed_along(): return lax.ppermute(shard, axis, pairs)]
    all_to_all x2 -> x3, starting transfers between devices: 16.1 us -> 52.6 us  [exchanged(): lax.all_to_all(pieces, ('row', 'col'), 0, 0, axis_index_groups=groups)]
    all_to_all x3 -> x2, blocking collectives: 56.1 us -> 24.4 us  [exchanged(): lax.all_to_all(pieces, ('row', 'col'), 0, 0, axis_index_groups=groups)]
    all_to_all x2 -> x3, waiting for transfers between devices: 0.01 us -> 30 us  [exchanged(): lax.all_to_all(pieces, ('row', 'col'), 0, 0, axis_index_groups=groups)]
    ppermute x0 -> x3, starting transfers between devices: none -> 8.21 us  [passed_across(): return lax.ppermute(shard, ('row', 'col'), pairs)]
    pallas_call x1 -> x2, Pallas kernels: 2.97 us -> 5.4 us  [the longest x1 2.99 us: fold_call(): pl.pallas_call(fold_kernel, out_shape=(shaped(*shape), shaped(1, 128)), i...]
    ppermute x12 -> x9, starting transfers between devices: 34 us -> 31.8 us  [passed_along(): return lax.ppermute(shard, axis, pairs)]
  transfers between devices with their start and end apart: 14 -> 15, of which waited for: 7 -> 5; matrix products, arithmetic and copies ran while one was open for 1% -> 1% of each run, Pallas kernels for 8% -> 11%
where the time goes in v4:
time: 194 us; the launch traced here: 193 us
  starting transfers between devices  92.6 us (48%)
  Pallas kernels  35.2 us (18%)
  waiting for transfers between devices  32.7 us (17%)
  blocking collectives  24.4 us (13%)
  local copies, waits for them, and re-layouts  6.46 us (3%)
    all_to_all x3, starting transfers between devices, exchanged(): lax.all_to_all(pieces, ('row', 'col'), 0, 0, axis_index_groups=groups)  52.6 us
    ppermute x9, starting transfers between devices, passed_along(): return lax.ppermute(shard, axis, pairs)  31.8 us
    all_to_all x3, waiting for transfers between devices, exchanged(): lax.all_to_all(pieces, ('row', 'col'), 0, 0, axis_index_groups=groups)  30 us
    all_to_all x2, blocking collectives, exchanged(): lax.all_to_all(pieces, ('row', 'col'), 0, 0, axis_index_groups=groups)  24.4 us
    pallas_call x1, Pallas kernels, gradient_call(): pl.pallas_call(gradient_kernel, out_shape=(shaped(2, width, width),) * 4...  15.5 us
    pallas_call x1, Pallas kernels, curvature_call(): pl.pallas_call(functools.partial(curvature_kernel, probe_scale=scale, pie...  10.5 us
    ppermute x3, starting transfers between devices, passed_across(): return lax.ppermute(shard, ('row', 'col'), pairs)  8.21 us
    unnamed x27, local copies, waits for them, and re-layouts  4.69 us
  transfers between devices with their start and end apart: 15, of which 5 were waited for; matrix products, arithmetic and copies ran while one was open for 1% of the time, Pallas kernels for 11%

profile of v4, /device:TPU:1, one launch (start us, length us, event | category | flops | bytes accessed | tf_op | source)
XLA Modules:
  0.0 193.1 jit_solution(994029546353459825)
XLA Ops:
  0.6 1.3 collective-permute-start
  1.9 8.8 %collective-permute-start.1 = (f32[2,256,256]{2,1,0:T(8,128)}, f32[2,256,256]{2,1,0:T(8,128)S(1)}, u32[]{:S(2)}, u32[]{:S(2)}) collective-permute-start(f32[2,256,256]{2,1,0:T(8,128)} %object_any.1), channel_id=1, source_target_pairs={{1,0},{2,1},{3,2},{4,3},{5,4},{6,5},{7,6},{8,7},{9,8},{10,9},{11,1... | collective-permute-start | bytes 1572872 | tf_op jit(solution)/shard_map/ppermute | solution.py:635
  11.4 9.3 %collective-permute-start.2 = (f32[2,256,256]{2,1,0:T(8,128)S(1)}, f32[2,256,256]{2,1,0:T(8,128)S(1)}, u32[]{:S(2)}, u32[]{:S(2)}) collective-permute-start(f32[2,256,256]{2,1,0:T(8,128)S(1)} %collective-permute-done.below_any), channel_id=1, source_target_pairs={{1,0},{2,1},{3,2},{4,3},{5,4},{6,5},{7,6},{8,7},{9,8},{10,9},{11,1... | collective-permute-start | bytes 1572872 | tf_op jit(solution)/shard_map/ppermute | solution.py:635
  20.7 1.3 copy.25.positions_ref
  22.0 1.3 collective-permute-start.6
  23.3 1.9 collective-permute-start.7
  25.3 1.3 collective-permute-start.8
  26.6 1.9 collective-permute-done.2.diag_any
  28.5 0.8 copy-done.12
  29.3 15.5 %gradient_frames.1 = (f32[2,256,256]{2,1,0:T(8,128)}, f32[2,256,256]{2,1,0:T(8,128)}, f32[2,256,256]{2,1,0:T(8,128)}, f32[2,256,256]{2,1,0:T(8,128)}, f32[1024,1...) custom-call(s32[1,1,4,2]{3,2,1,0:T(4,128)} %copy.25.positions_ref, ...), custom_call_target="tpu_custom_call" | custom-call | flops 10000000000 | bytes 10000000 | tf_op jit(solution)/shard_map/gradient_frames/pallas_call | solution.py:535
  44.8 1.9 collective-permute-start.3
  46.7 3.5 %collective-permute-start.4 = (f32[2,256,256]{2,1,0:T(8,128)}, f32[2,256,256]{2,1,0:T(8,128)S(1)}, u32[]{:S(2)}, u32[]{:S(2)}) collective-permute-start(f32[2,256,256]{2,1,0:T(8,128)} %get-tuple-element.34), channel_id=1, source_target_pairs={{0,32},{32,64},{64,96},{96,128},{128,160},{160,192},{192,224},{224... | collective-permute-start | bytes 1572872 | tf_op jit(solution)/shard_map/ppermute | solution.py:635
  50.3 5.6 %collective-permute-start.5 = (f32[2,256,256]{2,1,0:T(8,128)}, f32[2,256,256]{2,1,0:T(8,128)}, u32[]{:S(2)}, u32[]{:S(2)}) collective-permute-start(f32[2,256,256]{2,1,0:T(8,128)} %get-tuple-element.35), channel_id=1, source_target_pairs={{0,33},{1,34},{2,35},{3,36},{4,37},{5,38},{6,39},{7,40},{8,41},{9,... | collective-permute-start | bytes 1572872 | tf_op jit(solution)/shard_map/ppermute | solution.py:646
  55.9 11.7 %all-to-all-start = ((f32[64,16,128]{2,1,0:T(8,128)}), f32[64,16,128]{2,1,0:T(8,128)S(1)}, u32[]{:S(2)}, u32[]{:S(2)}) async-start(f32[64,16,128]{2,1,0:T(8,128)} %bitcast.8), calls=%async_computation | async-start | bytes 1048576 | tf_op jit(solution)/shard_map/all_to_all | solution.py:659
  67.7 0.8 copy-done.9
  68.6 3.0 %fold.1 = (f32[2,256,256]{2,1,0:T(8,128)}, f32[1,128]{1,0:T(1,128)}) custom-call(f32[2,256,256]{2,1,0:T(8,128)} %get-tuple-element.32.own_any, f32[2,256,256]{2,1,0:T(8,128)} %copy-done.9, f32[2,256,256]{2,1,0:T(8,128)} %copy-done.11, f32[2,256,256]{2,1,0:T(8,128)} %collective-permute-done.5.corner_any, f32[2,256,256]{2,1,0:T(8,128)} %prev_own_any.1), custom_call_target="tpu_custom_call" | custom-call | flops 20000000000 | bytes 10000000 | tf_op jit(solution)/shard_map/fold/pallas_call | solution.py:563
  71.6 2.4 %collective-permute-start.10 = (f32[2,256,256]{2,1,0:T(8,128)}, f32[2,256,256]{2,1,0:T(8,128)S(1)}, u32[]{:S(2)}, u32[]{:S(2)}) collective-permute-start(f32[2,256,256]{2,1,0:T(8,128)} %get-tuple-element.36.own_any), channel_id=1, source_target_pairs={{1,0},{2,1},{3,2},{4,3},{5,4},{6,5},{7,6},{8,7},{9,8},{10,9},{11,1... | collective-permute-start | bytes 1572872 | tf_op jit(solution)/shard_map/ppermute | solution.py:635
  74.0 1.3 collective-permute-start.11
  75.3 1.5 collective-permute-start.9
  76.8 5.2 %all-to-all-done.pieces_any = f32[64,16,128]{2,1,0:T(8,128)S(1)} async-done(((f32[64,16,128]{2,1,0:T(8,128)}), f32[64,16,128]{2,1,0:T(8,128)S(1)}, u32[]{:S(2)}, u32[]{:S(2)}) %all-to-all-start) | async-done | bytes 524320 | tf_op jit(solution)/shard_map/all_to_all | solution.py:659
  82.0 0.8 copy-done
  82.8 2.4 %payload.1 = f32[8,17,128]{2,1,0:T(8,128)} custom-call(f32[64,16,128]{2,1,0:T(8,128)} %copy-done, f32[1,128]{1,0:T(1,128)} %get-tuple-element.40.products_ref), custom_call_target="tpu_custom_call" | custom-call | flops 1000000 | bytes 10000000 | tf_op jit(solution)/shard_map/payload/pallas_call | solution.py:580
  85.2 18.9 %all-to-all-start.1 = ((f32[8,17,128]{2,1,0:T(8,128)}), f32[8,17,128]{2,1,0:T(8,128)S(1)}, u32[]{:S(2)}, u32[]{:S(2)}) async-start(f32[8,17,128]{2,1,0:T(8,128)} %payload.1), calls=%async_computation.1 | async-start | bytes 196608 | tf_op jit(solution)/shard_map/all_to_all | solution.py:659
  104.2 12.3 %all-to-all-done.1 = f32[8,17,128]{2,1,0:T(8,128)S(1)} async-done(((f32[8,17,128]{2,1,0:T(8,128)}), f32[8,17,128]{2,1,0:T(8,128)S(1)}, u32[]{:S(2)}, u32[]{:S(2)}) %all-to-all-start.1) | async-done | bytes 69664 | tf_op jit(solution)/shard_map/all_to_all | solution.py:659
  116.5 1.1 broadcast_in_dim.8
  117.6 22.0 %all-to-all-start.2 = ((f32[64,17,1,128]{3,2,1,0:T(1,128)}), f32[64,17,1,128]{3,2,1,0:T(1,128)S(1)}, u32[]{:S(2)}, u32[]{:S(2)}) async-start(f32[64,17,1,128]{3,2,1,0:T(1,128)} %broadcast_in_dim.8), calls=%async_computation.2 | async-start | bytes 1114112 | tf_op jit(solution)/shard_map/all_to_all | solution.py:659
  140.3 12.5 %all-to-all-done.2 = f32[64,17,1,128]{3,2,1,0:T(1,128)S(1)} async-done(((f32[64,17,1,128]{3,2,1,0:T(1,128)}), f32[64,17,1,128]{3,2,1,0:T(1,128)S(1)}, u32[]{:S(2)}, u32[]{:S(2)}) %all-to-all-start.2) | async-done | bytes 557088 | tf_op jit(solution)/shard_map/all_to_all | solution.py:659
  152.8 0.8 copy-done.1
  153.6 10.5 %curvature_frames.1 = (f32[2,256,256]{2,1,0:T(8,128)}, f32[2,256,256]{2,1,0:T(8,128)}, f32[1,128]{1,0:T(1,128)}) custom-call(s32[1,1,4,2]{3,2,1,0:T(4,128)} %copy.25.positions_ref, s32[1,32]{1,0:T(1,128)} %counts_ref.3, f32[1]{0:T(128)} %bitcast.6.prev_norm_ref, f32[2,256,256]{2,1,0:T(8,128)} %get-tuple-element.36.own_any, f32[2,256,256]{2,1,0:T(8,128)} %copy-done.7, ...), custom_call_target="tpu_custom_call" | custom-call | flops 5000000000 | bytes 10000000 | tf_op jit(solution)/shard_map/curvature_frames/pallas_call | solution.py:595
  164.8 9.9 %all_to_all.25 = f32[32,1,128]{2,1,0:T(1,128)S(1)} all-to-all(f32[32,1,128]{2,1,0:T(1,128)S(1)} %broadcast_in_dim.10), channel_id=1, replica_groups={{0,1,32,33,64,65,96,97,128,129,160,161,192,193,224,225,256,257,288,289,..., dimensions={0} | all-to-all | bytes 32768 | tf_op jit(solution)/shard_map/all_to_all | solution.py:659
  174.7 14.4 %all_to_all.26.gathered_ref = f32[16,1,128]{2,1,0:T(1,128)} all-to-all(f32[16,1,128]{2,1,0:T(1,128)S(1)} %broadcast_in_dim.22), channel_id=1, replica_groups={{0,2,4,6,8,10,12,14,16,18,20,22,24,26,28,30},{1,3,5,7,9,11,13,15,17,19,..., dimensions={0} | all-to-all | bytes 16384 | tf_op jit(solution)/shard_map/all_to_all | solution.py:659
  189.2 3.7 %update.1 = (f32[2,256,256]{2,1,0:T(8,128)}, f32[2,256,256]{2,1,0:T(8,128)}, f32[1,1]{1,0:T(1,128)}, f32[1,1,4]{2,1,0:T(1,128)}) custom-call(f32[16,1,128]{2,1,0:T(1,128)} %all_to_all.26.gathered_ref, f32[1,128]{1,0:T(1,128)} %get-tuple-element.51.sums_ref, f32[2,256,256]{2,1,0:T(8,128)} %object_any.1, f32[2,256,256]{2,1,0:T(8,128)} %get-tuple-element.28.direction_any, ...), custom_call_target="tpu_custom_call" | custom-call | flops 1000000 | bytes 10000000 | tf_op jit(solution)/shard_map/update/pallas_call | solution.py:621
  (37 shorter events, 1.7 us)
Async XLA Ops:
  0.6 10.8 %collective-permute-start = (f32[2,256,256]{2,1,0:T(8,128)}, f32[2,256,256]{2,1,0:T(8,128)S(1)}, u32[]{:S(2)}, u32[]{:S(2)}) collective-permute-start(f32[2,256,256]{2,1,0:T(8,128)} %object_any.1), channel_id=1, source_target_pairs={{32,0},{64,32},{96,64},{128,96},{160,128},{192,160},{224,192},{256... | collective-permute-start | bytes 1572872 | tf_op jit(solution)/shard_map/ppermute | solution.py:635
  1.9 24.6 %collective-permute-start.1 = (f32[2,256,256]{2,1,0:T(8,128)}, f32[2,256,256]{2,1,0:T(8,128)S(1)}, u32[]{:S(2)}, u32[]{:S(2)}) collective-permute-start(f32[2,256,256]{2,1,0:T(8,128)} %object_any.1), channel_id=1, source_target_pairs={{1,0},{2,1},{3,2},{4,3},{5,4},{6,5},{7,6},{8,7},{9,8},{10,9},{11,1... | collective-permute-start | bytes 1572872 | tf_op jit(solution)/shard_map/ppermute | solution.py:635
  11.4 17.0 %copy-start.8 = (f32[2,256,256]{2,1,0:T(8,128)}, f32[2,256,256]{2,1,0:T(8,128)S(1)}, u32[]{:S(2)}) copy-start(f32[2,256,256]{2,1,0:T(8,128)S(1)} %collective-permute-done.below_any) | copy-start | bytes 1572868
  11.4 17.0 %collective-permute-start.2 = (f32[2,256,256]{2,1,0:T(8,128)S(1)}, f32[2,256,256]{2,1,0:T(8,128)S(1)}, u32[]{:S(2)}, u32[]{:S(2)}) collective-permute-start(f32[2,256,256]{2,1,0:T(8,128)S(1)} %collective-permute-done.below_any), channel_id=1, source_target_pairs={{1,0},{2,1},{3,2},{4,3},{5,4},{6,5},{7,6},{8,7},{9,8},{10,9},{11,1... | collective-permute-start | bytes 1572872 | tf_op jit(solution)/shard_map/ppermute | solution.py:635
  22.0 28.2 %collective-permute-start.6 = (f32[2,256,256]{2,1,0:T(8,128)}, f32[2,256,256]{2,1,0:T(8,128)S(1)}, u32[]{:S(2)}, u32[]{:S(2)}) collective-permute-start(f32[2,256,256]{2,1,0:T(8,128)} %prev_own_any.1), channel_id=1, source_target_pairs={{32,0},{64,32},{96,64},{128,96},{160,128},{192,160},{224,192},{256... | collective-permute-start | bytes 1572872 | tf_op jit(solution)/shard_map/ppermute | solution.py:635
  23.3 32.6 %collective-permute-start.7 = (f32[2,256,256]{2,1,0:T(8,128)}, f32[2,256,256]{2,1,0:T(8,128)S(1)}, u32[]{:S(2)}, u32[]{:S(2)}) collective-permute-start(f32[2,256,256]{2,1,0:T(8,128)} %prev_own_any.1), channel_id=1, source_target_pairs={{1,0},{2,1},{3,2},{4,3},{5,4},{6,5},{7,6},{8,7},{9,8},{10,9},{11,1... | collective-permute-start | bytes 1572872 | tf_op jit(solution)/shard_map/ppermute | solution.py:635
  25.3 30.7 %collective-permute-start.8 = (f32[2,256,256]{2,1,0:T(8,128)}, f32[2,256,256]{2,1,0:T(8,128)S(1)}, u32[]{:S(2)}, u32[]{:S(2)}) collective-permute-start(f32[2,256,256]{2,1,0:T(8,128)} %prev_own_any.1), channel_id=1, source_target_pairs={{33,0},{34,1},{35,2},{36,3},{37,4},{38,5},{39,6},{40,7},{41,8},{42... | collective-permute-start | bytes 1572872 | tf_op jit(solution)/shard_map/ppermute | solution.py:646
  26.6 1.9 copy-start.10
  28.5 0.8 copy-start.12
  44.8 22.8 %collective-permute-start.3 = (f32[2,256,256]{2,1,0:T(8,128)}, f32[2,256,256]{2,1,0:T(8,128)S(1)}, u32[]{:S(2)}, u32[]{:S(2)}) collective-permute-start(f32[2,256,256]{2,1,0:T(8,128)} %get-tuple-element.33), channel_id=1, source_target_pairs={{0,1},{1,2},{2,3},{3,4},{4,5},{5,6},{6,7},{7,8},{8,9},{9,10},{10,1... | collective-permute-start | bytes 1572872 | tf_op jit(solution)/shard_map/ppermute | solution.py:635
  46.7 20.9 %collective-permute-start.4 = (f32[2,256,256]{2,1,0:T(8,128)}, f32[2,256,256]{2,1,0:T(8,128)S(1)}, u32[]{:S(2)}, u32[]{:S(2)}) collective-permute-start(f32[2,256,256]{2,1,0:T(8,128)} %get-tuple-element.34), channel_id=1, source_target_pairs={{0,32},{32,64},{64,96},{96,128},{128,160},{160,192},{192,224},{224... | collective-permute-start | bytes 1572872 | tf_op jit(solution)/shard_map/ppermute | solution.py:635
  50.3 21.3 %copy-start.2 = (f32[2,256,256]{2,1,0:T(8,128)}, f32[2,256,256]{2,1,0:T(8,128)S(1)}, u32[]{:S(2)}) copy-start(f32[2,256,256]{2,1,0:T(8,128)S(1)} %collective-permute-done.6.prev_below_any) | copy-start | bytes 1572868
  50.3 17.4 %collective-permute-start.5 = (f32[2,256,256]{2,1,0:T(8,128)}, f32[2,256,256]{2,1,0:T(8,128)}, u32[]{:S(2)}, u32[]{:S(2)}) collective-permute-start(f32[2,256,256]{2,1,0:T(8,128)} %get-tuple-element.35), channel_id=1, source_target_pairs={{0,33},{1,34},{2,35},{3,36},{4,37},{5,38},{6,39},{7,40},{8,41},{9,... | collective-permute-start | bytes 1572872 | tf_op jit(solution)/shard_map/ppermute | solution.py:646
  55.9 15.7 %copy-start.3 = (f32[2,256,256]{2,1,0:T(8,128)}, f32[2,256,256]{2,1,0:T(8,128)S(1)}, u32[]{:S(2)}) copy-start(f32[2,256,256]{2,1,0:T(8,128)S(1)} %collective-permute-done.7.prev_right_any) | copy-start | bytes 1572868
  55.9 15.7 %copy-start.4 = (f32[2,256,256]{2,1,0:T(8,128)}, f32[2,256,256]{2,1,0:T(8,128)S(1)}, u32[]{:S(2)}) copy-start(f32[2,256,256]{2,1,0:T(8,128)S(1)} %collective-permute-done.8.prev_diag_any) | copy-start | bytes 1572868
  55.9 26.0 %all-to-all-start = ((f32[64,16,128]{2,1,0:T(8,128)}), f32[64,16,128]{2,1,0:T(8,128)S(1)}, u32[]{:S(2)}, u32[]{:S(2)}) async-start(f32[64,16,128]{2,1,0:T(8,128)} %bitcast.8), calls=%async_computation | async-start | bytes 1048576 | tf_op jit(solution)/shard_map/all_to_all | solution.py:659
  67.6 0.8 copy-start.9
  67.6 0.9 copy-start.11
  71.6 32.5 %collective-permute-start.10 = (f32[2,256,256]{2,1,0:T(8,128)}, f32[2,256,256]{2,1,0:T(8,128)S(1)}, u32[]{:S(2)}, u32[]{:S(2)}) collective-permute-start(f32[2,256,256]{2,1,0:T(8,128)} %get-tuple-element.36.own_any), channel_id=1, source_target_pairs={{1,0},{2,1},{3,2},{4,3},{5,4},{6,5},{7,6},{8,7},{9,8},{10,9},{11,1... | collective-permute-start | bytes 1572872 | tf_op jit(solution)/shard_map/ppermute | solution.py:635
  74.0 30.1 %collective-permute-start.11 = (f32[2,256,256]{2,1,0:T(8,128)}, f32[2,256,256]{2,1,0:T(8,128)S(1)}, u32[]{:S(2)}, u32[]{:S(2)}) collective-permute-start(f32[2,256,256]{2,1,0:T(8,128)} %get-tuple-element.36.own_any), channel_id=1, source_target_pairs={{33,0},{34,1},{35,2},{36,3},{37,4},{38,5},{39,6},{40,7},{41,8},{42... | collective-permute-start | bytes 1572872 | tf_op jit(solution)/shard_map/ppermute | solution.py:646
  75.3 28.9 %collective-permute-start.9 = (f32[2,256,256]{2,1,0:T(8,128)}, f32[2,256,256]{2,1,0:T(8,128)S(1)}, u32[]{:S(2)}, u32[]{:S(2)}) collective-permute-start(f32[2,256,256]{2,1,0:T(8,128)} %get-tuple-element.36.own_any), channel_id=1, source_target_pairs={{32,0},{64,32},{96,64},{128,96},{160,128},{192,160},{224,192},{256... | collective-permute-start | bytes 1572872 | tf_op jit(solution)/shard_map/ppermute | solution.py:635
  82.0 0.8 copy-start
  85.2 31.3 %all-to-all-start.1 = ((f32[8,17,128]{2,1,0:T(8,128)}), f32[8,17,128]{2,1,0:T(8,128)S(1)}, u32[]{:S(2)}, u32[]{:S(2)}) async-start(f32[8,17,128]{2,1,0:T(8,128)} %payload.1), calls=%async_computation.1 | async-start | bytes 196608 | tf_op jit(solution)/shard_map/all_to_all | solution.py:659
  104.1 48.7 %copy-start.5 = (f32[2,256,256]{2,1,0:T(8,128)}, f32[2,256,256]{2,1,0:T(8,128)S(1)}, u32[]{:S(2)}) copy-start(f32[2,256,256]{2,1,0:T(8,128)S(1)} %collective-permute-done.10.right_any) | copy-start | bytes 1572868
  104.1 48.7 %copy-start.6 = (f32[2,256,256]{2,1,0:T(8,128)}, f32[2,256,256]{2,1,0:T(8,128)S(1)}, u32[]{:S(2)}) copy-start(f32[2,256,256]{2,1,0:T(8,128)S(1)} %collective-permute-done.11.diag_any) | copy-start | bytes 1572868
  104.2 48.6 %copy-start.7 = (f32[2,256,256]{2,1,0:T(8,128)}, f32[2,256,256]{2,1,0:T(8,128)S(1)}, u32[]{:S(2)}) copy-start(f32[2,256,256]{2,1,0:T(8,128)S(1)} %collective-permute-done.9.below_any) | copy-start | bytes 1572868
  117.6 35.2 %all-to-all-start.2 = ((f32[64,17,1,128]{3,2,1,0:T(1,128)}), f32[64,17,1,128]{3,2,1,0:T(1,128)S(1)}, u32[]{:S(2)}, u32[]{:S(2)}) async-start(f32[64,17,1,128]{3,2,1,0:T(1,128)} %broadcast_in_dim.8), calls=%async_computation.2 | async-start | bytes 1114112 | tf_op jit(solution)/shard_map/all_to_all | solution.py:659
  152.8 0.8 copy-start.1

commit v5 on v4

--- a/solution.py
+++ b/solution.py
@@ -11,8 +11,6 @@
 
 VMEM_BYTES = 60 * 1024 * 1024
 
-FOLD_FLOPS = 2 * 10**10
-
 
 def dft_blocks(width):
     at = np.arange(width)
@@ -25,16 +23,22 @@
         low = (table - high.astype(np.float32)).astype(jnp.bfloat16)
         return np.concatenate([high, low, high], axis=1)
 
-    real_rows = np.concatenate([thrice(cosine), thrice(sine)], axis=1)
-    imag_rows = np.concatenate([thrice(-sine), thrice(cosine)], axis=1)
-    left = np.concatenate([real_rows, imag_rows], axis=0)
-    return left, np.ascontiguousarray(left.T)
+    left = np.stack([thrice(cosine), thrice(cosine - sine), thrice(cosine + sine)])
+    return left, np.ascontiguousarray(left.transpose(0, 2, 1))
 
 
 def split_halves(value):
     high = value.astype(jnp.bfloat16)
     low = (value - high.astype(jnp.float32)).astype(jnp.bfloat16)
     return high, low
+
+
+def three_of(pair):
+    return (pair[0] + pair[1], pair[1], pair[0])
+
+
+def product(left, right):
+    return jnp.dot(left, right, preferred_element_type=jnp.float32)
 
 
 def dft_pairs(pairs, tables, scratch):
@@ -42,26 +46,24 @@
     tall_ref, wide_ref = scratch
     width = pairs[0][0].shape[0]
     for which, pair in enumerate(pairs):
-        for at, part in enumerate(pair):
+        for at, part in enumerate(three_of(pair)):
             high, low = split_halves(part)
-            base = 3 * at * width
-            tall_ref[which, base : base + width, :] = high
-            tall_ref[which, base + width : base + 2 * width, :] = high
-            tall_ref[which, base + 2 * width : base + 3 * width, :] = low
+            tall_ref[which, at, :width] = high
+            tall_ref[which, at, width : 2 * width] = high
+            tall_ref[which, at, 2 * width :] = low
     results = []
     left_ref = left_ref()
     for which in range(len(pairs)):
-        middle = jnp.dot(left_ref[...], tall_ref[which], preferred_element_type=jnp.float32)
-        for at in range(2):
-            high, low = split_halves(middle[at * width : (at + 1) * width])
-            base = 3 * at * width
-            wide_ref[which, :, base : base + width] = high
-            wide_ref[which, :, base + width : base + 2 * width] = high
-            wide_ref[which, :, base + 2 * width : base + 3 * width] = low
+        both, second, first = [product(left_ref[at], tall_ref[which, at]) for at in range(3)]
+        for at, part in enumerate(three_of((both - second, both - first))):
+            high, low = split_halves(part)
+            wide_ref[which, at, :, :width] = high
+            wide_ref[which, at, :, width : 2 * width] = high
+            wide_ref[which, at, :, 2 * width :] = low
     right_ref = right_ref()
     for which in range(len(pairs)):
-        done = jnp.dot(wide_ref[which], right_ref[...], preferred_element_type=jnp.float32)
-        results.append((done[:, :width], done[:, width:]))
+        both, second, first = [product(wide_ref[which, at], right_ref[at]) for at in range(3)]
+        results.append((both - second, both - first))
     return results
 
 
@@ -293,41 +295,6 @@
     return [(array.at[pl.ds(first, 2)], ref.at[pl.ds(first, 2)]) for first in (0, 2)]
 
 
-def fold_kernel(
-    own_any,
-    left_any,
-    above_any,
-    corner_any,
-    prev_any,
-    grad_any,
-    products_ref,
-    held_ref,
-    grad_ref,
-    in_sems,
-    out_sem,
-):
-    sources = [own_any, left_any, above_any, corner_any, prev_any]
-    targets = [held_ref.at[at] for at in range(5)]
-    own, left, above, diag, prev = incoming(sources, targets, in_sems)
-    grad_ref[...] = own()[...] + left()[...] + above()[...] + diag()[...]
-    copy = pltpu.make_async_copy(grad_ref, grad_any, out_sem)
-    copy.start()
-    square = jnp.sum(grad_ref[...] * grad_ref[...])
-    along = jnp.sum(grad_ref[...] * prev()[...])
-    lanes = lax.broadcasted_iota(jnp.int32, products_ref.shape, 1)
-    products_ref[...] = jnp.where(lanes == 0, square, jnp.where(lanes == 1, along, 0.0))
-    copy.wait()
-
-
-def payload_kernel(pieces_any, products_ref, payload_ref, pieces_ref, in_sem):
-    (pieces,) = incoming([pieces_any], [pieces_ref], in_sem)
-    piece = jnp.sum(pieces()[...], axis=0)
-    depth = piece.shape[0]
-    for at in range(payload_ref.shape[0]):
-        payload_ref[at, :depth] = piece
-        payload_ref[at, depth:] = products_ref[...]
-
-
 def curvature_kernel(
     positions_ref,
     counts_ref,
@@ -389,22 +356,21 @@
 
     total()
     depth = 4 * width // pieces
-    products = jnp.zeros((1, total_ref.shape[-1]), jnp.float32)
+    products = jnp.zeros((2, total_ref.shape[-1]), jnp.float32)
     for piece in range(pieces):
-        base = piece * (depth + 1)
+        base = piece * (depth + 2)
         part, rest = divmod(piece * depth, 2 * width)
         half, first = divmod(rest, width)
         lanes = slice(half * (width // 2), (half + 1) * (width // 2))
         change_ref[part, first : first + depth, lanes] = (
             total_ref[base : base + depth, :] * probe_scale
         )
-        products = products + total_ref[base + depth : base + depth + 1, :]
+        products = products + total_ref[base + depth : base + depth + 2, :]
     lane = lax.broadcasted_iota(jnp.int32, (1, 128), 1)
     probe_grad = change_ref[...]
     prev_probe()
-    grad_norm = jnp.sum(jnp.where(lane == 0, products, 0.0)) + jnp.sum(probe_grad * probe_grad)
-    along_prev = jnp.sum(jnp.where(lane == 1, products, 0.0))
-    along_prev = along_prev + jnp.sum(probe_grad * prev_probe_ref[...])
+    grad_norm = whole_sum(products[:1]) + whole_sum(probe_grad * probe_grad)
+    along_prev = whole_sum(products[1:]) + whole_sum(probe_grad * prev_probe_ref[...])
     ratio = grad_norm / prev_norm_ref[0]
     descent = grad_norm - ratio * along_prev
     change_ref[...] = ratio * prev_probe_ref[...] - change_ref[...]
@@ -421,7 +387,7 @@
     def finish(slots, quads):
         row = sums_ref[...]
         for slot, quad in zip(slots, quads):
-            square = jnp.sum(quad * quad)
+            square = whole_sum(quad * quad)
             row = row + jnp.where((lane == 0) | (lane == 1 + slot), square, 0.0)
         sums_ref[...] = row
 
@@ -461,7 +427,7 @@
     lane = lax.broadcasted_iota(jnp.int32, (1, 128), 1)
 
     def pick(row, at):
-        return jnp.sum(jnp.where(lane == at, row, 0.0))
+        return jnp.sum(jnp.where(lane == at, row, 0.0), axis=1, keepdims=True)
 
     curvature = pick(total, 0)
     step_size = pick(local, 6) / (0.5 * curvature + 1e-06)
@@ -471,14 +437,17 @@
         field, direction = [arrival() for arrival in arrivals[2 * which : 2 * which + 2]]
         field[...] = field[...] + step_size * direction[...]
         sent += outgoing([field], [outs[which]], out_sems, which)
-    norm_ref[0, 0] = pick(local, 5)
+    norm_ref[...] = pick(local, 5)
     pixels = held_ref.shape[-1] * held_ref.shape[-2]
-    for slot in range(frames_ref.shape[-1]):
-        frames_ref[0, 0, slot] = pick(local, 1 + slot) / pixels
+    frames_ref[0] = local[:, 1 : 1 + frames_ref.shape[-1]] / pixels
     for copy in sent:
         copy.wait()
 
 
+def whole_sum(value):
+    return jnp.sum(jnp.sum(value, axis=tuple(range(value.ndim - 1)))[None], axis=1, keepdims=True)
+
+
 def shaped(*dims):
     return jax.ShapeDtypeStruct(dims, jnp.float32)
 
@@ -509,15 +478,15 @@
 
 def table_buffers(width):
     return [
-        buffer(2 * width, 6 * width, dtype=jnp.bfloat16),
-        buffer(6 * width, 2 * width, dtype=jnp.bfloat16),
+        buffer(3, width, 3 * width, dtype=jnp.bfloat16),
+        buffer(3, 3 * width, width, dtype=jnp.bfloat16),
     ]
 
 
 def dft_scratch(width):
     return [
-        buffer(2, 6 * width, width, dtype=jnp.bfloat16),
-        buffer(2, width, 6 * width, dtype=jnp.bfloat16),
+        buffer(2, 3, 3 * width, width, dtype=jnp.bfloat16),
+        buffer(2, 3, width, 3 * width, dtype=jnp.bfloat16),
     ]
 
 
@@ -558,36 +527,6 @@
     )(positions, counts, *tiles, probe, measured, *tables)
 
 
-def fold_call(parts, prev):
-    shape = prev.shape
-    return pl.pallas_call(
-        fold_kernel,
-        out_shape=(shaped(*shape), shaped(1, 128)),
-        in_specs=anywhere(5),
-        out_specs=(*anywhere(1), *in_vmem(1)),
-        scratch_shapes=[
-            buffer(5, *shape),
-            buffer(*shape),
-            arrivals_of(5),
-            pltpu.SemaphoreType.DMA,
-        ],
-        name="fold",
-        **costing(FOLD_FLOPS),
-    )(*parts, prev)
-
-
-def payload_call(pieces, products, targets):
-    return pl.pallas_call(
-        payload_kernel,
-        out_shape=shaped(targets, pieces.shape[1] + 1, pieces.shape[2]),
-        in_specs=anywhere(1) + in_vmem(1),
-        out_specs=in_vmem(1)[0],
-        scratch_shapes=[buffer(*pieces.shape), arrivals_of(1)],
-        name="payload",
-        **costing(10**6),
-    )(pieces, products)
-
-
 def curvature_call(positions, counts, prev_norm, tiles, total, pieces, kept, tables, probe_prev, scale):
     width = tiles[0].shape[-1]
     slots = kept[0].shape[0]
@@ -622,7 +561,7 @@
         update_kernel,
         out_shape=(shaped(*shape),) * 2 + (shaped(1, 1), shaped(1, 1, slots)),
         in_specs=in_vmem(2) + in_hbm(4),
-        out_specs=(*in_hbm(2), *in_smem(2)),
+        out_specs=(*in_hbm(2), *in_vmem(2)),
         scratch_shapes=[buffer(4, *shape), arrivals_of(4), arrivals_of(2)],
         name="update",
         **costing(10**6),
@@ -706,10 +645,12 @@
     from_above = passed_along(below_grad, "row", 1)
     from_left = passed_along(right_grad, "col", 1)
     pieces = exchanged(probe_part.reshape((len(near[0]), -1, width // 2)), near)
-    object_grad, products = fold_call(
-        (own_grad, from_left, from_above, corner_part), object_dir_prev
-    )
-    payload = payload_call(pieces, products, len(apart[0]))
+    object_grad = own_grad + from_left + from_above + corner_part
+    sums = [
+        jnp.sum(jnp.sum(object_grad * other, axis=(0, 1)).reshape(2, -1), axis=0, keepdims=True)
+        for other in (object_grad, object_dir_prev)
+    ]
+    payload = copies(jnp.concatenate([jnp.sum(pieces, axis=0), *sums], axis=0), apart)
     grad_below = passed_along(object_grad, "row", -1)
     grad_right = passed_along(object_grad, "col", -1)
     grad_diag = passed_across(object_grad, -1)

time: 194 us -> 199 us (1.026)
  Pallas kernels: 35.2 us -> 28 us
  waiting for transfers between devices: 32.7 us -> 39.3 us
  blocking collectives: 24.4 us -> 28 us
  starting transfers between devices: 92.6 us -> 95.1 us
    ppermute x9, waiting for transfers between devices: 2.63 us -> 16 us  [passed_along(): return lax.ppermute(shard, axis, pairs)]
    all_to_all x3, waiting for transfers between devices: 30 us -> 23.3 us  [exchanged(): lax.all_to_all(pieces, ('row', 'col'), 0, 0, axis_index_groups=groups)]
    ppermute x9, starting transfers between devices: 31.8 us -> 38.5 us  [passed_along(): return lax.ppermute(shard, axis, pairs)]
    pallas_call x2 -> x0, Pallas kernels: 5.4 us -> none  [the longest x1 2.99 us: fold_call(): pl.pallas_call(fold_kernel, out_shape=(shaped(*shape), shaped(1, 128)), i...]
    all_to_all x2, blocking collectives: 24.4 us -> 28 us  [exchanged(): lax.all_to_all(pieces, ('row', 'col'), 0, 0, axis_index_groups=groups)]
    unnamed x27 -> x23, local copies, waits for them, and re-layouts: 4.69 us -> 2.18 us
    ppermute x3, starting transfers between devices: 8.21 us -> 5.82 us  [passed_across(): return lax.ppermute(shard, ('row', 'col'), pairs)]
  transfers between devices with their start and end apart: 15 -> 15, of which waited for: 5 -> 8; matrix products, arithmetic and copies ran while one was open for 1% -> 2% of each run, Pallas kernels for 11% -> 7%
where the time goes in v5:
time: 199 us; the launch traced here: 198 us
  starting transfers between devices  95.1 us (48%)
  waiting for transfers between devices  39.3 us (20%)
  Pallas kernels  28 us (14%)
  blocking collectives  28 us (14%)
  local copies, waits for them, and re-layouts  4.58 us (2%)
    all_to_all x3, starting transfers between devices, exchanged(): lax.all_to_all(pieces, ('row', 'col'), 0, 0, axis_index_groups=groups)  50.8 us
    ppermute x9, starting transfers between devices, passed_along(): return lax.ppermute(shard, axis, pairs)  38.5 us
    all_to_all x2, blocking collectives, exchanged(): lax.all_to_all(pieces, ('row', 'col'), 0, 0, axis_index_groups=groups)  28 us
    all_to_all x3, waiting for transfers between devices, exchanged(): lax.all_to_all(pieces, ('row', 'col'), 0, 0, axis_index_groups=groups)  23.3 us
    ppermute x9, waiting for transfers between devices, passed_along(): return lax.ppermute(shard, axis, pairs)  16 us
    pallas_call x1, Pallas kernels, gradient_call(): pl.pallas_call(gradient_kernel, out_shape=(shaped(2, width, width),) * 4...  14.6 us
    pallas_call x1, Pallas kernels, curvature_call(): pl.pallas_call(functools.partial(curvature_kernel, probe_scale=scale, pie...  9.76 us
    ppermute x3, starting transfers between devices, passed_across(): return lax.ppermute(shard, ('row', 'col'), pairs)  5.82 us
  transfers between devices with their start and end apart: 15, of which 8 were waited for; matrix products, arithmetic and copies ran while one was open for 2% of the time, Pallas kernels for 7%

profile of v5, /device:TPU:1, one launch (start us, length us, event | category | flops | bytes accessed | tf_op | source)
XLA Modules:
  0.0 198.0 jit_solution(15886676696276728310)
XLA Ops:
  0.6 1.3 collective-permute-start
  1.9 8.8 %collective-permute-start.1 = (f32[2,256,256]{2,1,0:T(8,128)}, f32[2,256,256]{2,1,0:T(8,128)S(1)}, u32[]{:S(2)}, u32[]{:S(2)}) collective-permute-start(f32[2,256,256]{2,1,0:T(8,128)} %object_any.1), channel_id=1, source_target_pairs={{1,0},{2,1},{3,2},{4,3},{5,4},{6,5},{7,6},{8,7},{9,8},{10,9},{11,1... | collective-permute-start | bytes 1572872 | tf_op jit(solution)/shard_map/ppermute | solution.py:574
  10.7 0.7 collective-permute-done.below_any
  11.4 9.3 %collective-permute-start.2 = (f32[2,256,256]{2,1,0:T(8,128)S(1)}, f32[2,256,256]{2,1,0:T(8,128)}, u32[]{:S(2)}, u32[]{:S(2)}) collective-permute-start(f32[2,256,256]{2,1,0:T(8,128)S(1)} %collective-permute-done.below_any), channel_id=1, source_target_pairs={{1,0},{2,1},{3,2},{4,3},{5,4},{6,5},{7,6},{8,7},{9,8},{10,9},{11,1... | collective-permute-start | bytes 1572872 | tf_op jit(solution)/shard_map/ppermute | solution.py:574
  20.7 1.3 copy.25.positions_ref
  22.0 1.4 collective-permute-start.6
  23.5 1.9 collective-permute-start.7
  25.4 1.3 collective-permute-start.8
  26.7 1.8 collective-permute-done.2.diag_any
  28.5 14.6 %gradient_frames.1 = (f32[2,256,256]{2,1,0:T(8,128)}, f32[2,256,256]{2,1,0:T(8,128)}, f32[2,256,256]{2,1,0:T(8,128)}, f32[2,256,256]{2,1,0:T(8,128)}, f32[1024,1...) custom-call(s32[1,1,4,2]{3,2,1,0:T(4,128)} %copy.25.positions_ref, ...), custom_call_target="tpu_custom_call" | custom-call | flops 10000000000 | bytes 10000000 | tf_op jit(solution)/shard_map/gradient_frames/pallas_call | solution.py:504
  43.5 18.3 %all-to-all-start = ((f32[64,16,128]{2,1,0:T(8,128)}), f32[64,16,128]{2,1,0:T(8,128)S(1)}, u32[]{:S(2)}, u32[]{:S(2)}) async-start(f32[64,16,128]{2,1,0:T(8,128)} %bitcast.14), calls=%async_computation | async-start | bytes 1048576 | tf_op jit(solution)/shard_map/all_to_all | solution.py:598
  61.8 3.5 %collective-permute-start.3 = (f32[2,256,256]{2,1,0:T(8,128)}, f32[2,256,256]{2,1,0:T(8,128)S(1)}, u32[]{:S(2)}, u32[]{:S(2)}) collective-permute-start(f32[2,256,256]{2,1,0:T(8,128)} %get-tuple-element.31), channel_id=1, source_target_pairs={{0,1},{1,2},{2,3},{3,4},{4,5},{5,6},{6,7},{7,8},{8,9},{9,10},{10,1... | collective-permute-start | bytes 1572872 | tf_op jit(solution)/shard_map/ppermute | solution.py:574
  65.4 3.1 %collective-permute-start.4 = (f32[2,256,256]{2,1,0:T(8,128)}, f32[2,256,256]{2,1,0:T(8,128)S(1)}, u32[]{:S(2)}, u32[]{:S(2)}) collective-permute-start(f32[2,256,256]{2,1,0:T(8,128)} %get-tuple-element.32), channel_id=1, source_target_pairs={{0,32},{32,64},{64,96},{96,128},{128,160},{160,192},{192,224},{224... | collective-permute-start | bytes 1572872 | tf_op jit(solution)/shard_map/ppermute | solution.py:574
  68.5 3.2 %collective-permute-start.5 = (f32[2,256,256]{2,1,0:T(8,128)}, f32[2,256,256]{2,1,0:T(8,128)S(1)}, u32[]{:S(2)}, u32[]{:S(2)}) collective-permute-start(f32[2,256,256]{2,1,0:T(8,128)} %get-tuple-element.33), channel_id=1, source_target_pairs={{0,33},{1,34},{2,35},{3,36},{4,37},{5,38},{6,39},{7,40},{8,41},{9,... | collective-permute-start | bytes 1572872 | tf_op jit(solution)/shard_map/ppermute | solution.py:585
  71.8 1.8 collective-permute-done.3
  73.5 7.5 %collective-permute-done.4 = f32[2,256,256]{2,1,0:T(8,128)S(1)} collective-permute-done((f32[2,256,256]{2,1,0:T(8,128)}, f32[2,256,256]{2,1,0:T(8,128)S(1)}, u32[]{:S(2)}, u32[]{:S(2)}) %collective-permute-start.4) | collective-permute-done | bytes 524320 | tf_op jit(solution)/shard_map/ppermute | solution.py:574
  81.0 1.3 multiply_reduce_fusion.1
  82.3 7.9 %collective-permute-start.10 = (f32[2,256,256]{2,1,0:T(8,128)S(1)}, f32[2,256,256]{2,1,0:T(8,128)S(1)}, u32[]{:S(2)}, u32[]{:S(2)}) collective-permute-start(f32[2,256,256]{2,1,0:T(8,128)S(1)} %get-tuple-element.56.own_any), channel_id=1, source_target_pairs={{1,0},{2,1},{3,2},{4,3},{5,4},{6,5},{7,6},{8,7},{9,8},{10,9},{11,1... | collective-permute-start | bytes 1572872 | tf_op jit(solution)/shard_map/ppermute | solution.py:574
  90.2 1.3 collective-permute-start.11
  91.5 1.3 collective-permute-start.9
  92.9 0.6 broadcast_in_dim.16
  93.6 19.5 %all-to-all-start.1 = ((f32[8,18,128]{2,1,0:T(8,128)}), f32[8,18,128]{2,1,0:T(8,128)S(1)}, u32[]{:S(2)}, u32[]{:S(2)}) async-start(f32[8,18,128]{2,1,0:T(8,128)} %broadcast_in_dim.16), calls=%async_computation.1 | async-start | bytes 196608 | tf_op jit(solution)/shard_map/all_to_all | solution.py:598
  113.2 3.8 %collective-permute-done.9.below_any = f32[2,256,256]{2,1,0:T(8,128)S(1)} collective-permute-done((f32[2,256,256]{2,1,0:T(8,128)S(1)}, f32[2,256,256]{2,1,0:T(8,128)S(1)}, u32[]{:S(2)}, u32[]{:S(2)}) %collective-permute-start.9) | collective-permute-done | bytes 524320 | tf_op jit(solution)/shard_map/ppermute | solution.py:574
  117.0 10.5 %all-to-all-done.1 = f32[8,18,128]{2,1,0:T(8,128)S(1)} async-done(((f32[8,18,128]{2,1,0:T(8,128)}), f32[8,18,128]{2,1,0:T(8,128)S(1)}, u32[]{:S(2)}, u32[]{:S(2)}) %all-to-all-start.1) | async-done | bytes 73760 | tf_op jit(solution)/shard_map/all_to_all | solution.py:598
  127.4 1.1 broadcast_in_dim.34
  128.6 12.9 %all-to-all-start.2 = ((f32[64,18,1,128]{3,2,1,0:T(1,128)}), f32[64,18,1,128]{3,2,1,0:T(1,128)S(1)}, u32[]{:S(2)}, u32[]{:S(2)}) async-start(f32[64,18,1,128]{3,2,1,0:T(1,128)} %broadcast_in_dim.34), calls=%async_computation.2 | async-start | bytes 1179648 | tf_op jit(solution)/shard_map/all_to_all | solution.py:598
  142.2 12.8 %all-to-all-done.2 = f32[64,18,1,128]{3,2,1,0:T(1,128)S(1)} async-done(((f32[64,18,1,128]{3,2,1,0:T(1,128)}), f32[64,18,1,128]{3,2,1,0:T(1,128)S(1)}, u32[]{:S(2)}, u32[]{:S(2)}) %all-to-all-start.2) | async-done | bytes 589856 | tf_op jit(solution)/shard_map/all_to_all | solution.py:598
  155.0 0.8 copy-done
  155.8 9.8 %curvature_frames.1 = (f32[2,256,256]{2,1,0:T(8,128)}, f32[2,256,256]{2,1,0:T(8,128)}, f32[1,128]{1,0:T(1,128)}) custom-call(s32[1,1,4,2]{3,2,1,0:T(4,128)} %copy.25.positions_ref, s32[1,32]{1,0:T(1,128)} %counts_ref.3, f32[1]{0:T(128)} %bitcast.12.prev_norm_ref, f32[2,256,256]{2,1,0:T(8,128)} %copy-done.2, f32[2,256,256]{2,1,0:T(8,128)} %copy-done.8, ...), custom_call_target="tpu_custom_call" | custom-call | flops 5000000000 | bytes 10000000 | tf_op jit(solution)/shard_map/curvature_frames/pallas_call | solution.py:534
  166.2 9.7 %all_to_all.25 = f32[32,1,128]{2,1,0:T(1,128)S(1)} all-to-all(f32[32,1,128]{2,1,0:T(1,128)S(1)} %broadcast_in_dim.36), channel_id=1, replica_groups={{0,1,32,33,64,65,96,97,128,129,160,161,192,193,224,225,256,257,288,289,..., dimensions={0} | all-to-all | bytes 32768 | tf_op jit(solution)/shard_map/all_to_all | solution.py:598
  175.9 18.3 %all_to_all.26.gathered_ref = f32[16,1,128]{2,1,0:T(1,128)} all-to-all(f32[16,1,128]{2,1,0:T(1,128)S(1)} %broadcast_in_dim.37), channel_id=1, replica_groups={{0,2,4,6,8,10,12,14,16,18,20,22,24,26,28,30},{1,3,5,7,9,11,13,15,17,19,..., dimensions={0} | all-to-all | bytes 16384 | tf_op jit(solution)/shard_map/all_to_all | solution.py:598
  194.2 3.6 %update.1 = (f32[2,256,256]{2,1,0:T(8,128)}, f32[2,256,256]{2,1,0:T(8,128)}, f32[1,1]{1,0:T(1,128)}, f32[1,1,4]{2,1,0:T(1,128)}) custom-call(f32[16,1,128]{2,1,0:T(1,128)} %all_to_all.26.gathered_ref, f32[1,128]{1,0:T(1,128)} %get-tuple-element.47.sums_ref, f32[2,256,256]{2,1,0:T(8,128)} %object_any.1, f32[2,256,256]{2,1,0:T(8,128)} %get-tuple-element.26.direction_any, ...), custom_call_target="tpu_custom_call" | custom-call | flops 1000000 | bytes 10000000 | tf_op jit(solution)/shard_map/update/pallas_call | solution.py:560
  (36 shorter events, 1.2 us)
Async XLA Ops:
  0.6 10.8 %collective-permute-start = (f32[2,256,256]{2,1,0:T(8,128)}, f32[2,256,256]{2,1,0:T(8,128)S(1)}, u32[]{:S(2)}, u32[]{:S(2)}) collective-permute-start(f32[2,256,256]{2,1,0:T(8,128)} %object_any.1), channel_id=1, source_target_pairs={{32,0},{64,32},{96,64},{128,96},{160,128},{192,160},{224,192},{256... | collective-permute-start | bytes 1572872 | tf_op jit(solution)/shard_map/ppermute | solution.py:574
  1.9 24.8 %collective-permute-start.1 = (f32[2,256,256]{2,1,0:T(8,128)}, f32[2,256,256]{2,1,0:T(8,128)S(1)}, u32[]{:S(2)}, u32[]{:S(2)}) collective-permute-start(f32[2,256,256]{2,1,0:T(8,128)} %object_any.1), channel_id=1, source_target_pairs={{1,0},{2,1},{3,2},{4,3},{5,4},{6,5},{7,6},{8,7},{9,8},{10,9},{11,1... | collective-permute-start | bytes 1572872 | tf_op jit(solution)/shard_map/ppermute | solution.py:574
  11.4 17.0 %copy-start.9 = (f32[2,256,256]{2,1,0:T(8,128)}, f32[2,256,256]{2,1,0:T(8,128)S(1)}, u32[]{:S(2)}) copy-start(f32[2,256,256]{2,1,0:T(8,128)S(1)} %collective-permute-done.below_any) | copy-start | bytes 1572868
  11.4 17.0 %collective-permute-start.2 = (f32[2,256,256]{2,1,0:T(8,128)S(1)}, f32[2,256,256]{2,1,0:T(8,128)}, u32[]{:S(2)}, u32[]{:S(2)}) collective-permute-start(f32[2,256,256]{2,1,0:T(8,128)S(1)} %collective-permute-done.below_any), channel_id=1, source_target_pairs={{1,0},{2,1},{3,2},{4,3},{5,4},{6,5},{7,6},{8,7},{9,8},{10,9},{11,1... | collective-permute-start | bytes 1572872 | tf_op jit(solution)/shard_map/ppermute | solution.py:574
  22.0 59.0 %copy-start.1 = (f32[2,256,256]{2,1,0:T(8,128)S(1)}, f32[2,256,256]{2,1,0:T(8,128)}, u32[]{:S(2)}) copy-start(f32[2,256,256]{2,1,0:T(8,128)} %prev_own_any.1) | copy-start | bytes 1572868
  22.0 21.5 %collective-permute-start.6 = (f32[2,256,256]{2,1,0:T(8,128)}, f32[2,256,256]{2,1,0:T(8,128)S(1)}, u32[]{:S(2)}, u32[]{:S(2)}) collective-permute-start(f32[2,256,256]{2,1,0:T(8,128)} %prev_own_any.1), channel_id=1, source_target_pairs={{32,0},{64,32},{96,64},{128,96},{160,128},{192,160},{224,192},{256... | collective-permute-start | bytes 1572872 | tf_op jit(solution)/shard_map/ppermute | solution.py:574
  23.5 20.1 %collective-permute-start.7 = (f32[2,256,256]{2,1,0:T(8,128)}, f32[2,256,256]{2,1,0:T(8,128)S(1)}, u32[]{:S(2)}, u32[]{:S(2)}) collective-permute-start(f32[2,256,256]{2,1,0:T(8,128)} %prev_own_any.1), channel_id=1, source_target_pairs={{1,0},{2,1},{3,2},{4,3},{5,4},{6,5},{7,6},{8,7},{9,8},{10,9},{11,1... | collective-permute-start | bytes 1572872 | tf_op jit(solution)/shard_map/ppermute | solution.py:574
  25.4 18.1 %collective-permute-start.8 = (f32[2,256,256]{2,1,0:T(8,128)}, f32[2,256,256]{2,1,0:T(8,128)S(1)}, u32[]{:S(2)}, u32[]{:S(2)}) collective-permute-start(f32[2,256,256]{2,1,0:T(8,128)} %prev_own_any.1), channel_id=1, source_target_pairs={{33,0},{34,1},{35,2},{36,3},{37,4},{38,5},{39,6},{40,7},{41,8},{42... | collective-permute-start | bytes 1572872 | tf_op jit(solution)/shard_map/ppermute | solution.py:585
  26.7 1.8 copy-start.10
  43.5 38.8 %copy-start.3 = (f32[2,256,256]{2,1,0:T(8,128)}, f32[2,256,256]{2,1,0:T(8,128)S(1)}, u32[]{:S(2)}) copy-start(f32[2,256,256]{2,1,0:T(8,128)S(1)} %collective-permute-done.6.prev_below_any) | copy-start | bytes 1572868
  43.5 38.8 %copy-start.4 = (f32[2,256,256]{2,1,0:T(8,128)}, f32[2,256,256]{2,1,0:T(8,128)S(1)}, u32[]{:S(2)}) copy-start(f32[2,256,256]{2,1,0:T(8,128)S(1)} %collective-permute-done.7.prev_right_any) | copy-start | bytes 1572868
  43.5 38.8 %copy-start.5 = (f32[2,256,256]{2,1,0:T(8,128)}, f32[2,256,256]{2,1,0:T(8,128)S(1)}, u32[]{:S(2)}) copy-start(f32[2,256,256]{2,1,0:T(8,128)S(1)} %collective-permute-done.8.prev_diag_any) | copy-start | bytes 1572868
  43.5 49.3 %all-to-all-start = ((f32[64,16,128]{2,1,0:T(8,128)}), f32[64,16,128]{2,1,0:T(8,128)S(1)}, u32[]{:S(2)}, u32[]{:S(2)}) async-start(f32[64,16,128]{2,1,0:T(8,128)} %bitcast.14), calls=%async_computation | async-start | bytes 1048576 | tf_op jit(solution)/shard_map/all_to_all | solution.py:598
  61.8 11.7 %collective-permute-start.3 = (f32[2,256,256]{2,1,0:T(8,128)}, f32[2,256,256]{2,1,0:T(8,128)S(1)}, u32[]{:S(2)}, u32[]{:S(2)}) collective-permute-start(f32[2,256,256]{2,1,0:T(8,128)} %get-tuple-element.31), channel_id=1, source_target_pairs={{0,1},{1,2},{2,3},{3,4},{4,5},{5,6},{6,7},{7,8},{8,9},{9,10},{10,1... | collective-permute-start | bytes 1572872 | tf_op jit(solution)/shard_map/ppermute | solution.py:574
  65.4 15.6 %collective-permute-start.4 = (f32[2,256,256]{2,1,0:T(8,128)}, f32[2,256,256]{2,1,0:T(8,128)S(1)}, u32[]{:S(2)}, u32[]{:S(2)}) collective-permute-start(f32[2,256,256]{2,1,0:T(8,128)} %get-tuple-element.32), channel_id=1, source_target_pairs={{0,32},{32,64},{64,96},{96,128},{128,160},{160,192},{192,224},{224... | collective-permute-start | bytes 1572872 | tf_op jit(solution)/shard_map/ppermute | solution.py:574
  68.5 12.5 %collective-permute-start.5 = (f32[2,256,256]{2,1,0:T(8,128)}, f32[2,256,256]{2,1,0:T(8,128)S(1)}, u32[]{:S(2)}, u32[]{:S(2)}) collective-permute-start(f32[2,256,256]{2,1,0:T(8,128)} %get-tuple-element.33), channel_id=1, source_target_pairs={{0,33},{1,34},{2,35},{3,36},{4,37},{5,38},{6,39},{7,40},{8,41},{9,... | collective-permute-start | bytes 1572872 | tf_op jit(solution)/shard_map/ppermute | solution.py:585
  82.3 72.7 %copy-start.2 = (f32[2,256,256]{2,1,0:T(8,128)}, f32[2,256,256]{2,1,0:T(8,128)S(1)}, u32[]{:S(2)}) copy-start(f32[2,256,256]{2,1,0:T(8,128)S(1)} %get-tuple-element.56.own_any) | copy-start | bytes 1572868
  82.3 30.8 %collective-permute-start.10 = (f32[2,256,256]{2,1,0:T(8,128)S(1)}, f32[2,256,256]{2,1,0:T(8,128)S(1)}, u32[]{:S(2)}, u32[]{:S(2)}) collective-permute-start(f32[2,256,256]{2,1,0:T(8,128)S(1)} %get-tuple-element.56.own_any), channel_id=1, source_target_pairs={{1,0},{2,1},{3,2},{4,3},{5,4},{6,5},{7,6},{8,7},{9,8},{10,9},{11,1... | collective-permute-start | bytes 1572872 | tf_op jit(solution)/shard_map/ppermute | solution.py:574
  90.2 22.9 %collective-permute-start.11 = (f32[2,256,256]{2,1,0:T(8,128)S(1)}, f32[2,256,256]{2,1,0:T(8,128)S(1)}, u32[]{:S(2)}, u32[]{:S(2)}) collective-permute-start(f32[2,256,256]{2,1,0:T(8,128)S(1)} %get-tuple-element.56.own_any), channel_id=1, source_target_pairs={{33,0},{34,1},{35,2},{36,3},{37,4},{38,5},{39,6},{40,7},{41,8},{42... | collective-permute-start | bytes 1572872 | tf_op jit(solution)/shard_map/ppermute | solution.py:585
  91.5 25.4 %collective-permute-start.9 = (f32[2,256,256]{2,1,0:T(8,128)S(1)}, f32[2,256,256]{2,1,0:T(8,128)S(1)}, u32[]{:S(2)}, u32[]{:S(2)}) collective-permute-start(f32[2,256,256]{2,1,0:T(8,128)S(1)} %get-tuple-element.56.own_any), channel_id=1, source_target_pairs={{32,0},{64,32},{96,64},{128,96},{160,128},{192,160},{224,192},{256... | collective-permute-start | bytes 1572872 | tf_op jit(solution)/shard_map/ppermute | solution.py:574
  93.6 33.8 %all-to-all-start.1 = ((f32[8,18,128]{2,1,0:T(8,128)}), f32[8,18,128]{2,1,0:T(8,128)S(1)}, u32[]{:S(2)}, u32[]{:S(2)}) async-start(f32[8,18,128]{2,1,0:T(8,128)} %broadcast_in_dim.16), calls=%async_computation.1 | async-start | bytes 196608 | tf_op jit(solution)/shard_map/all_to_all | solution.py:598
  113.1 41.9 %copy-start.6 = (f32[2,256,256]{2,1,0:T(8,128)}, f32[2,256,256]{2,1,0:T(8,128)S(1)}, u32[]{:S(2)}) copy-start(f32[2,256,256]{2,1,0:T(8,128)S(1)} %collective-permute-done.10.right_any) | copy-start | bytes 1572868
  113.1 41.9 %copy-start.7 = (f32[2,256,256]{2,1,0:T(8,128)}, f32[2,256,256]{2,1,0:T(8,128)S(1)}, u32[]{:S(2)}) copy-start(f32[2,256,256]{2,1,0:T(8,128)S(1)} %collective-permute-done.11.diag_any) | copy-start | bytes 1572868
  117.0 38.0 %copy-start.8 = (f32[2,256,256]{2,1,0:T(8,128)}, f32[2,256,256]{2,1,0:T(8,128)S(1)}, u32[]{:S(2)}) copy-start(f32[2,256,256]{2,1,0:T(8,128)S(1)} %collective-permute-done.9.below_any) | copy-start | bytes 1572868
  128.6 26.4 %all-to-all-start.2 = ((f32[64,18,1,128]{3,2,1,0:T(1,128)}), f32[64,18,1,128]{3,2,1,0:T(1,128)S(1)}, u32[]{:S(2)}, u32[]{:S(2)}) async-start(f32[64,18,1,128]{3,2,1,0:T(1,128)} %broadcast_in_dim.34), calls=%async_computation.2 | async-start | bytes 1179648 | tf_op jit(solution)/shard_map/all_to_all | solution.py:598
  155.0 0.8 copy-start

commit v6 on v5

--- a/solution.py
+++ b/solution.py
@@ -295,6 +295,19 @@
     return [(array.at[pl.ds(first, 2)], ref.at[pl.ds(first, 2)]) for first in (0, 2)]
 
 
+def joined_kernel(*refs):
+    *sources, out_any, held_ref, in_sems, out_sem = refs
+    count = len(sources)
+    arrivals = incoming(sources, [held_ref.at[at] for at in range(count)], in_sems)
+    for arrival in arrivals:
+        arrival()
+    if count > 1:
+        held_ref[0] = sum((held_ref[at] for at in range(1, count)), held_ref[0])
+    copy = pltpu.make_async_copy(held_ref.at[0], out_any, out_sem)
+    copy.start()
+    copy.wait()
+
+
 def curvature_kernel(
     positions_ref,
     counts_ref,
@@ -406,8 +419,8 @@
 
 
 def update_kernel(
-    gathered_ref,
-    sums_ref,
+    gathered_any,
+    sums_any,
     object_any,
     direction_any,
     probe_any,
@@ -416,14 +429,17 @@
     probe_new_any,
     norm_ref,
     frames_ref,
+    gathered_ref,
+    sums_ref,
     held_ref,
     in_sems,
     out_sems,
 ):
-    sources = [object_any, direction_any, probe_any, probe_direction_any]
-    arrivals = incoming(sources, [held_ref.at[at] for at in range(4)], in_sems)
-    total = jnp.sum(gathered_ref[...], axis=0)
-    local = sums_ref[...]
+    sources = [gathered_any, sums_any, object_any, direction_any, probe_any, probe_direction_any]
+    targets = [gathered_ref, sums_ref] + [held_ref.at[at] for at in range(4)]
+    gathered, sums, *arrivals = incoming(sources, targets, in_sems)
+    total = jnp.sum(gathered()[...], axis=0)
+    local = sums()[...]
     lane = lax.broadcasted_iota(jnp.int32, (1, 128), 1)
 
     def pick(row, at):
@@ -527,6 +543,23 @@
     )(positions, counts, *tiles, probe, measured, *tables)
 
 
+def joined_call(arrays, flops):
+    shape = arrays[0].shape
+    return pl.pallas_call(
+        joined_kernel,
+        out_shape=shaped(*shape),
+        in_specs=anywhere(len(arrays)),
+        out_specs=anywhere(1)[0],
+        scratch_shapes=[
+            buffer(len(arrays), *shape),
+            arrivals_of(len(arrays)),
+            pltpu.SemaphoreType.DMA,
+        ],
+        name="joined",
+        **costing(flops),
+    )(*arrays)
+
+
 def curvature_call(positions, counts, prev_norm, tiles, total, pieces, kept, tables, probe_prev, scale):
     width = tiles[0].shape[-1]
     slots = kept[0].shape[0]
@@ -560,9 +593,15 @@
     return pl.pallas_call(
         update_kernel,
         out_shape=(shaped(*shape),) * 2 + (shaped(1, 1), shaped(1, 1, slots)),
-        in_specs=in_vmem(2) + in_hbm(4),
+        in_specs=anywhere(2) + in_hbm(4),
         out_specs=(*in_hbm(2), *in_vmem(2)),
-        scratch_shapes=[buffer(4, *shape), arrivals_of(4), arrivals_of(2)],
+        scratch_shapes=[
+            buffer(*gathered.shape),
+            buffer(*sums.shape),
+            buffer(4, *shape),
+            arrivals_of(6),
+            arrivals_of(2),
+        ],
         name="update",
         **costing(10**6),
     )(gathered, sums, *arrays)
@@ -572,17 +611,6 @@
     count = lax.axis_size(axis)
     pairs = [(i, i + by) for i in range(count) if 0 <= i + by < count]
     return lax.ppermute(shard, axis, pairs)
-
-
-def passed_across(shard, by):
-    rows, cols = lax.axis_size("row"), lax.axis_size("col")
-    pairs = [
-        (row * cols + col, (row + by) * cols + col + by)
-        for row in range(rows)
-        for col in range(cols)
-        if 0 <= row + by < rows and 0 <= col + by < cols
-    ]
-    return lax.ppermute(shard, ("row", "col"), pairs)
 
 
 def device_groups(block):
@@ -628,7 +656,6 @@
     prev = held(object_dir_prev, below)
     prev_below = passed_along(prev, "row", -1)
     prev_right = passed_along(prev, "col", -1)
-    prev_diag = passed_across(prev, -1)
 
     own_grad, below_grad, right_grad, diag_grad, probe_part, *kept = gradient_call(
         positions,
@@ -638,14 +665,16 @@
         intensities,
         tables,
     )
-    probe_part, prev_below, prev_right, prev_diag = lax.optimization_barrier(
-        (probe_part, prev_below, prev_right, prev_diag)
-    )
-    corner_part = passed_across(diag_grad, 1)
-    from_above = passed_along(below_grad, "row", 1)
+    probe_part, prev_below, prev_right = lax.optimization_barrier(
+        (probe_part, prev_below, prev_right)
+    )
+    from_left_corner = passed_along(diag_grad, "col", 1)
+    pieces = exchanged(probe_part.reshape((len(near[0]), -1, width // 2)), near)
+    from_above = passed_along(joined_call((below_grad, from_left_corner), 10**10), "row", 1)
     from_left = passed_along(right_grad, "col", 1)
-    pieces = exchanged(probe_part.reshape((len(near[0]), -1, width // 2)), near)
-    object_grad = own_grad + from_left + from_above + corner_part
+    prev_diag = passed_along(held(prev_below, diag_grad), "col", -1)
+    from_above = held(from_above, prev_diag)
+    object_grad = own_grad + from_left + from_above
     sums = [
         jnp.sum(jnp.sum(object_grad * other, axis=(0, 1)).reshape(2, -1), axis=0, keepdims=True)
         for other in (object_grad, object_dir_prev)
@@ -653,10 +682,11 @@
     payload = copies(jnp.concatenate([jnp.sum(pieces, axis=0), *sums], axis=0), apart)
     grad_below = passed_along(object_grad, "row", -1)
     grad_right = passed_along(object_grad, "col", -1)
-    grad_diag = passed_across(object_grad, -1)
-    payload, grad_below, grad_right, grad_diag = lax.optimization_barrier(
-        (exchanged(payload, apart), grad_below, grad_right, grad_diag)
-    )
+    payload, grad_below, grad_right = lax.optimization_barrier(
+        (exchanged(payload, apart), grad_below, grad_right)
+    )
+    grad_diag = passed_along(grad_below, "col", -1)
+    grad_diag = joined_call((grad_diag,), 2 * 10**10)
     payload = jnp.sum(payload, axis=0)[:, None, :]
     total = exchanged(copies(payload, near), near)
     object_direction, probe_direction, sums = curvature_call(

time: 199 us -> 178 us (0.89)
  starting transfers between devices: 95.1 us -> 77.1 us
  waiting for transfers between devices: 39.3 us -> 35.2 us
  blocking collectives: 28 us -> 24.3 us
  Pallas kernels: 28 us -> 31.4 us
  local copies, waits for them, and re-layouts: 4.58 us -> 6.92 us
    all_to_all x3, starting transfers between devices: 50.8 us -> 36.5 us  [exchanged(): lax.all_to_all(pieces, ('row', 'col'), 0, 0, axis_index_groups=groups)]
    ppermute x3 -> x0, starting transfers between devices: 5.82 us -> none  [passed_across(): return lax.ppermute(shard, ('row', 'col'), pairs)]
    pallas_call x0 -> x2, Pallas kernels: none -> 4.06 us  [joined_call(): pl.pallas_call(joined_kernel, out_shape=shaped(*shape), in_specs=anywhere...]
    all_to_all x2, blocking collectives: 28 us -> 24.3 us  [exchanged(): lax.all_to_all(pieces, ('row', 'col'), 0, 0, axis_index_groups=groups)]
    ppermute x9 -> x12, waiting for transfers between devices: 16 us -> 12.3 us  [passed_along(): return lax.ppermute(shard, axis, pairs)]
    unnamed x23 -> x31, local copies, waits for them, and re-layouts: 2.18 us -> 4.53 us
    ppermute x9 -> x12, starting transfers between devices: 38.5 us -> 40.6 us  [passed_along(): return lax.ppermute(shard, axis, pairs)]
  transfers between devices with their start and end apart: 15 -> 15, of which waited for: 8 -> 6; matrix products, arithmetic and copies ran while one was open for 2% -> 2% of each run, Pallas kernels for 7% -> 11%
where the time goes in v6:
time: 178 us; the launch traced here: 177 us
  starting transfers between devices  77.1 us (43%)
  waiting for transfers between devices  35.2 us (20%)
  Pallas kernels  31.4 us (18%)
  blocking collectives  24.3 us (14%)
  local copies, waits for them, and re-layouts  6.92 us (4%)
  between operations  1.79 us (1%)
    ppermute x12, starting transfers between devices, passed_along(): return lax.ppermute(shard, axis, pairs)  40.6 us
    all_to_all x3, starting transfers between devices, exchanged(): lax.all_to_all(pieces, ('row', 'col'), 0, 0, axis_index_groups=groups)  36.5 us
    all_to_all x2, blocking collectives, exchanged(): lax.all_to_all(pieces, ('row', 'col'), 0, 0, axis_index_groups=groups)  24.3 us
    all_to_all x3, waiting for transfers between devices, exchanged(): lax.all_to_all(pieces, ('row', 'col'), 0, 0, axis_index_groups=groups)  22.9 us
    pallas_call x1, Pallas kernels, gradient_call(): pl.pallas_call(gradient_kernel, out_shape=(shaped(2, width, width),) * 4...  14.6 us
    ppermute x12, waiting for transfers between devices, passed_along(): return lax.ppermute(shard, axis, pairs)  12.3 us
    pallas_call x1, Pallas kernels, curvature_call(): pl.pallas_call(functools.partial(curvature_kernel, probe_scale=scale, pie...  9.76 us
    unnamed x31, local copies, waits for them, and re-layouts  4.53 us
  transfers between devices with their start and end apart: 15, of which 6 were waited for; matrix products, arithmetic and copies ran while one was open for 2% of the time, Pallas kernels for 11%

profile of v6, /device:TPU:1, one launch (start us, length us, event | category | flops | bytes accessed | tf_op | source)
XLA Modules:
  0.0 177.0 jit_solution(7114865866051834785)
XLA Ops:
  0.6 1.3 collective-permute-start
  1.9 8.8 %collective-permute-start.1 = (f32[2,256,256]{2,1,0:T(8,128)}, f32[2,256,256]{2,1,0:T(8,128)S(1)}, u32[]{:S(2)}, u32[]{:S(2)}) collective-permute-start(f32[2,256,256]{2,1,0:T(8,128)} %object_any.1), channel_id=1, source_target_pairs={{1,0},{2,1},{3,2},{4,3},{5,4},{6,5},{7,6},{8,7},{9,8},{10,9},{11,1... | collective-permute-start | bytes 1572872 | tf_op jit(solution)/shard_map/ppermute | solution.py:613
  11.4 9.3 %collective-permute-start.2 = (f32[2,256,256]{2,1,0:T(8,128)S(1)}, f32[2,256,256]{2,1,0:T(8,128)S(1)}, u32[]{:S(2)}, u32[]{:S(2)}) collective-permute-start(f32[2,256,256]{2,1,0:T(8,128)S(1)} %collective-permute-done.below_any), channel_id=1, source_target_pairs={{1,0},{2,1},{3,2},{4,3},{5,4},{6,5},{7,6},{8,7},{9,8},{10,9},{11,1... | collective-permute-start | bytes 1572872 | tf_op jit(solution)/shard_map/ppermute | solution.py:613
  20.7 1.3 copy.25.positions_ref
  22.0 1.9 %collective-permute-start.7 = (f32[2,256,256]{2,1,0:T(8,128)}, f32[2,256,256]{2,1,0:T(8,128)S(1)}, u32[]{:S(2)}, u32[]{:S(2)}) collective-permute-start(f32[2,256,256]{2,1,0:T(8,128)} %prev_own_any.1), channel_id=1, source_target_pairs={{1,0},{2,1},{3,2},{4,3},{5,4},{6,5},{7,6},{8,7},{9,8},{10,9},{11,1... | collective-permute-start | bytes 1572872 | tf_op jit(solution)/shard_map/ppermute | solution.py:613
  23.9 1.3 collective-permute-start.6
  25.2 3.2 %collective-permute-done.2.diag_any = f32[2,256,256]{2,1,0:T(8,128)S(1)} collective-permute-done((f32[2,256,256]{2,1,0:T(8,128)S(1)}, f32[2,256,256]{2,1,0:T(8,128)S(1)}, u32[]{:S(2)}, u32[]{:S(2)}) %collective-permute-start.2) | collective-permute-done | bytes 524320 | tf_op jit(solution)/shard_map/ppermute | solution.py:613
  28.5 0.8 copy-done.12
  29.3 14.6 %gradient_frames.1 = (f32[2,256,256]{2,1,0:T(8,128)}, f32[2,256,256]{2,1,0:T(8,128)}, f32[2,256,256]{2,1,0:T(8,128)}, f32[2,256,256]{2,1,0:T(8,128)}, f32[1024,1...) custom-call(s32[1,1,4,2]{3,2,1,0:T(4,128)} %copy.25.positions_ref, ...), custom_call_target="tpu_custom_call" | custom-call | flops 10000000000 | bytes 10000000 | tf_op jit(solution)/shard_map/gradient_frames/pallas_call | solution.py:520
  43.9 1.9 %collective-permute-start.4 = (f32[2,256,256]{2,1,0:T(8,128)}, f32[2,256,256]{2,1,0:T(8,128)S(1)}, u32[]{:S(2)}, u32[]{:S(2)}) collective-permute-start(f32[2,256,256]{2,1,0:T(8,128)} %get-tuple-element.33), channel_id=1, source_target_pairs={{0,1},{1,2},{2,3},{3,4},{4,5},{5,6},{6,7},{7,8},{8,9},{9,10},{10,1... | collective-permute-start | bytes 1572872 | tf_op jit(solution)/shard_map/ppermute | solution.py:613
  45.9 11.0 %all-to-all-start = ((f32[64,16,128]{2,1,0:T(8,128)}), f32[64,16,128]{2,1,0:T(8,128)S(1)}, u32[]{:S(2)}, u32[]{:S(2)}) async-start(f32[64,16,128]{2,1,0:T(8,128)} %bitcast.14), calls=%async_computation | async-start | bytes 1048576 | tf_op jit(solution)/shard_map/all_to_all | solution.py:626
  56.9 2.4 %collective-permute-start.8 = (f32[2,256,256]{2,1,0:T(8,128)S(1)}, f32[2,256,256]{2,1,0:T(8,128)S(1)}, u32[]{:S(2)}, u32[]{:S(2)}) collective-permute-start(f32[2,256,256]{2,1,0:T(8,128)S(1)} %collective-permute-done.6.prev_below_any), channel_id=1, source_target_pairs={{1,0},{2,1},{3,2},{4,3},{5,4},{6,5},{7,6},{8,7},{9,8},{10,9},{11,1... | collective-permute-start | bytes 1572872 | tf_op jit(solution)/shard_map/ppermute | solution.py:613
  60.1 2.2 %joined.2 = f32[2,256,256]{2,1,0:T(8,128)} custom-call(f32[2,256,256]{2,1,0:T(8,128)} %get-tuple-element.32.refs_0_, f32[2,256,256]{2,1,0:T(8,128)} %copy-done.13), custom_call_target="tpu_custom_call" | custom-call | flops 10000000000 | bytes 10000000 | tf_op jit(solution)/shard_map/joined/pallas_call | solution.py:548
  62.3 3.2 %collective-permute-start.5 = (f32[2,256,256]{2,1,0:T(8,128)}, f32[2,256,256]{2,1,0:T(8,128)S(1)}, u32[]{:S(2)}, u32[]{:S(2)}) collective-permute-start(f32[2,256,256]{2,1,0:T(8,128)} %joined.2), channel_id=1, source_target_pairs={{0,32},{32,64},{64,96},{96,128},{128,160},{160,192},{192,224},{224... | collective-permute-start | bytes 1572872 | tf_op jit(solution)/shard_map/ppermute | solution.py:613
  65.5 3.6 %collective-permute-start.3 = (f32[2,256,256]{2,1,0:T(8,128)S(1)}, f32[2,256,256]{2,1,0:T(8,128)S(1)}, u32[]{:S(2)}, u32[]{:S(2)}) collective-permute-start(f32[2,256,256]{2,1,0:T(8,128)S(1)} %copy-done.9), channel_id=1, source_target_pairs={{0,1},{1,2},{2,3},{3,4},{4,5},{5,6},{6,7},{7,8},{8,9},{9,10},{10,1... | collective-permute-start | bytes 1572872 | tf_op jit(solution)/shard_map/ppermute | solution.py:613
  69.1 1.2 collective-permute-done.8.prev_diag_any
  70.3 7.2 %collective-permute-done.5 = f32[2,256,256]{2,1,0:T(8,128)S(1)} collective-permute-done((f32[2,256,256]{2,1,0:T(8,128)}, f32[2,256,256]{2,1,0:T(8,128)S(1)}, u32[]{:S(2)}, u32[]{:S(2)}) %collective-permute-start.5) | collective-permute-done | bytes 524320 | tf_op jit(solution)/shard_map/ppermute | solution.py:613
  77.7 1.3 collective-permute-start.9
  79.0 2.2 %collective-permute-start.10 = (f32[2,256,256]{2,1,0:T(8,128)S(1)}, f32[2,256,256]{2,1,0:T(8,128)S(1)}, u32[]{:S(2)}, u32[]{:S(2)}) collective-permute-start(f32[2,256,256]{2,1,0:T(8,128)S(1)} %get-tuple-element.56.own_any), channel_id=1, source_target_pairs={{1,0},{2,1},{3,2},{4,3},{5,4},{6,5},{7,6},{8,7},{9,8},{10,9},{11,1... | collective-permute-start | bytes 1572872 | tf_op jit(solution)/shard_map/ppermute | solution.py:613
  81.9 15.2 %all-to-all-start.1 = ((f32[8,18,128]{2,1,0:T(8,128)}), f32[8,18,128]{2,1,0:T(8,128)S(1)}, u32[]{:S(2)}, u32[]{:S(2)}) async-start(f32[8,18,128]{2,1,0:T(8,128)} %broadcast_in_dim.16), calls=%async_computation.1 | async-start | bytes 196608 | tf_op jit(solution)/shard_map/all_to_all | solution.py:626
  97.2 12.7 %all-to-all-done.1 = f32[8,18,128]{2,1,0:T(8,128)S(1)} async-done(((f32[8,18,128]{2,1,0:T(8,128)}), f32[8,18,128]{2,1,0:T(8,128)S(1)}, u32[]{:S(2)}, u32[]{:S(2)}) %all-to-all-start.1) | async-done | bytes 73760 | tf_op jit(solution)/shard_map/all_to_all | solution.py:626
  109.9 3.5 %collective-permute-start.11 = (f32[2,256,256]{2,1,0:T(8,128)S(1)}, f32[2,256,256]{2,1,0:T(8,128)S(1)}, u32[]{:S(2)}, u32[]{:S(2)}) collective-permute-start(f32[2,256,256]{2,1,0:T(8,128)S(1)} %collective-permute-done.9.below_any), channel_id=1, source_target_pairs={{1,0},{2,1},{3,2},{4,3},{5,4},{6,5},{7,6},{8,7},{9,8},{10,9},{11,1... | collective-permute-start | bytes 1572872 | tf_op jit(solution)/shard_map/ppermute | solution.py:613
  113.4 1.1 broadcast_in_dim.34
  114.5 10.3 %all-to-all-start.2 = ((f32[64,18,1,128]{3,2,1,0:T(1,128)}), f32[64,18,1,128]{3,2,1,0:T(1,128)S(1)}, u32[]{:S(2)}, u32[]{:S(2)}) async-start(f32[64,18,1,128]{3,2,1,0:T(1,128)} %broadcast_in_dim.34), calls=%async_computation.2 | async-start | bytes 1179648 | tf_op jit(solution)/shard_map/all_to_all | solution.py:626
  125.5 0.8 copy-done.14
  126.3 1.9 %joined.3.diag_any = f32[2,256,256]{2,1,0:T(8,128)} custom-call(f32[2,256,256]{2,1,0:T(8,128)} %copy-done.14), custom_call_target="tpu_custom_call" | custom-call | flops 20000000000 | bytes 10000000 | tf_op jit(solution)/shard_map/joined/pallas_call | solution.py:548
  128.2 10.1 %all-to-all-done.2 = f32[64,18,1,128]{3,2,1,0:T(1,128)S(1)} async-done(((f32[64,18,1,128]{3,2,1,0:T(1,128)}), f32[64,18,1,128]{3,2,1,0:T(1,128)S(1)}, u32[]{:S(2)}, u32[]{:S(2)}) %all-to-all-start.2) | async-done | bytes 589856 | tf_op jit(solution)/shard_map/all_to_all | solution.py:626
  138.3 0.8 copy-done
  139.2 9.8 %curvature_frames.1 = (f32[2,256,256]{2,1,0:T(8,128)}, f32[2,256,256]{2,1,0:T(8,128)}, f32[1,128]{1,0:T(1,128)}) custom-call(s32[1,1,4,2]{3,2,1,0:T(4,128)} %copy.25.positions_ref, s32[1,32]{1,0:T(1,128)} %counts_ref.3, f32[1]{0:T(128)} %bitcast.12.prev_norm_ref, f32[2,256,256]{2,1,0:T(8,128)} %copy-done.2, f32[2,256,256]{2,1,0:T(8,128)} %copy-done.7, ...), custom_call_target="tpu_custom_call" | custom-call | flops 5000000000 | bytes 10000000 | tf_op jit(solution)/shard_map/curvature_frames/pallas_call | solution.py:567
  149.5 9.9 %all_to_all.25 = f32[32,1,128]{2,1,0:T(1,128)S(1)} all-to-all(f32[32,1,128]{2,1,0:T(1,128)S(1)} %broadcast_in_dim.36), channel_id=1, replica_groups={{0,1,32,33,64,65,96,97,128,129,160,161,192,193,224,225,256,257,288,289,..., dimensions={0} | all-to-all | bytes 32768 | tf_op jit(solution)/shard_map/all_to_all | solution.py:626
  159.4 14.4 %all_to_all.26.gathered_any = f32[16,1,128]{2,1,0:T(1,128)} all-to-all(f32[16,1,128]{2,1,0:T(1,128)S(1)} %broadcast_in_dim.37), channel_id=1, replica_groups={{0,2,4,6,8,10,12,14,16,18,20,22,24,26,28,30},{1,3,5,7,9,11,13,15,17,19,..., dimensions={0} | all-to-all | bytes 16384 | tf_op jit(solution)/shard_map/all_to_all | solution.py:626
  173.8 3.0 %update.1 = (f32[2,256,256]{2,1,0:T(8,128)}, f32[2,256,256]{2,1,0:T(8,128)}, f32[1,1]{1,0:T(1,128)}, f32[1,1,4]{2,1,0:T(1,128)}) custom-call(f32[16,1,128]{2,1,0:T(1,128)} %all_to_all.26.gathered_any, f32[1,128]{1,0:T(1,128)} %get-tuple-element.47.sums_any, f32[2,256,256]{2,1,0:T(8,128)} %object_any.1, f32[2,256,256]{2,1,0:T(8,128)} %get-tuple-element.26.direction_any, ...), custom_call_target="tpu_custom_call" | custom-call | flops 1000000 | bytes 10000000 | tf_op jit(solution)/shard_map/update/pallas_call | solution.py:593
  (46 shorter events, 3.1 us)
Async XLA Ops:
  0.6 10.8 %collective-permute-start = (f32[2,256,256]{2,1,0:T(8,128)}, f32[2,256,256]{2,1,0:T(8,128)S(1)}, u32[]{:S(2)}, u32[]{:S(2)}) collective-permute-start(f32[2,256,256]{2,1,0:T(8,128)} %object_any.1), channel_id=1, source_target_pairs={{32,0},{64,32},{96,64},{128,96},{160,128},{192,160},{224,192},{256... | collective-permute-start | bytes 1572872 | tf_op jit(solution)/shard_map/ppermute | solution.py:613
  1.9 23.3 %collective-permute-start.1 = (f32[2,256,256]{2,1,0:T(8,128)}, f32[2,256,256]{2,1,0:T(8,128)S(1)}, u32[]{:S(2)}, u32[]{:S(2)}) collective-permute-start(f32[2,256,256]{2,1,0:T(8,128)} %object_any.1), channel_id=1, source_target_pairs={{1,0},{2,1},{3,2},{4,3},{5,4},{6,5},{7,6},{8,7},{9,8},{10,9},{11,1... | collective-permute-start | bytes 1572872 | tf_op jit(solution)/shard_map/ppermute | solution.py:613
  11.4 17.0 %copy-start.10 = (f32[2,256,256]{2,1,0:T(8,128)}, f32[2,256,256]{2,1,0:T(8,128)S(1)}, u32[]{:S(2)}) copy-start(f32[2,256,256]{2,1,0:T(8,128)S(1)} %collective-permute-done.below_any) | copy-start | bytes 1572868
  11.4 17.0 %collective-permute-start.2 = (f32[2,256,256]{2,1,0:T(8,128)S(1)}, f32[2,256,256]{2,1,0:T(8,128)S(1)}, u32[]{:S(2)}, u32[]{:S(2)}) collective-permute-start(f32[2,256,256]{2,1,0:T(8,128)S(1)} %collective-permute-done.below_any), channel_id=1, source_target_pairs={{1,0},{2,1},{3,2},{4,3},{5,4},{6,5},{7,6},{8,7},{9,8},{10,9},{11,1... | collective-permute-start | bytes 1572872 | tf_op jit(solution)/shard_map/ppermute | solution.py:613
  22.0 23.8 %collective-permute-start.7 = (f32[2,256,256]{2,1,0:T(8,128)}, f32[2,256,256]{2,1,0:T(8,128)S(1)}, u32[]{:S(2)}, u32[]{:S(2)}) collective-permute-start(f32[2,256,256]{2,1,0:T(8,128)} %prev_own_any.1), channel_id=1, source_target_pairs={{1,0},{2,1},{3,2},{4,3},{5,4},{6,5},{7,6},{8,7},{9,8},{10,9},{11,1... | collective-permute-start | bytes 1572872 | tf_op jit(solution)/shard_map/ppermute | solution.py:613
  23.9 21.9 %collective-permute-start.6 = (f32[2,256,256]{2,1,0:T(8,128)}, f32[2,256,256]{2,1,0:T(8,128)S(1)}, u32[]{:S(2)}, u32[]{:S(2)}) collective-permute-start(f32[2,256,256]{2,1,0:T(8,128)} %prev_own_any.1), channel_id=1, source_target_pairs={{32,0},{64,32},{96,64},{128,96},{160,128},{192,160},{224,192},{256... | collective-permute-start | bytes 1572872 | tf_op jit(solution)/shard_map/ppermute | solution.py:613
  25.2 3.2 %copy-start.11 = (f32[2,256,256]{2,1,0:T(8,128)}, f32[2,256,256]{2,1,0:T(8,128)S(1)}, u32[]{:S(2)}) copy-start(f32[2,256,256]{2,1,0:T(8,128)S(1)} %collective-permute-done.1.right_any) | copy-start | bytes 1572868
  28.5 0.8 copy-start.12
  43.9 15.3 %collective-permute-start.4 = (f32[2,256,256]{2,1,0:T(8,128)}, f32[2,256,256]{2,1,0:T(8,128)S(1)}, u32[]{:S(2)}, u32[]{:S(2)}) collective-permute-start(f32[2,256,256]{2,1,0:T(8,128)} %get-tuple-element.33), channel_id=1, source_target_pairs={{0,1},{1,2},{2,3},{3,4},{4,5},{5,6},{6,7},{7,8},{8,9},{9,10},{10,1... | collective-permute-start | bytes 1572872 | tf_op jit(solution)/shard_map/ppermute | solution.py:613
  45.9 16.4 %copy-start.4 = (f32[2,256,256]{2,1,0:T(8,128)}, f32[2,256,256]{2,1,0:T(8,128)S(1)}, u32[]{:S(2)}) copy-start(f32[2,256,256]{2,1,0:T(8,128)S(1)} %collective-permute-done.7.prev_right_any) | copy-start | bytes 1572868
  45.9 16.4 %copy-start.5 = (f32[2,256,256]{2,1,0:T(8,128)}, f32[2,256,256]{2,1,0:T(8,128)S(1)}, u32[]{:S(2)}) copy-start(f32[2,256,256]{2,1,0:T(8,128)S(1)} %collective-permute-done.6.prev_below_any) | copy-start | bytes 1572868
  45.9 35.3 %all-to-all-start = ((f32[64,16,128]{2,1,0:T(8,128)}), f32[64,16,128]{2,1,0:T(8,128)S(1)}, u32[]{:S(2)}, u32[]{:S(2)}) async-start(f32[64,16,128]{2,1,0:T(8,128)} %bitcast.14), calls=%async_computation | async-start | bytes 1048576 | tf_op jit(solution)/shard_map/all_to_all | solution.py:626
  56.9 13.4 %collective-permute-start.8 = (f32[2,256,256]{2,1,0:T(8,128)S(1)}, f32[2,256,256]{2,1,0:T(8,128)S(1)}, u32[]{:S(2)}, u32[]{:S(2)}) collective-permute-start(f32[2,256,256]{2,1,0:T(8,128)S(1)} %collective-permute-done.6.prev_below_any), channel_id=1, source_target_pairs={{1,0},{2,1},{3,2},{4,3},{5,4},{6,5},{7,6},{8,7},{9,8},{10,9},{11,1... | collective-permute-start | bytes 1572872 | tf_op jit(solution)/shard_map/ppermute | solution.py:613
  59.3 0.8 copy-start.13
  60.1 5.5 %copy-start.9 = (f32[2,256,256]{2,1,0:T(8,128)S(1)}, f32[2,256,256]{2,1,0:T(8,128)}, u32[]{:S(2)}) copy-start(f32[2,256,256]{2,1,0:T(8,128)} %get-tuple-element.31) | copy-start | bytes 1572868
  60.1 17.4 %copy-start.1 = (f32[2,256,256]{2,1,0:T(8,128)S(1)}, f32[2,256,256]{2,1,0:T(8,128)}, u32[]{:S(2)}) copy-start(f32[2,256,256]{2,1,0:T(8,128)} %prev_own_any.1) | copy-start | bytes 1572868
  60.1 17.4 %copy-start.3 = (f32[2,256,256]{2,1,0:T(8,128)S(1)}, f32[2,256,256]{2,1,0:T(8,128)}, u32[]{:S(2)}) copy-start(f32[2,256,256]{2,1,0:T(8,128)} %get-tuple-element.30) | copy-start | bytes 1572868
  62.3 15.2 %collective-permute-start.5 = (f32[2,256,256]{2,1,0:T(8,128)}, f32[2,256,256]{2,1,0:T(8,128)S(1)}, u32[]{:S(2)}, u32[]{:S(2)}) collective-permute-start(f32[2,256,256]{2,1,0:T(8,128)} %joined.2), channel_id=1, source_target_pairs={{0,32},{32,64},{64,96},{96,128},{128,160},{160,192},{192,224},{224... | collective-permute-start | bytes 1572872 | tf_op jit(solution)/shard_map/ppermute | solution.py:613
  65.5 12.0 %collective-permute-start.3 = (f32[2,256,256]{2,1,0:T(8,128)S(1)}, f32[2,256,256]{2,1,0:T(8,128)S(1)}, u32[]{:S(2)}, u32[]{:S(2)}) collective-permute-start(f32[2,256,256]{2,1,0:T(8,128)S(1)} %copy-done.9), channel_id=1, source_target_pairs={{0,1},{1,2},{2,3},{3,4},{4,5},{5,6},{6,7},{7,8},{8,9},{9,10},{10,1... | collective-permute-start | bytes 1572872 | tf_op jit(solution)/shard_map/ppermute | solution.py:613
  70.3 44.3 %copy-start.6 = (f32[2,256,256]{2,1,0:T(8,128)}, f32[2,256,256]{2,1,0:T(8,128)S(1)}, u32[]{:S(2)}) copy-start(f32[2,256,256]{2,1,0:T(8,128)S(1)} %collective-permute-done.8.prev_diag_any) | copy-start | bytes 1572868
  77.7 50.5 %copy-start.2 = (f32[2,256,256]{2,1,0:T(8,128)}, f32[2,256,256]{2,1,0:T(8,128)S(1)}, u32[]{:S(2)}) copy-start(f32[2,256,256]{2,1,0:T(8,128)S(1)} %get-tuple-element.56.own_any) | copy-start | bytes 1572868
  77.7 19.5 %collective-permute-start.9 = (f32[2,256,256]{2,1,0:T(8,128)S(1)}, f32[2,256,256]{2,1,0:T(8,128)S(1)}, u32[]{:S(2)}, u32[]{:S(2)}) collective-permute-start(f32[2,256,256]{2,1,0:T(8,128)S(1)} %get-tuple-element.56.own_any), channel_id=1, source_target_pairs={{32,0},{64,32},{96,64},{128,96},{160,128},{192,160},{224,192},{256... | collective-permute-start | bytes 1572872 | tf_op jit(solution)/shard_map/ppermute | solution.py:613
  79.0 18.2 %collective-permute-start.10 = (f32[2,256,256]{2,1,0:T(8,128)S(1)}, f32[2,256,256]{2,1,0:T(8,128)S(1)}, u32[]{:S(2)}, u32[]{:S(2)}) collective-permute-start(f32[2,256,256]{2,1,0:T(8,128)S(1)} %get-tuple-element.56.own_any), channel_id=1, source_target_pairs={{1,0},{2,1},{3,2},{4,3},{5,4},{6,5},{7,6},{8,7},{9,8},{10,9},{11,1... | collective-permute-start | bytes 1572872 | tf_op jit(solution)/shard_map/ppermute | solution.py:613
  81.9 28.0 %all-to-all-start.1 = ((f32[8,18,128]{2,1,0:T(8,128)}), f32[8,18,128]{2,1,0:T(8,128)S(1)}, u32[]{:S(2)}, u32[]{:S(2)}) async-start(f32[8,18,128]{2,1,0:T(8,128)} %broadcast_in_dim.16), calls=%async_computation.1 | async-start | bytes 196608 | tf_op jit(solution)/shard_map/all_to_all | solution.py:626
  97.1 31.1 %copy-start.7 = (f32[2,256,256]{2,1,0:T(8,128)}, f32[2,256,256]{2,1,0:T(8,128)S(1)}, u32[]{:S(2)}) copy-start(f32[2,256,256]{2,1,0:T(8,128)S(1)} %collective-permute-done.9.below_any) | copy-start | bytes 1572868
  97.1 31.1 %copy-start.8 = (f32[2,256,256]{2,1,0:T(8,128)}, f32[2,256,256]{2,1,0:T(8,128)S(1)}, u32[]{:S(2)}) copy-start(f32[2,256,256]{2,1,0:T(8,128)S(1)} %collective-permute-done.10.right_any) | copy-start | bytes 1572868
  109.9 15.6 %collective-permute-start.11 = (f32[2,256,256]{2,1,0:T(8,128)S(1)}, f32[2,256,256]{2,1,0:T(8,128)S(1)}, u32[]{:S(2)}, u32[]{:S(2)}) collective-permute-start(f32[2,256,256]{2,1,0:T(8,128)S(1)} %collective-permute-done.9.below_any), channel_id=1, source_target_pairs={{1,0},{2,1},{3,2},{4,3},{5,4},{6,5},{7,6},{8,7},{9,8},{10,9},{11,1... | collective-permute-start | bytes 1572872 | tf_op jit(solution)/shard_map/ppermute | solution.py:613
  114.5 23.8 %all-to-all-start.2 = ((f32[64,18,1,128]{3,2,1,0:T(1,128)}), f32[64,18,1,128]{3,2,1,0:T(1,128)S(1)}, u32[]{:S(2)}, u32[]{:S(2)}) async-start(f32[64,18,1,128]{3,2,1,0:T(1,128)} %broadcast_in_dim.34), calls=%async_computation.2 | async-start | bytes 1179648 | tf_op jit(solution)/shard_map/all_to_all | solution.py:626
  125.5 0.8 copy-start.14
  138.3 0.8 copy-start

commit v7 on v6

--- a/solution.py
+++ b/solution.py
@@ -8,8 +8,6 @@
 from jax.experimental import pallas as pl
 from jax.experimental.pallas import tpu as pltpu
 from jax.sharding import PartitionSpec as P
-
-VMEM_BYTES = 60 * 1024 * 1024
 
 
 def dft_blocks(width):
@@ -506,9 +504,9 @@
     ]
 
 
-def costing(flops):
+def costing(flops, mebibytes=60):
     return {
-        "compiler_params": pltpu.CompilerParams(vmem_limit_bytes=VMEM_BYTES),
+        "compiler_params": pltpu.CompilerParams(vmem_limit_bytes=mebibytes * 2**20),
         "cost_estimate": pl.CostEstimate(flops=flops, bytes_accessed=10**7, transcendentals=0),
     }
 
@@ -539,7 +537,7 @@
             arrivals_of(11),
         ],
         name="gradient_frames",
-        **costing(10**10),
+        **costing(10**10, 60),
     )(positions, counts, *tiles, probe, measured, *tables)
 
 
@@ -556,7 +554,7 @@
             pltpu.SemaphoreType.DMA,
         ],
         name="joined",
-        **costing(flops),
+        **costing(flops, 4),
     )(*arrays)
 
 
@@ -670,10 +668,11 @@
     )
     from_left_corner = passed_along(diag_grad, "col", 1)
     pieces = exchanged(probe_part.reshape((len(near[0]), -1, width // 2)), near)
-    from_above = passed_along(joined_call((below_grad, from_left_corner), 10**10), "row", 1)
-    from_left = passed_along(right_grad, "col", 1)
+    below_sum = joined_call((below_grad, from_left_corner), 10**10)
+    from_above = passed_along(below_sum, "row", 1)
+    from_left = passed_along(held(right_grad, below_sum), "col", 1)
     prev_diag = passed_along(held(prev_below, diag_grad), "col", -1)
-    from_above = held(from_above, prev_diag)
+    prev_diag = joined_call((prev_diag,), 10**9)
     object_grad = own_grad + from_left + from_above
     sums = [
         jnp.sum(jnp.sum(object_grad * other, axis=(0, 1)).reshape(2, -1), axis=0, keepdims=True)

time: 178 us -> 179 us (level)
  Pallas kernels: 31.4 us -> 20.2 us
  starting transfers between devices: 77.1 us -> 84.2 us
  blocking collectives: 24.3 us -> 26.8 us
  local copies, waits for them, and re-layouts: 6.92 us -> 8.89 us
    pallas_call x1, Pallas kernels: 14.6 us -> 9.37 us  [gradient_call(): pl.pallas_call(gradient_kernel, out_shape=(shaped(2, width, width),) * 4...]
    all_to_all x3, starting transfers between devices: 36.5 us -> 41.3 us  [exchanged(): lax.all_to_all(pieces, ('row', 'col'), 0, 0, axis_index_groups=groups)]
    pallas_call x2 -> x3, Pallas kernels: 4.06 us -> 0.38 us  [joined_call(): pl.pallas_call(joined_kernel, out_shape=shaped(*shape), in_specs=anywhere...]
    ppermute x12, waiting for transfers between devices: 12.3 us -> 15.5 us  [passed_along(): return lax.ppermute(shard, axis, pairs)]
    all_to_all x3, waiting for transfers between devices: 22.9 us -> 20.1 us  [exchanged(): lax.all_to_all(pieces, ('row', 'col'), 0, 0, axis_index_groups=groups)]
    all_to_all x2, blocking collectives: 24.3 us -> 26.8 us  [exchanged(): lax.all_to_all(pieces, ('row', 'col'), 0, 0, axis_index_groups=groups)]
    ppermute x12, starting transfers between devices: 40.6 us -> 43 us  [passed_along(): return lax.ppermute(shard, axis, pairs)]
    pallas_call x1, Pallas kernels: 9.76 us -> 7.44 us  [curvature_call(): pl.pallas_call(functools.partial(curvature_kernel, probe_scale=scale, pie...]
  transfers between devices with their start and end apart: 15 -> 15, of which waited for: 6 -> 6; matrix products, arithmetic and copies ran while one was open for 2% -> 2% of each run, Pallas kernels for 11% -> 5%
where the time goes in v7:
time: 179 us; the launch traced here: 178 us
  starting transfers between devices  84.2 us (47%)
  waiting for transfers between devices  35.6 us (20%)
  blocking collectives  26.8 us (15%)
  Pallas kernels  20.2 us (11%)
  local copies, waits for them, and re-layouts  8.89 us (5%)
    ppermute x12, starting transfers between devices, passed_along(): return lax.ppermute(shard, axis, pairs)  43 us
    all_to_all x3, starting transfers between devices, exchanged(): lax.all_to_all(pieces, ('row', 'col'), 0, 0, axis_index_groups=groups)  41.3 us
    all_to_all x2, blocking collectives, exchanged(): lax.all_to_all(pieces, ('row', 'col'), 0, 0, axis_index_groups=groups)  26.8 us
    all_to_all x3, waiting for transfers between devices, exchanged(): lax.all_to_all(pieces, ('row', 'col'), 0, 0, axis_index_groups=groups)  20.1 us
    ppermute x12, waiting for transfers between devices, passed_along(): return lax.ppermute(shard, axis, pairs)  15.5 us
    pallas_call x1, Pallas kernels, gradient_call(): pl.pallas_call(gradient_kernel, out_shape=(shaped(2, width, width),) * 4...  9.37 us
    pallas_call x1, Pallas kernels, curvature_call(): pl.pallas_call(functools.partial(curvature_kernel, probe_scale=scale, pie...  7.44 us
    unnamed x27, local copies, waits for them, and re-layouts  6.49 us
  transfers between devices with their start and end apart: 15, of which 6 were waited for; matrix products, arithmetic and copies ran while one was open for 2% of the time, Pallas kernels for 5%

profile of v7, /device:TPU:1, one launch (start us, length us, event | category | flops | bytes accessed | tf_op | source)
XLA Modules:
  0.0 177.8 jit_solution(3117485924968461303)
XLA Ops:
  0.6 1.3 collective-permute-start
  1.9 8.8 %collective-permute-start.1 = (f32[2,256,256]{2,1,0:T(8,128)}, f32[2,256,256]{2,1,0:T(8,128)S(1)}, u32[]{:S(2)}, u32[]{:S(2)}) collective-permute-start(f32[2,256,256]{2,1,0:T(8,128)} %object_any.1), channel_id=1, source_target_pairs={{1,0},{2,1},{3,2},{4,3},{5,4},{6,5},{7,6},{8,7},{9,8},{10,9},{11,1... | collective-permute-start | bytes 1572872 | tf_op jit(solution)/shard_map/ppermute | solution.py:611
  11.4 9.3 %collective-permute-start.2 = (f32[2,256,256]{2,1,0:T(8,128)S(1)}, f32[2,256,256]{2,1,0:T(8,128)S(1)}, u32[]{:S(2)}, u32[]{:S(2)}) collective-permute-start(f32[2,256,256]{2,1,0:T(8,128)S(1)} %collective-permute-done.below_any), channel_id=1, source_target_pairs={{1,0},{2,1},{3,2},{4,3},{5,4},{6,5},{7,6},{8,7},{9,8},{10,9},{11,1... | collective-permute-start | bytes 1572872 | tf_op jit(solution)/shard_map/ppermute | solution.py:611
  20.7 1.3 copy.25.positions_ref
  22.1 1.9 %collective-permute-start.7 = (f32[2,256,256]{2,1,0:T(8,128)}, f32[2,256,256]{2,1,0:T(8,128)S(1)}, u32[]{:S(2)}, u32[]{:S(2)}) collective-permute-start(f32[2,256,256]{2,1,0:T(8,128)} %prev_own_any.1), channel_id=1, source_target_pairs={{1,0},{2,1},{3,2},{4,3},{5,4},{6,5},{7,6},{8,7},{9,8},{10,9},{11,1... | collective-permute-start | bytes 1572872 | tf_op jit(solution)/shard_map/ppermute | solution.py:611
  24.0 1.3 collective-permute-start.6
  25.3 3.3 %collective-permute-done.2.diag_any = f32[2,256,256]{2,1,0:T(8,128)S(1)} collective-permute-done((f32[2,256,256]{2,1,0:T(8,128)S(1)}, f32[2,256,256]{2,1,0:T(8,128)S(1)}, u32[]{:S(2)}, u32[]{:S(2)}) %collective-permute-start.2) | collective-permute-done | bytes 524320 | tf_op jit(solution)/shard_map/ppermute | solution.py:611
  29.4 9.4 %gradient_frames.1 = (f32[2,256,256]{2,1,0:T(8,128)}, f32[2,256,256]{2,1,0:T(8,128)}, f32[2,256,256]{2,1,0:T(8,128)}, f32[2,256,256]{2,1,0:T(8,128)}, f32[1024,1...) custom-call(s32[1,1,4,2]{3,2,1,0:T(4,128)} %copy.25.positions_ref, ...), custom_call_target="tpu_custom_call" | custom-call | flops 10000000000 | bytes 10000000 | tf_op jit(solution)/shard_map/gradient_frames/pallas_call | solution.py:518
  38.8 1.9 %collective-permute-start.3 = (f32[2,256,256]{2,1,0:T(8,128)}, f32[2,256,256]{2,1,0:T(8,128)S(1)}, u32[]{:S(2)}, u32[]{:S(2)}) collective-permute-start(f32[2,256,256]{2,1,0:T(8,128)} %get-tuple-element.33), channel_id=1, source_target_pairs={{0,1},{1,2},{2,3},{3,4},{4,5},{5,6},{6,7},{7,8},{8,9},{9,10},{10,1... | collective-permute-start | bytes 1572872 | tf_op jit(solution)/shard_map/ppermute | solution.py:611
  40.7 16.1 %all-to-all-start = ((f32[64,16,128]{2,1,0:T(8,128)}), f32[64,16,128]{2,1,0:T(8,128)S(1)}, u32[]{:S(2)}, u32[]{:S(2)}) async-start(f32[64,16,128]{2,1,0:T(8,128)} %bitcast.14), calls=%async_computation | async-start | bytes 1048576 | tf_op jit(solution)/shard_map/all_to_all | solution.py:624
  56.9 1.0 copy-done.2
  58.1 0.8 copy-done.9
  58.9 3.5 %collective-permute-start.4 = (f32[2,256,256]{2,1,0:T(8,128)S(1)}, f32[2,256,256]{2,1,0:T(8,128)S(1)}, u32[]{:S(2)}, u32[]{:S(2)}) collective-permute-start(f32[2,256,256]{2,1,0:T(8,128)S(1)} %copy-done.9), channel_id=1, source_target_pairs={{0,1},{1,2},{2,3},{3,4},{4,5},{5,6},{6,7},{7,8},{8,9},{9,10},{10,1... | collective-permute-start | bytes 1572872 | tf_op jit(solution)/shard_map/ppermute | solution.py:611
  62.5 3.1 %collective-permute-start.5 = (f32[2,256,256]{2,1,0:T(8,128)S(1)}, f32[2,256,256]{2,1,0:T(8,128)S(1)}, u32[]{:S(2)}, u32[]{:S(2)}) collective-permute-start(f32[2,256,256]{2,1,0:T(8,128)S(1)} %joined.3), channel_id=1, source_target_pairs={{0,32},{32,64},{64,96},{96,128},{128,160},{160,192},{192,224},{224... | collective-permute-start | bytes 1572872 | tf_op jit(solution)/shard_map/ppermute | solution.py:611
  65.6 3.0 %collective-permute-done.4 = f32[2,256,256]{2,1,0:T(8,128)S(1)} collective-permute-done((f32[2,256,256]{2,1,0:T(8,128)S(1)}, f32[2,256,256]{2,1,0:T(8,128)S(1)}, u32[]{:S(2)}, u32[]{:S(2)}) %collective-permute-start.4) | collective-permute-done | bytes 524320 | tf_op jit(solution)/shard_map/ppermute | solution.py:611
  68.6 8.5 %collective-permute-done.5 = f32[2,256,256]{2,1,0:T(8,128)S(1)} collective-permute-done((f32[2,256,256]{2,1,0:T(8,128)S(1)}, f32[2,256,256]{2,1,0:T(8,128)S(1)}, u32[]{:S(2)}, u32[]{:S(2)}) %collective-permute-start.5) | collective-permute-done | bytes 524320 | tf_op jit(solution)/shard_map/ppermute | solution.py:611
  77.2 1.3 collective-permute-start.8
  78.5 2.0 %collective-permute-start.9 = (f32[2,256,256]{2,1,0:T(8,128)S(1)}, f32[2,256,256]{2,1,0:T(8,128)}, u32[]{:S(2)}, u32[]{:S(2)}) collective-permute-start(f32[2,256,256]{2,1,0:T(8,128)S(1)} %get-tuple-element.56.own_any), channel_id=1, source_target_pairs={{1,0},{2,1},{3,2},{4,3},{5,4},{6,5},{7,6},{8,7},{9,8},{10,9},{11,1... | collective-permute-start | bytes 1572872 | tf_op jit(solution)/shard_map/ppermute | solution.py:611
  81.3 13.4 %all-to-all-start.1 = ((f32[8,18,128]{2,1,0:T(8,128)}), f32[8,18,128]{2,1,0:T(8,128)S(1)}, u32[]{:S(2)}, u32[]{:S(2)}) async-start(f32[8,18,128]{2,1,0:T(8,128)} %broadcast_in_dim.16), calls=%async_computation.1 | async-start | bytes 196608 | tf_op jit(solution)/shard_map/all_to_all | solution.py:624
  94.7 4.0 %collective-permute-start.11 = (f32[2,256,256]{2,1,0:T(8,128)}, f32[2,256,256]{2,1,0:T(8,128)S(1)}, u32[]{:S(2)}, u32[]{:S(2)}) collective-permute-start(f32[2,256,256]{2,1,0:T(8,128)} %collective-permute-done.6.prev_below_any), channel_id=1, source_target_pairs={{1,0},{2,1},{3,2},{4,3},{5,4},{6,5},{7,6},{8,7},{9,8},{10,9},{11,1... | collective-permute-start | bytes 1572872 | tf_op jit(solution)/shard_map/ppermute | solution.py:611
  98.7 9.2 %all-to-all-done.1 = f32[8,18,128]{2,1,0:T(8,128)S(1)} async-done(((f32[8,18,128]{2,1,0:T(8,128)}), f32[8,18,128]{2,1,0:T(8,128)S(1)}, u32[]{:S(2)}, u32[]{:S(2)}) %all-to-all-start.1) | async-done | bytes 73760 | tf_op jit(solution)/shard_map/all_to_all | solution.py:624
  107.9 4.6 %collective-permute-start.10 = (f32[2,256,256]{2,1,0:T(8,128)S(1)}, f32[2,256,256]{2,1,0:T(8,128)S(1)}, u32[]{:S(2)}, u32[]{:S(2)}) collective-permute-start(f32[2,256,256]{2,1,0:T(8,128)S(1)} %collective-permute-done.8.below_any), channel_id=1, source_target_pairs={{1,0},{2,1},{3,2},{4,3},{5,4},{6,5},{7,6},{8,7},{9,8},{10,9},{11,1... | collective-permute-start | bytes 1572872 | tf_op jit(solution)/shard_map/ppermute | solution.py:611
  112.5 1.1 broadcast_in_dim.34
  113.6 11.8 %all-to-all-start.2 = ((f32[64,18,1,128]{3,2,1,0:T(1,128)}), f32[64,18,1,128]{3,2,1,0:T(1,128)S(1)}, u32[]{:S(2)}, u32[]{:S(2)}) async-start(f32[64,18,1,128]{3,2,1,0:T(1,128)} %broadcast_in_dim.34), calls=%async_computation.2 | async-start | bytes 1179648 | tf_op jit(solution)/shard_map/all_to_all | solution.py:624
  126.2 0.8 copy-done
  127.1 0.8 copy-done.1
  128.0 10.9 %all-to-all-done.2 = f32[64,18,1,128]{3,2,1,0:T(1,128)S(1)} async-done(((f32[64,18,1,128]{3,2,1,0:T(1,128)}), f32[64,18,1,128]{3,2,1,0:T(1,128)S(1)}, u32[]{:S(2)}, u32[]{:S(2)}) %all-to-all-start.2) | async-done | bytes 589856 | tf_op jit(solution)/shard_map/all_to_all | solution.py:624
  138.9 0.8 copy-done.3
  139.7 7.4 %curvature_frames.1 = (f32[2,256,256]{2,1,0:T(8,128)}, f32[2,256,256]{2,1,0:T(8,128)}, f32[1,128]{1,0:T(1,128)}) custom-call(s32[1,1,4,2]{3,2,1,0:T(4,128)} %copy.25.positions_ref, s32[1,32]{1,0:T(1,128)} %counts_ref.3, f32[1]{0:T(128)} %bitcast.12.prev_norm_ref, f32[2,256,256]{2,1,0:T(8,128)} %copy-done.5, f32[2,256,256]{2,1,0:T(8,128)} %copy-done.8, ...), custom_call_target="tpu_custom_call" | custom-call | flops 5000000000 | bytes 10000000 | tf_op jit(solution)/shard_map/curvature_frames/pallas_call | solution.py:565
  147.8 12.5 %all_to_all.25 = f32[32,1,128]{2,1,0:T(1,128)S(1)} all-to-all(f32[32,1,128]{2,1,0:T(1,128)S(1)} %broadcast_in_dim.36), channel_id=1, replica_groups={{0,1,32,33,64,65,96,97,128,129,160,161,192,193,224,225,256,257,288,289,..., dimensions={0} | all-to-all | bytes 32768 | tf_op jit(solution)/shard_map/all_to_all | solution.py:624
  160.3 14.3 %all_to_all.26.gathered_any = f32[16,1,128]{2,1,0:T(1,128)} all-to-all(f32[16,1,128]{2,1,0:T(1,128)S(1)} %broadcast_in_dim.37), channel_id=1, replica_groups={{0,2,4,6,8,10,12,14,16,18,20,22,24,26,28,30},{1,3,5,7,9,11,13,15,17,19,..., dimensions={0} | all-to-all | bytes 16384 | tf_op jit(solution)/shard_map/all_to_all | solution.py:624
  174.6 3.0 %update.1 = (f32[2,256,256]{2,1,0:T(8,128)}, f32[2,256,256]{2,1,0:T(8,128)}, f32[1,1]{1,0:T(1,128)}, f32[1,1,4]{2,1,0:T(1,128)}) custom-call(f32[16,1,128]{2,1,0:T(1,128)} %all_to_all.26.gathered_any, f32[1,128]{1,0:T(1,128)} %get-tuple-element.47.sums_any, f32[2,256,256]{2,1,0:T(8,128)} %object_any.1, f32[2,256,256]{2,1,0:T(8,128)} %get-tuple-element.26.direction_any, ...), custom_call_target="tpu_custom_call" | custom-call | flops 1000000 | bytes 10000000 | tf_op jit(solution)/shard_map/update/pallas_call | solution.py:591
  (43 shorter events, 3.5 us)
Async XLA Ops:
  0.6 10.8 %collective-permute-start = (f32[2,256,256]{2,1,0:T(8,128)}, f32[2,256,256]{2,1,0:T(8,128)S(1)}, u32[]{:S(2)}, u32[]{:S(2)}) collective-permute-start(f32[2,256,256]{2,1,0:T(8,128)} %object_any.1), channel_id=1, source_target_pairs={{32,0},{64,32},{96,64},{128,96},{160,128},{192,160},{224,192},{256... | collective-permute-start | bytes 1572872 | tf_op jit(solution)/shard_map/ppermute | solution.py:611
  1.9 23.3 %collective-permute-start.1 = (f32[2,256,256]{2,1,0:T(8,128)}, f32[2,256,256]{2,1,0:T(8,128)S(1)}, u32[]{:S(2)}, u32[]{:S(2)}) collective-permute-start(f32[2,256,256]{2,1,0:T(8,128)} %object_any.1), channel_id=1, source_target_pairs={{1,0},{2,1},{3,2},{4,3},{5,4},{6,5},{7,6},{8,7},{9,8},{10,9},{11,1... | collective-permute-start | bytes 1572872 | tf_op jit(solution)/shard_map/ppermute | solution.py:611
  11.4 17.1 %copy-start.10 = (f32[2,256,256]{2,1,0:T(8,128)}, f32[2,256,256]{2,1,0:T(8,128)S(1)}, u32[]{:S(2)}) copy-start(f32[2,256,256]{2,1,0:T(8,128)S(1)} %collective-permute-done.below_any) | copy-start | bytes 1572868
  11.4 17.1 %collective-permute-start.2 = (f32[2,256,256]{2,1,0:T(8,128)S(1)}, f32[2,256,256]{2,1,0:T(8,128)S(1)}, u32[]{:S(2)}, u32[]{:S(2)}) collective-permute-start(f32[2,256,256]{2,1,0:T(8,128)S(1)} %collective-permute-done.below_any), channel_id=1, source_target_pairs={{1,0},{2,1},{3,2},{4,3},{5,4},{6,5},{7,6},{8,7},{9,8},{10,9},{11,1... | collective-permute-start | bytes 1572872 | tf_op jit(solution)/shard_map/ppermute | solution.py:611
  22.1 18.6 %collective-permute-start.7 = (f32[2,256,256]{2,1,0:T(8,128)}, f32[2,256,256]{2,1,0:T(8,128)S(1)}, u32[]{:S(2)}, u32[]{:S(2)}) collective-permute-start(f32[2,256,256]{2,1,0:T(8,128)} %prev_own_any.1), channel_id=1, source_target_pairs={{1,0},{2,1},{3,2},{4,3},{5,4},{6,5},{7,6},{8,7},{9,8},{10,9},{11,1... | collective-permute-start | bytes 1572872 | tf_op jit(solution)/shard_map/ppermute | solution.py:611
  24.0 16.7 %collective-permute-start.6 = (f32[2,256,256]{2,1,0:T(8,128)}, f32[2,256,256]{2,1,0:T(8,128)}, u32[]{:S(2)}, u32[]{:S(2)}) collective-permute-start(f32[2,256,256]{2,1,0:T(8,128)} %prev_own_any.1), channel_id=1, source_target_pairs={{32,0},{64,32},{96,64},{128,96},{160,128},{192,160},{224,192},{256... | collective-permute-start | bytes 1572872 | tf_op jit(solution)/shard_map/ppermute | solution.py:611
  25.3 3.3 %copy-start.11 = (f32[2,256,256]{2,1,0:T(8,128)}, f32[2,256,256]{2,1,0:T(8,128)S(1)}, u32[]{:S(2)}) copy-start(f32[2,256,256]{2,1,0:T(8,128)S(1)} %collective-permute-done.1.right_any) | copy-start | bytes 1572868
  28.6 0.8 copy-start.12
  38.8 18.1 %collective-permute-start.3 = (f32[2,256,256]{2,1,0:T(8,128)}, f32[2,256,256]{2,1,0:T(8,128)S(1)}, u32[]{:S(2)}, u32[]{:S(2)}) collective-permute-start(f32[2,256,256]{2,1,0:T(8,128)} %get-tuple-element.33), channel_id=1, source_target_pairs={{0,1},{1,2},{2,3},{3,4},{4,5},{5,6},{6,7},{7,8},{8,9},{9,10},{10,1... | collective-permute-start | bytes 1572872 | tf_op jit(solution)/shard_map/ppermute | solution.py:611
  40.7 17.4 %copy-start.7 = (f32[2,256,256]{2,1,0:T(8,128)}, f32[2,256,256]{2,1,0:T(8,128)S(1)}, u32[]{:S(2)}) copy-start(f32[2,256,256]{2,1,0:T(8,128)S(1)} %collective-permute-done.7.prev_right_any) | copy-start | bytes 1572868
  40.7 39.8 %all-to-all-start = ((f32[64,16,128]{2,1,0:T(8,128)}), f32[64,16,128]{2,1,0:T(8,128)S(1)}, u32[]{:S(2)}, u32[]{:S(2)}) async-start(f32[64,16,128]{2,1,0:T(8,128)} %bitcast.14), calls=%async_computation | async-start | bytes 1048576 | tf_op jit(solution)/shard_map/all_to_all | solution.py:624
  56.8 1.0 copy-start.2
  57.9 1.0 copy-start.9
  57.9 19.1 %copy-start.4 = (f32[2,256,256]{2,1,0:T(8,128)S(1)}, f32[2,256,256]{2,1,0:T(8,128)}, u32[]{:S(2)}) copy-start(f32[2,256,256]{2,1,0:T(8,128)} %prev_own_any.1) | copy-start | bytes 1572868
  57.9 19.1 %copy-start.6 = (f32[2,256,256]{2,1,0:T(8,128)S(1)}, f32[2,256,256]{2,1,0:T(8,128)}, u32[]{:S(2)}) copy-start(f32[2,256,256]{2,1,0:T(8,128)} %get-tuple-element.30) | copy-start | bytes 1572868
  58.9 9.6 %collective-permute-start.4 = (f32[2,256,256]{2,1,0:T(8,128)S(1)}, f32[2,256,256]{2,1,0:T(8,128)S(1)}, u32[]{:S(2)}, u32[]{:S(2)}) collective-permute-start(f32[2,256,256]{2,1,0:T(8,128)S(1)} %copy-done.9), channel_id=1, source_target_pairs={{0,1},{1,2},{2,3},{3,4},{4,5},{5,6},{6,7},{7,8},{8,9},{9,10},{10,1... | collective-permute-start | bytes 1572872 | tf_op jit(solution)/shard_map/ppermute | solution.py:611
  62.5 14.6 %collective-permute-start.5 = (f32[2,256,256]{2,1,0:T(8,128)S(1)}, f32[2,256,256]{2,1,0:T(8,128)S(1)}, u32[]{:S(2)}, u32[]{:S(2)}) collective-permute-start(f32[2,256,256]{2,1,0:T(8,128)S(1)} %joined.3), channel_id=1, source_target_pairs={{0,32},{32,64},{64,96},{96,128},{128,160},{160,192},{192,224},{224... | collective-permute-start | bytes 1572872 | tf_op jit(solution)/shard_map/ppermute | solution.py:611
  77.2 49.0 %copy-start.5 = (f32[2,256,256]{2,1,0:T(8,128)}, f32[2,256,256]{2,1,0:T(8,128)S(1)}, u32[]{:S(2)}) copy-start(f32[2,256,256]{2,1,0:T(8,128)S(1)} %get-tuple-element.56.own_any) | copy-start | bytes 1572868
  77.2 21.4 %collective-permute-start.8 = (f32[2,256,256]{2,1,0:T(8,128)S(1)}, f32[2,256,256]{2,1,0:T(8,128)S(1)}, u32[]{:S(2)}, u32[]{:S(2)}) collective-permute-start(f32[2,256,256]{2,1,0:T(8,128)S(1)} %get-tuple-element.56.own_any), channel_id=1, source_target_pairs={{32,0},{64,32},{96,64},{128,96},{160,128},{192,160},{224,192},{256... | collective-permute-start | bytes 1572872 | tf_op jit(solution)/shard_map/ppermute | solution.py:611
  78.5 20.2 %collective-permute-start.9 = (f32[2,256,256]{2,1,0:T(8,128)S(1)}, f32[2,256,256]{2,1,0:T(8,128)}, u32[]{:S(2)}, u32[]{:S(2)}) collective-permute-start(f32[2,256,256]{2,1,0:T(8,128)S(1)} %get-tuple-element.56.own_any), channel_id=1, source_target_pairs={{1,0},{2,1},{3,2},{4,3},{5,4},{6,5},{7,6},{8,7},{9,8},{10,9},{11,1... | collective-permute-start | bytes 1572872 | tf_op jit(solution)/shard_map/ppermute | solution.py:611
  81.3 26.6 %all-to-all-start.1 = ((f32[8,18,128]{2,1,0:T(8,128)}), f32[8,18,128]{2,1,0:T(8,128)S(1)}, u32[]{:S(2)}, u32[]{:S(2)}) async-start(f32[8,18,128]{2,1,0:T(8,128)} %broadcast_in_dim.16), calls=%async_computation.1 | async-start | bytes 196608 | tf_op jit(solution)/shard_map/all_to_all | solution.py:624
  94.7 31.4 %collective-permute-start.11 = (f32[2,256,256]{2,1,0:T(8,128)}, f32[2,256,256]{2,1,0:T(8,128)S(1)}, u32[]{:S(2)}, u32[]{:S(2)}) collective-permute-start(f32[2,256,256]{2,1,0:T(8,128)} %collective-permute-done.6.prev_below_any), channel_id=1, source_target_pairs={{1,0},{2,1},{3,2},{4,3},{5,4},{6,5},{7,6},{8,7},{9,8},{10,9},{11,1... | collective-permute-start | bytes 1572872 | tf_op jit(solution)/shard_map/ppermute | solution.py:611
  98.6 27.6 %copy-start.8 = (f32[2,256,256]{2,1,0:T(8,128)}, f32[2,256,256]{2,1,0:T(8,128)S(1)}, u32[]{:S(2)}) copy-start(f32[2,256,256]{2,1,0:T(8,128)S(1)} %collective-permute-done.8.below_any) | copy-start | bytes 1572868
  107.9 19.1 %collective-permute-start.10 = (f32[2,256,256]{2,1,0:T(8,128)S(1)}, f32[2,256,256]{2,1,0:T(8,128)S(1)}, u32[]{:S(2)}, u32[]{:S(2)}) collective-permute-start(f32[2,256,256]{2,1,0:T(8,128)S(1)} %collective-permute-done.8.below_any), channel_id=1, source_target_pairs={{1,0},{2,1},{3,2},{4,3},{5,4},{6,5},{7,6},{8,7},{9,8},{10,9},{11,1... | collective-permute-start | bytes 1572872 | tf_op jit(solution)/shard_map/ppermute | solution.py:611
  113.6 25.3 %all-to-all-start.2 = ((f32[64,18,1,128]{3,2,1,0:T(1,128)}), f32[64,18,1,128]{3,2,1,0:T(1,128)S(1)}, u32[]{:S(2)}, u32[]{:S(2)}) async-start(f32[64,18,1,128]{3,2,1,0:T(1,128)} %broadcast_in_dim.34), calls=%async_computation.2 | async-start | bytes 1179648 | tf_op jit(solution)/shard_map/all_to_all | solution.py:624
  126.2 0.8 copy-start
  127.1 0.8 copy-start.1
  138.9 0.8 copy-start.3

commit v8 on v7

--- a/solution.py
+++ b/solution.py
@@ -133,8 +133,7 @@
     right_table_any,
     own_grad_any,
     below_grad_any,
-    right_grad_any,
-    diag_grad_any,
+    side_grad_any,
     probe_grad_any,
     patch_any,
     moved_any,
@@ -243,7 +242,8 @@
 
     both(0)
     pl.when(live > 2)(lambda: both(2))
-    outs = [own_grad_any, below_grad_any, right_grad_any, diag_grad_any, probe_grad_any]
+    sides = [side_grad_any.at[:, pl.ds(first, width)] for first in (0, width)]
+    outs = [own_grad_any, below_grad_any, *sides, probe_grad_any]
     made = [grads_ref.at[at] for at in range(4)] + [probe_sum_ref]
     for copy in outgoing(made, outs, out_sems):
         copy.wait()
@@ -296,6 +296,11 @@
 def joined_kernel(*refs):
     *sources, out_any, held_ref, in_sems, out_sem = refs
     count = len(sources)
+    width = held_ref.shape[-1]
+    sources = [
+        source if source.shape[1] == width else source.at[:, pl.ds(width, width)]
+        for source in sources
+    ]
     arrivals = incoming(sources, [held_ref.at[at] for at in range(count)], in_sems)
     for arrival in arrivals:
         arrival()
@@ -517,11 +522,11 @@
     frames = buffer(slots, 2, width, width)
     return pl.pallas_call(
         gradient_kernel,
-        out_shape=(shaped(2, width, width),) * 4
-        + (shaped(4 * width, width // 2),)
+        out_shape=(shaped(2, width, width),) * 2
+        + (shaped(2, 2 * width, width), shaped(4 * width, width // 2))
         + (shaped(slots, 2, width, width),) * 3,
         in_specs=in_smem(2) + anywhere(4) + in_hbm(4),
-        out_specs=(*anywhere(5), *in_hbm(3)),
+        out_specs=(*anywhere(4), *in_hbm(3)),
         scratch_shapes=[
             buffer(4, 2, width, width),
             buffer(2, width, width),
@@ -655,7 +660,7 @@
     prev_below = passed_along(prev, "row", -1)
     prev_right = passed_along(prev, "col", -1)
 
-    own_grad, below_grad, right_grad, diag_grad, probe_part, *kept = gradient_call(
+    own_grad, below_grad, side_grad, probe_part, *kept = gradient_call(
         positions,
         counts,
         (object_field, below, right, diag),
@@ -663,17 +668,16 @@
         intensities,
         tables,
     )
-    probe_part, prev_below, prev_right = lax.optimization_barrier(
-        (probe_part, prev_below, prev_right)
-    )
-    from_left_corner = passed_along(diag_grad, "col", 1)
+    side_grad, probe_part, prev_below, prev_right = lax.optimization_barrier(
+        (side_grad, probe_part, prev_below, prev_right)
+    )
+    from_left = passed_along(side_grad, "col", 1)
     pieces = exchanged(probe_part.reshape((len(near[0]), -1, width // 2)), near)
-    below_sum = joined_call((below_grad, from_left_corner), 10**10)
+    below_sum = joined_call((below_grad, from_left), 10**10)
     from_above = passed_along(below_sum, "row", 1)
-    from_left = passed_along(held(right_grad, below_sum), "col", 1)
-    prev_diag = passed_along(held(prev_below, diag_grad), "col", -1)
+    prev_diag = passed_along(held(prev_below, side_grad), "col", -1)
     prev_diag = joined_call((prev_diag,), 10**9)
-    object_grad = own_grad + from_left + from_above
+    object_grad = own_grad + from_left[:, :width] + from_above
     sums = [
         jnp.sum(jnp.sum(object_grad * other, axis=(0, 1)).reshape(2, -1), axis=0, keepdims=True)
         for other in (object_grad, object_dir_prev)
@@ -681,9 +685,8 @@
     payload = copies(jnp.concatenate([jnp.sum(pieces, axis=0), *sums], axis=0), apart)
     grad_below = passed_along(object_grad, "row", -1)
     grad_right = passed_along(object_grad, "col", -1)
-    payload, grad_below, grad_right = lax.optimization_barrier(
-        (exchanged(payload, apart), grad_below, grad_right)
-    )
+    payload, grad_below = lax.optimization_barrier((exchanged(payload, apart), grad_below))
+    grad_right = joined_call((grad_right,), 10**9)
     grad_diag = passed_along(grad_below, "col", -1)
     grad_diag = joined_call((grad_diag,), 2 * 10**10)
     payload = jnp.sum(payload, axis=0)[:, None, :]

time: 179 us -> 179 us (level)
  waiting for transfers between devices: 35.6 us -> 31.7 us
  blocking collectives: 26.8 us -> 29.5 us
    all_to_all x3, waiting for transfers between devices: 20.1 us -> 17.1 us  [exchanged(): lax.all_to_all(pieces, ('row', 'col'), 0, 0, axis_index_groups=groups)]
    ppermute x12 -> x11, starting transfers between devices: 43 us -> 45.9 us  [passed_along(): return lax.ppermute(shard, axis, pairs)]
    all_to_all x2, blocking collectives: 26.8 us -> 29.5 us  [exchanged(): lax.all_to_all(pieces, ('row', 'col'), 0, 0, axis_index_groups=groups)]
    ppermute x12 -> x11, waiting for transfers between devices: 15.5 us -> 14.5 us  [passed_along(): return lax.ppermute(shard, axis, pairs)]
    unnamed x27 -> x29, local copies, waits for them, and re-layouts: 6.49 us -> 6.99 us
  transfers between devices with their start and end apart: 15 -> 14, of which waited for: 6 -> 6; matrix products, arithmetic and copies ran while one was open for 2% -> 2% of each run, Pallas kernels for 5% -> 6%
where the time goes in v8:
time: 179 us; the launch traced here: 178 us
  starting transfers between devices  85.4 us (48%)
  waiting for transfers between devices  31.7 us (18%)
  blocking collectives  29.5 us (16%)
  Pallas kernels  20.3 us (11%)
  local copies, waits for them, and re-layouts  9.45 us (5%)
    ppermute x11, starting transfers between devices, passed_along(): return lax.ppermute(shard, axis, pairs)  45.9 us
    all_to_all x3, starting transfers between devices, exchanged(): lax.all_to_all(pieces, ('row', 'col'), 0, 0, axis_index_groups=groups)  39.5 us
    all_to_all x2, blocking collectives, exchanged(): lax.all_to_all(pieces, ('row', 'col'), 0, 0, axis_index_groups=groups)  29.5 us
    all_to_all x3, waiting for transfers between devices, exchanged(): lax.all_to_all(pieces, ('row', 'col'), 0, 0, axis_index_groups=groups)  17.1 us
    ppermute x11, waiting for transfers between devices, passed_along(): return lax.ppermute(shard, axis, pairs)  14.5 us
    pallas_call x1, Pallas kernels, gradient_call(): pl.pallas_call(gradient_kernel, out_shape=(shaped(2, width, width),) * 2...  9.41 us
    pallas_call x1, Pallas kernels, curvature_call(): pl.pallas_call(functools.partial(curvature_kernel, probe_scale=scale, pie...  7.46 us
    unnamed x29, local copies, waits for them, and re-layouts  6.99 us
  transfers between devices with their start and end apart: 14, of which 6 were waited for; matrix products, arithmetic and copies ran while one was open for 2% of the time, Pallas kernels for 6%

profile of v8, /device:TPU:1, one launch (start us, length us, event | category | flops | bytes accessed | tf_op | source)
XLA Modules:
  0.0 178.5 jit_solution(3393522233745354685)
XLA Ops:
  0.6 1.3 collective-permute-start
  1.9 8.8 %collective-permute-start.1 = (f32[2,256,256]{2,1,0:T(8,128)}, f32[2,256,256]{2,1,0:T(8,128)S(1)}, u32[]{:S(2)}, u32[]{:S(2)}) collective-permute-start(f32[2,256,256]{2,1,0:T(8,128)} %object_any.1), channel_id=1, source_target_pairs={{1,0},{2,1},{3,2},{4,3},{5,4},{6,5},{7,6},{8,7},{9,8},{10,9},{11,1... | collective-permute-start | bytes 1572872 | tf_op jit(solution)/shard_map/ppermute | solution.py:616
  10.7 0.7 collective-permute-done.below_any
  11.4 9.3 %collective-permute-start.2 = (f32[2,256,256]{2,1,0:T(8,128)S(1)}, f32[2,256,256]{2,1,0:T(8,128)S(1)}, u32[]{:S(2)}, u32[]{:S(2)}) collective-permute-start(f32[2,256,256]{2,1,0:T(8,128)S(1)} %collective-permute-done.below_any), channel_id=1, source_target_pairs={{1,0},{2,1},{3,2},{4,3},{5,4},{6,5},{7,6},{8,7},{9,8},{10,9},{11,1... | collective-permute-start | bytes 1572872 | tf_op jit(solution)/shard_map/ppermute | solution.py:616
  20.7 1.3 copy.25.positions_ref
  22.0 1.9 %collective-permute-start.4 = (f32[2,256,256]{2,1,0:T(8,128)}, f32[2,256,256]{2,1,0:T(8,128)S(1)}, u32[]{:S(2)}, u32[]{:S(2)}) collective-permute-start(f32[2,256,256]{2,1,0:T(8,128)} %prev_own_any.1), channel_id=1, source_target_pairs={{1,0},{2,1},{3,2},{4,3},{5,4},{6,5},{7,6},{8,7},{9,8},{10,9},{11,1... | collective-permute-start | bytes 1572872 | tf_op jit(solution)/shard_map/ppermute | solution.py:616
  24.0 1.3 collective-permute-start.3
  25.3 3.2 %collective-permute-done.2.diag_any = f32[2,256,256]{2,1,0:T(8,128)S(1)} collective-permute-done((f32[2,256,256]{2,1,0:T(8,128)S(1)}, f32[2,256,256]{2,1,0:T(8,128)S(1)}, u32[]{:S(2)}, u32[]{:S(2)}) %collective-permute-start.2) | collective-permute-done | bytes 524320 | tf_op jit(solution)/shard_map/ppermute | solution.py:616
  28.5 0.8 copy-done.13
  29.3 9.4 %gradient_frames.1 = (f32[2,256,256]{2,1,0:T(8,128)}, f32[2,256,256]{2,1,0:T(8,128)}, f32[2,512,256]{2,1,0:T(8,128)}, f32[1024,128]{1,0:T(8,128)}, f32[4,2,256,2...) custom-call(s32[1,1,4,2]{3,2,1,0:T(4,128)} %copy.25.positions_ref, s32[1,32]{1,0:T(1,128)} %counts_ref.3, ...), custom_call_target="tpu_custom_call" | custom-call | flops 10000000000 | bytes 10000000 | tf_op jit(solution)/shard_map/gradient_frames/pallas_call | solution.py:523
  39.5 3.4 %collective-permute-start.5 = (f32[2,512,256]{2,1,0:T(8,128)}, f32[2,512,256]{2,1,0:T(8,128)S(1)}, u32[]{:S(2)}, u32[]{:S(2)}) collective-permute-start(f32[2,512,256]{2,1,0:T(8,128)} %get-tuple-element.32), channel_id=1, source_target_pairs={{0,1},{1,2},{2,3},{3,4},{4,5},{5,6},{6,7},{7,8},{8,9},{9,10},{10,1... | collective-permute-start | bytes 3145736 | tf_op jit(solution)/shard_map/ppermute | solution.py:616
  42.9 13.2 %all-to-all-start = ((f32[64,16,128]{2,1,0:T(8,128)}), f32[64,16,128]{2,1,0:T(8,128)S(1)}, u32[]{:S(2)}, u32[]{:S(2)}) async-start(f32[64,16,128]{2,1,0:T(8,128)} %bitcast.14), calls=%async_computation | async-start | bytes 1048576 | tf_op jit(solution)/shard_map/all_to_all | solution.py:629
  56.1 1.0 copy-done.3
  57.4 7.4 %collective-permute-start.6 = (f32[2,256,256]{2,1,0:T(8,128)S(1)}, f32[2,256,256]{2,1,0:T(8,128)S(1)}, u32[]{:S(2)}, u32[]{:S(2)}) collective-permute-start(f32[2,256,256]{2,1,0:T(8,128)S(1)} %joined.4), channel_id=1, source_target_pairs={{0,32},{32,64},{64,96},{96,128},{128,160},{160,192},{192,224},{224... | collective-permute-start | bytes 1572872 | tf_op jit(solution)/shard_map/ppermute | solution.py:616
  64.7 10.4 %collective-permute-done.6 = f32[2,256,256]{2,1,0:T(8,128)S(1)} collective-permute-done((f32[2,256,256]{2,1,0:T(8,128)S(1)}, f32[2,256,256]{2,1,0:T(8,128)S(1)}, u32[]{:S(2)}, u32[]{:S(2)}) %collective-permute-start.6) | collective-permute-done | bytes 524320 | tf_op jit(solution)/shard_map/ppermute | solution.py:616
  75.4 1.3 collective-permute-start.7
  77.4 13.7 %all-to-all-start.1 = ((f32[8,18,128]{2,1,0:T(8,128)}), f32[8,18,128]{2,1,0:T(8,128)S(1)}, u32[]{:S(2)}, u32[]{:S(2)}) async-start(f32[8,18,128]{2,1,0:T(8,128)} %broadcast_in_dim.16), calls=%async_computation.1 | async-start | bytes 196608 | tf_op jit(solution)/shard_map/all_to_all | solution.py:629
  91.1 3.6 %collective-permute-start.10 = (f32[2,256,256]{2,1,0:T(8,128)S(1)}, f32[2,256,256]{2,1,0:T(8,128)S(1)}, u32[]{:S(2)}, u32[]{:S(2)}) collective-permute-start(f32[2,256,256]{2,1,0:T(8,128)S(1)} %collective-permute-done.3.prev_below_any), channel_id=1, source_target_pairs={{1,0},{2,1},{3,2},{4,3},{5,4},{6,5},{7,6},{8,7},{9,8},{10,9},{11,1... | collective-permute-start | bytes 1572872 | tf_op jit(solution)/shard_map/ppermute | solution.py:616
  94.7 2.1 %collective-permute-start.8 = (f32[2,256,256]{2,1,0:T(8,128)S(1)}, f32[2,256,256]{2,1,0:T(8,128)S(1)}, u32[]{:S(2)}, u32[]{:S(2)}) collective-permute-start(f32[2,256,256]{2,1,0:T(8,128)S(1)} %get-tuple-element.52.own_any), channel_id=1, source_target_pairs={{1,0},{2,1},{3,2},{4,3},{5,4},{6,5},{7,6},{8,7},{9,8},{10,9},{11,1... | collective-permute-start | bytes 1572872 | tf_op jit(solution)/shard_map/ppermute | solution.py:616
  96.9 0.8 copy-done.10
  97.7 6.3 %all-to-all-done.1 = f32[8,18,128]{2,1,0:T(8,128)S(1)} async-done(((f32[8,18,128]{2,1,0:T(8,128)}), f32[8,18,128]{2,1,0:T(8,128)S(1)}, u32[]{:S(2)}, u32[]{:S(2)}) %all-to-all-start.1) | async-done | bytes 73760 | tf_op jit(solution)/shard_map/all_to_all | solution.py:629
  103.9 5.6 %collective-permute-start.9 = (f32[2,256,256]{2,1,0:T(8,128)}, f32[2,256,256]{2,1,0:T(8,128)S(1)}, u32[]{:S(2)}, u32[]{:S(2)}) collective-permute-start(f32[2,256,256]{2,1,0:T(8,128)} %copy-done.10), channel_id=1, source_target_pairs={{1,0},{2,1},{3,2},{4,3},{5,4},{6,5},{7,6},{8,7},{9,8},{10,9},{11,1... | collective-permute-start | bytes 1572872 | tf_op jit(solution)/shard_map/ppermute | solution.py:616
  109.5 1.2 broadcast_in_dim.34
  110.7 12.7 %all-to-all-start.2 = ((f32[64,18,1,128]{3,2,1,0:T(1,128)}), f32[64,18,1,128]{3,2,1,0:T(1,128)S(1)}, u32[]{:S(2)}, u32[]{:S(2)}) async-start(f32[64,18,1,128]{3,2,1,0:T(1,128)} %broadcast_in_dim.34), calls=%async_computation.2 | async-start | bytes 1179648 | tf_op jit(solution)/shard_map/all_to_all | solution.py:629
  124.3 0.7 copy-done
  125.1 0.8 copy-done.2
  126.0 10.9 %all-to-all-done.2 = f32[64,18,1,128]{3,2,1,0:T(1,128)S(1)} async-done(((f32[64,18,1,128]{3,2,1,0:T(1,128)}), f32[64,18,1,128]{3,2,1,0:T(1,128)S(1)}, u32[]{:S(2)}, u32[]{:S(2)}) %all-to-all-start.2) | async-done | bytes 589856 | tf_op jit(solution)/shard_map/all_to_all | solution.py:629
  136.8 0.8 copy-done.4
  137.7 7.5 %curvature_frames.1 = (f32[2,256,256]{2,1,0:T(8,128)}, f32[2,256,256]{2,1,0:T(8,128)}, f32[1,128]{1,0:T(1,128)}) custom-call(s32[1,1,4,2]{3,2,1,0:T(4,128)} %copy.25.positions_ref, s32[1,32]{1,0:T(1,128)} %counts_ref.3, f32[1]{0:T(128)} %bitcast.12.prev_norm_ref, f32[2,256,256]{2,1,0:T(8,128)} %copy-done.6, f32[2,256,256]{2,1,0:T(8,128)} %copy-done.10, ...), custom_call_target="tpu_custom_call" | custom-call | flops 5000000000 | bytes 10000000 | tf_op jit(solution)/shard_map/curvature_frames/pallas_call | solution.py:570
  145.8 12.5 %all_to_all.25 = f32[32,1,128]{2,1,0:T(1,128)S(1)} all-to-all(f32[32,1,128]{2,1,0:T(1,128)S(1)} %broadcast_in_dim.36), channel_id=1, replica_groups={{0,1,32,33,64,65,96,97,128,129,160,161,192,193,224,225,256,257,288,289,..., dimensions={0} | all-to-all | bytes 32768 | tf_op jit(solution)/shard_map/all_to_all | solution.py:629
  158.3 17.1 %all_to_all.26.gathered_any = f32[16,1,128]{2,1,0:T(1,128)} all-to-all(f32[16,1,128]{2,1,0:T(1,128)S(1)} %broadcast_in_dim.37), channel_id=1, replica_groups={{0,2,4,6,8,10,12,14,16,18,20,22,24,26,28,30},{1,3,5,7,9,11,13,15,17,19,..., dimensions={0} | all-to-all | bytes 16384 | tf_op jit(solution)/shard_map/all_to_all | solution.py:629
  175.4 3.0 %update.1 = (f32[2,256,256]{2,1,0:T(8,128)}, f32[2,256,256]{2,1,0:T(8,128)}, f32[1,1]{1,0:T(1,128)}, f32[1,1,4]{2,1,0:T(1,128)}) custom-call(f32[16,1,128]{2,1,0:T(1,128)} %all_to_all.26.gathered_any, f32[1,128]{1,0:T(1,128)} %get-tuple-element.43.sums_any, f32[2,256,256]{2,1,0:T(8,128)} %object_any.1, f32[2,256,256]{2,1,0:T(8,128)} %get-tuple-element.24.direction_any, ...), custom_call_target="tpu_custom_call" | custom-call | flops 1000000 | bytes 10000000 | tf_op jit(solution)/shard_map/update/pallas_call | solution.py:596
  (44 shorter events, 3.0 us)
Async XLA Ops:
  0.6 10.8 %collective-permute-start = (f32[2,256,256]{2,1,0:T(8,128)}, f32[2,256,256]{2,1,0:T(8,128)S(1)}, u32[]{:S(2)}, u32[]{:S(2)}) collective-permute-start(f32[2,256,256]{2,1,0:T(8,128)} %object_any.1), channel_id=1, source_target_pairs={{32,0},{64,32},{96,64},{128,96},{160,128},{192,160},{224,192},{256... | collective-permute-start | bytes 1572872 | tf_op jit(solution)/shard_map/ppermute | solution.py:616
  1.9 23.3 %collective-permute-start.1 = (f32[2,256,256]{2,1,0:T(8,128)}, f32[2,256,256]{2,1,0:T(8,128)S(1)}, u32[]{:S(2)}, u32[]{:S(2)}) collective-permute-start(f32[2,256,256]{2,1,0:T(8,128)} %object_any.1), channel_id=1, source_target_pairs={{1,0},{2,1},{3,2},{4,3},{5,4},{6,5},{7,6},{8,7},{9,8},{10,9},{11,1... | collective-permute-start | bytes 1572872 | tf_op jit(solution)/shard_map/ppermute | solution.py:616
  11.4 17.0 %copy-start.11 = (f32[2,256,256]{2,1,0:T(8,128)}, f32[2,256,256]{2,1,0:T(8,128)S(1)}, u32[]{:S(2)}) copy-start(f32[2,256,256]{2,1,0:T(8,128)S(1)} %collective-permute-done.below_any) | copy-start | bytes 1572868
  11.4 17.0 %collective-permute-start.2 = (f32[2,256,256]{2,1,0:T(8,128)S(1)}, f32[2,256,256]{2,1,0:T(8,128)S(1)}, u32[]{:S(2)}, u32[]{:S(2)}) collective-permute-start(f32[2,256,256]{2,1,0:T(8,128)S(1)} %collective-permute-done.below_any), channel_id=1, source_target_pairs={{1,0},{2,1},{3,2},{4,3},{5,4},{6,5},{7,6},{8,7},{9,8},{10,9},{11,1... | collective-permute-start | bytes 1572872 | tf_op jit(solution)/shard_map/ppermute | solution.py:616
  22.0 16.7 %collective-permute-start.4 = (f32[2,256,256]{2,1,0:T(8,128)}, f32[2,256,256]{2,1,0:T(8,128)S(1)}, u32[]{:S(2)}, u32[]{:S(2)}) collective-permute-start(f32[2,256,256]{2,1,0:T(8,128)} %prev_own_any.1), channel_id=1, source_target_pairs={{1,0},{2,1},{3,2},{4,3},{5,4},{6,5},{7,6},{8,7},{9,8},{10,9},{11,1... | collective-permute-start | bytes 1572872 | tf_op jit(solution)/shard_map/ppermute | solution.py:616
  24.0 15.0 %collective-permute-start.3 = (f32[2,256,256]{2,1,0:T(8,128)}, f32[2,256,256]{2,1,0:T(8,128)S(1)}, u32[]{:S(2)}, u32[]{:S(2)}) collective-permute-start(f32[2,256,256]{2,1,0:T(8,128)} %prev_own_any.1), channel_id=1, source_target_pairs={{32,0},{64,32},{96,64},{128,96},{160,128},{192,160},{224,192},{256... | collective-permute-start | bytes 1572872 | tf_op jit(solution)/shard_map/ppermute | solution.py:616
  25.3 3.2 %copy-start.12 = (f32[2,256,256]{2,1,0:T(8,128)}, f32[2,256,256]{2,1,0:T(8,128)S(1)}, u32[]{:S(2)}) copy-start(f32[2,256,256]{2,1,0:T(8,128)S(1)} %collective-permute-done.1.right_any) | copy-start | bytes 1572868
  28.5 0.8 copy-start.13
  38.7 0.8 copy-start.8
  38.9 52.2 %copy-start.9 = (f32[2,256,256]{2,1,0:T(8,128)}, f32[2,256,256]{2,1,0:T(8,128)S(1)}, u32[]{:S(2)}) copy-start(f32[2,256,256]{2,1,0:T(8,128)S(1)} %collective-permute-done.3.prev_below_any) | copy-start | bytes 1572868
  39.5 16.6 %collective-permute-start.5 = (f32[2,512,256]{2,1,0:T(8,128)}, f32[2,512,256]{2,1,0:T(8,128)S(1)}, u32[]{:S(2)}, u32[]{:S(2)}) collective-permute-start(f32[2,512,256]{2,1,0:T(8,128)} %get-tuple-element.32), channel_id=1, source_target_pairs={{0,1},{1,2},{2,3},{3,4},{4,5},{5,6},{6,7},{7,8},{8,9},{9,10},{10,1... | collective-permute-start | bytes 3145736 | tf_op jit(solution)/shard_map/ppermute | solution.py:616
  42.9 33.7 %all-to-all-start = ((f32[64,16,128]{2,1,0:T(8,128)}), f32[64,16,128]{2,1,0:T(8,128)S(1)}, u32[]{:S(2)}, u32[]{:S(2)}) async-start(f32[64,16,128]{2,1,0:T(8,128)} %bitcast.14), calls=%async_computation | async-start | bytes 1048576 | tf_op jit(solution)/shard_map/all_to_all | solution.py:629
  56.1 1.0 copy-start.3
  57.2 18.0 %copy-start.5 = (f32[2,256,256]{2,1,0:T(8,128)S(1)}, f32[2,256,256]{2,1,0:T(8,128)}, u32[]{:S(2)}) copy-start(f32[2,256,256]{2,1,0:T(8,128)} %prev_own_any.1) | copy-start | bytes 1572868
  57.2 18.0 %copy-start.7 = (f32[2,256,256]{2,1,0:T(8,128)S(1)}, f32[2,256,256]{2,1,0:T(8,128)}, u32[]{:S(2)}) copy-start(f32[2,256,256]{2,1,0:T(8,128)} %get-tuple-element.28) | copy-start | bytes 1572868
  57.4 17.8 %collective-permute-start.6 = (f32[2,256,256]{2,1,0:T(8,128)S(1)}, f32[2,256,256]{2,1,0:T(8,128)S(1)}, u32[]{:S(2)}, u32[]{:S(2)}) collective-permute-start(f32[2,256,256]{2,1,0:T(8,128)S(1)} %joined.4), channel_id=1, source_target_pairs={{0,32},{32,64},{64,96},{96,128},{128,160},{160,192},{192,224},{224... | collective-permute-start | bytes 1572872 | tf_op jit(solution)/shard_map/ppermute | solution.py:616
  75.4 48.8 %copy-start.6 = (f32[2,256,256]{2,1,0:T(8,128)}, f32[2,256,256]{2,1,0:T(8,128)S(1)}, u32[]{:S(2)}) copy-start(f32[2,256,256]{2,1,0:T(8,128)S(1)} %get-tuple-element.52.own_any) | copy-start | bytes 1572868
  75.4 21.5 %collective-permute-start.7 = (f32[2,256,256]{2,1,0:T(8,128)S(1)}, f32[2,256,256]{2,1,0:T(8,128)S(1)}, u32[]{:S(2)}, u32[]{:S(2)}) collective-permute-start(f32[2,256,256]{2,1,0:T(8,128)S(1)} %get-tuple-element.52.own_any), channel_id=1, source_target_pairs={{32,0},{64,32},{96,64},{128,96},{160,128},{192,160},{224,192},{256... | collective-permute-start | bytes 1572872 | tf_op jit(solution)/shard_map/ppermute | solution.py:616
  77.4 26.5 %all-to-all-start.1 = ((f32[8,18,128]{2,1,0:T(8,128)}), f32[8,18,128]{2,1,0:T(8,128)S(1)}, u32[]{:S(2)}, u32[]{:S(2)}) async-start(f32[8,18,128]{2,1,0:T(8,128)} %broadcast_in_dim.16), calls=%async_computation.1 | async-start | bytes 196608 | tf_op jit(solution)/shard_map/all_to_all | solution.py:629
  91.1 32.9 %collective-permute-start.10 = (f32[2,256,256]{2,1,0:T(8,128)S(1)}, f32[2,256,256]{2,1,0:T(8,128)S(1)}, u32[]{:S(2)}, u32[]{:S(2)}) collective-permute-start(f32[2,256,256]{2,1,0:T(8,128)S(1)} %collective-permute-done.3.prev_below_any), channel_id=1, source_target_pairs={{1,0},{2,1},{3,2},{4,3},{5,4},{6,5},{7,6},{8,7},{9,8},{10,9},{11,1... | collective-permute-start | bytes 1572872 | tf_op jit(solution)/shard_map/ppermute | solution.py:616
  94.7 29.4 %collective-permute-start.8 = (f32[2,256,256]{2,1,0:T(8,128)S(1)}, f32[2,256,256]{2,1,0:T(8,128)S(1)}, u32[]{:S(2)}, u32[]{:S(2)}) collective-permute-start(f32[2,256,256]{2,1,0:T(8,128)S(1)} %get-tuple-element.52.own_any), channel_id=1, source_target_pairs={{1,0},{2,1},{3,2},{4,3},{5,4},{6,5},{7,6},{8,7},{9,8},{10,9},{11,1... | collective-permute-start | bytes 1572872 | tf_op jit(solution)/shard_map/ppermute | solution.py:616
  96.9 0.8 copy-start.10
  103.9 20.3 %collective-permute-start.9 = (f32[2,256,256]{2,1,0:T(8,128)}, f32[2,256,256]{2,1,0:T(8,128)S(1)}, u32[]{:S(2)}, u32[]{:S(2)}) collective-permute-start(f32[2,256,256]{2,1,0:T(8,128)} %copy-done.10), channel_id=1, source_target_pairs={{1,0},{2,1},{3,2},{4,3},{5,4},{6,5},{7,6},{8,7},{9,8},{10,9},{11,1... | collective-permute-start | bytes 1572872 | tf_op jit(solution)/shard_map/ppermute | solution.py:616
  110.7 26.2 %all-to-all-start.2 = ((f32[64,18,1,128]{3,2,1,0:T(1,128)}), f32[64,18,1,128]{3,2,1,0:T(1,128)S(1)}, u32[]{:S(2)}, u32[]{:S(2)}) async-start(f32[64,18,1,128]{3,2,1,0:T(1,128)} %broadcast_in_dim.34), calls=%async_computation.2 | async-start | bytes 1179648 | tf_op jit(solution)/shard_map/all_to_all | solution.py:629
  124.1 0.8 copy-start
  124.3 0.9 copy-start.1
  125.1 0.9 copy-start.2
  136.8 0.8 copy-start.4

commit v9 on v8

--- a/solution.py
+++ b/solution.py
@@ -675,14 +675,14 @@
     pieces = exchanged(probe_part.reshape((len(near[0]), -1, width // 2)), near)
     below_sum = joined_call((below_grad, from_left), 10**10)
     from_above = passed_along(below_sum, "row", 1)
-    prev_diag = passed_along(held(prev_below, side_grad), "col", -1)
-    prev_diag = joined_call((prev_diag,), 10**9)
+    prev_diag = passed_along(held(prev_below, below_sum), "col", -1)
     object_grad = own_grad + from_left[:, :width] + from_above
     sums = [
         jnp.sum(jnp.sum(object_grad * other, axis=(0, 1)).reshape(2, -1), axis=0, keepdims=True)
         for other in (object_grad, object_dir_prev)
     ]
     payload = copies(jnp.concatenate([jnp.sum(pieces, axis=0), *sums], axis=0), apart)
+    object_grad, prev_diag = lax.optimization_barrier((object_grad, prev_diag))
     grad_below = passed_along(object_grad, "row", -1)
     grad_right = passed_along(object_grad, "col", -1)
     payload, grad_below = lax.optimization_barrier((exchanged(payload, apart), grad_below))

time: 179 us -> 176 us (0.983)
  waiting for transfers between devices: 31.7 us -> 35.7 us
  starting transfers between devices: 85.4 us -> 82.6 us
  blocking collectives: 29.5 us -> 26.7 us
    all_to_all x3, waiting for transfers between devices: 17.1 us -> 20.6 us  [exchanged(): lax.all_to_all(pieces, ('row', 'col'), 0, 0, axis_index_groups=groups)]
    all_to_all x2, blocking collectives: 29.5 us -> 26.7 us  [exchanged(): lax.all_to_all(pieces, ('row', 'col'), 0, 0, axis_index_groups=groups)]
    all_to_all x3, starting transfers between devices: 39.5 us -> 37.2 us  [exchanged(): lax.all_to_all(pieces, ('row', 'col'), 0, 0, axis_index_groups=groups)]
    unnamed x29 -> x25, local copies, waits for them, and re-layouts: 6.99 us -> 5.63 us
  transfers between devices with their start and end apart: 14 -> 14, of which waited for: 6 -> 7; matrix products, arithmetic and copies ran while one was open for 2% -> 2% of each run, Pallas kernels for 6% -> 6%
where the time goes in v9:
time: 176 us; the launch traced here: 175 us
  starting transfers between devices  82.6 us (47%)
  waiting for transfers between devices  35.7 us (20%)
  blocking collectives  26.7 us (15%)
  Pallas kernels  20.2 us (11%)
  local copies, waits for them, and re-layouts  8.04 us (5%)
    ppermute x11, starting transfers between devices, passed_along(): return lax.ppermute(shard, axis, pairs)  45.5 us
    all_to_all x3, starting transfers between devices, exchanged(): lax.all_to_all(pieces, ('row', 'col'), 0, 0, axis_index_groups=groups)  37.2 us
    all_to_all x2, blocking collectives, exchanged(): lax.all_to_all(pieces, ('row', 'col'), 0, 0, axis_index_groups=groups)  26.7 us
    all_to_all x3, waiting for transfers between devices, exchanged(): lax.all_to_all(pieces, ('row', 'col'), 0, 0, axis_index_groups=groups)  20.6 us
    ppermute x11, waiting for transfers between devices, passed_along(): return lax.ppermute(shard, axis, pairs)  15.1 us
    pallas_call x1, Pallas kernels, gradient_call(): pl.pallas_call(gradient_kernel, out_shape=(shaped(2, width, width),) * 2...  9.43 us
    pallas_call x1, Pallas kernels, curvature_call(): pl.pallas_call(functools.partial(curvature_kernel, probe_scale=scale, pie...  7.44 us
    unnamed x25, local copies, waits for them, and re-layouts  5.63 us
  transfers between devices with their start and end apart: 14, of which 7 were waited for; matrix products, arithmetic and copies ran while one was open for 2% of the time, Pallas kernels for 6%

profile of v9, /device:TPU:1, one launch (start us, length us, event | category | flops | bytes accessed | tf_op | source)
XLA Modules:
  0.0 175.4 jit_solution(11051969599745956137)
XLA Ops:
  0.6 1.3 collective-permute-start
  1.9 8.8 %collective-permute-start.1 = (f32[2,256,256]{2,1,0:T(8,128)}, f32[2,256,256]{2,1,0:T(8,128)S(1)}, u32[]{:S(2)}, u32[]{:S(2)}) collective-permute-start(f32[2,256,256]{2,1,0:T(8,128)} %object_any.1), channel_id=1, source_target_pairs={{1,0},{2,1},{3,2},{4,3},{5,4},{6,5},{7,6},{8,7},{9,8},{10,9},{11,1... | collective-permute-start | bytes 1572872 | tf_op jit(solution)/shard_map/ppermute | solution.py:616
  10.7 0.7 collective-permute-done.below_any
  11.4 9.3 %collective-permute-start.2 = (f32[2,256,256]{2,1,0:T(8,128)S(1)}, f32[2,256,256]{2,1,0:T(8,128)S(1)}, u32[]{:S(2)}, u32[]{:S(2)}) collective-permute-start(f32[2,256,256]{2,1,0:T(8,128)S(1)} %collective-permute-done.below_any), channel_id=1, source_target_pairs={{1,0},{2,1},{3,2},{4,3},{5,4},{6,5},{7,6},{8,7},{9,8},{10,9},{11,1... | collective-permute-start | bytes 1572872 | tf_op jit(solution)/shard_map/ppermute | solution.py:616
  20.7 1.3 copy.25.positions_ref
  22.0 1.9 %collective-permute-start.4 = (f32[2,256,256]{2,1,0:T(8,128)}, f32[2,256,256]{2,1,0:T(8,128)S(1)}, u32[]{:S(2)}, u32[]{:S(2)}) collective-permute-start(f32[2,256,256]{2,1,0:T(8,128)} %prev_own_any.1), channel_id=1, source_target_pairs={{1,0},{2,1},{3,2},{4,3},{5,4},{6,5},{7,6},{8,7},{9,8},{10,9},{11,1... | collective-permute-start | bytes 1572872 | tf_op jit(solution)/shard_map/ppermute | solution.py:616
  24.0 1.3 collective-permute-start.3
  25.3 3.3 %collective-permute-done.2.diag_any = f32[2,256,256]{2,1,0:T(8,128)S(1)} collective-permute-done((f32[2,256,256]{2,1,0:T(8,128)S(1)}, f32[2,256,256]{2,1,0:T(8,128)S(1)}, u32[]{:S(2)}, u32[]{:S(2)}) %collective-permute-start.2) | collective-permute-done | bytes 524320 | tf_op jit(solution)/shard_map/ppermute | solution.py:616
  28.6 0.8 copy-done.11
  29.4 9.4 %gradient_frames.1 = (f32[2,256,256]{2,1,0:T(8,128)}, f32[2,256,256]{2,1,0:T(8,128)}, f32[2,512,256]{2,1,0:T(8,128)}, f32[1024,128]{1,0:T(8,128)}, f32[4,2,256,2...) custom-call(s32[1,1,4,2]{3,2,1,0:T(4,128)} %copy.25.positions_ref, s32[1,32]{1,0:T(1,128)} %counts_ref.3, ...), custom_call_target="tpu_custom_call" | custom-call | flops 10000000000 | bytes 10000000 | tf_op jit(solution)/shard_map/gradient_frames/pallas_call | solution.py:523
  39.0 6.3 %collective-permute-start.5 = (f32[2,512,256]{2,1,0:T(8,128)}, f32[2,512,256]{2,1,0:T(8,128)S(1)}, u32[]{:S(2)}, u32[]{:S(2)}) collective-permute-start(f32[2,512,256]{2,1,0:T(8,128)} %get-tuple-element.34), channel_id=1, source_target_pairs={{0,1},{1,2},{2,3},{3,4},{4,5},{5,6},{6,7},{7,8},{8,9},{9,10},{10,1... | collective-permute-start | bytes 3145736 | tf_op jit(solution)/shard_map/ppermute | solution.py:616
  45.4 11.0 %all-to-all-start = ((f32[64,16,128]{2,1,0:T(8,128)}), f32[64,16,128]{2,1,0:T(8,128)S(1)}, u32[]{:S(2)}, u32[]{:S(2)}) async-start(f32[64,16,128]{2,1,0:T(8,128)} %bitcast.14), calls=%async_computation | async-start | bytes 1048576 | tf_op jit(solution)/shard_map/all_to_all | solution.py:629
  56.3 1.1 collective-permute-done.5.refs_1_
  57.4 1.0 copy-done.2
  58.7 5.0 %collective-permute-start.6 = (f32[2,256,256]{2,1,0:T(8,128)S(1)}, f32[2,256,256]{2,1,0:T(8,128)S(1)}, u32[]{:S(2)}, u32[]{:S(2)}) collective-permute-start(f32[2,256,256]{2,1,0:T(8,128)S(1)} %joined.3), channel_id=1, source_target_pairs={{0,32},{32,64},{64,96},{96,128},{128,160},{160,192},{192,224},{224... | collective-permute-start | bytes 1572872 | tf_op jit(solution)/shard_map/ppermute | solution.py:616
  63.6 1.9 %collective-permute-start.7 = (f32[2,256,256]{2,1,0:T(8,128)}, f32[2,256,256]{2,1,0:T(8,128)S(1)}, u32[]{:S(2)}, u32[]{:S(2)}) collective-permute-start(f32[2,256,256]{2,1,0:T(8,128)} %collective-permute-done.3.prev_below_any), channel_id=1, source_target_pairs={{1,0},{2,1},{3,2},{4,3},{5,4},{6,5},{7,6},{8,7},{9,8},{10,9},{11,1... | collective-permute-start | bytes 1572872 | tf_op jit(solution)/shard_map/ppermute | solution.py:616
  65.6 9.8 %collective-permute-done.6 = f32[2,256,256]{2,1,0:T(8,128)S(1)} collective-permute-done((f32[2,256,256]{2,1,0:T(8,128)S(1)}, f32[2,256,256]{2,1,0:T(8,128)S(1)}, u32[]{:S(2)}, u32[]{:S(2)}) %collective-permute-start.6) | collective-permute-done | bytes 524320 | tf_op jit(solution)/shard_map/ppermute | solution.py:616
  75.6 1.3 collective-permute-start.8
  77.6 13.6 %all-to-all-start.1 = ((f32[8,18,128]{2,1,0:T(8,128)}), f32[8,18,128]{2,1,0:T(8,128)S(1)}, u32[]{:S(2)}, u32[]{:S(2)}) async-start(f32[8,18,128]{2,1,0:T(8,128)} %broadcast_in_dim.16), calls=%async_computation.1 | async-start | bytes 196608 | tf_op jit(solution)/shard_map/all_to_all | solution.py:629
  91.3 3.2 %collective-permute-start.9 = (f32[2,256,256]{2,1,0:T(8,128)S(1)}, f32[2,256,256]{2,1,0:T(8,128)S(1)}, u32[]{:S(2)}, u32[]{:S(2)}) collective-permute-start(f32[2,256,256]{2,1,0:T(8,128)S(1)} %get-tuple-element.38.own_any), channel_id=1, source_target_pairs={{1,0},{2,1},{3,2},{4,3},{5,4},{6,5},{7,6},{8,7},{9,8},{10,9},{11,1... | collective-permute-start | bytes 1572872 | tf_op jit(solution)/shard_map/ppermute | solution.py:616
  94.5 9.7 %all-to-all-done.1 = f32[8,18,128]{2,1,0:T(8,128)S(1)} async-done(((f32[8,18,128]{2,1,0:T(8,128)}), f32[8,18,128]{2,1,0:T(8,128)S(1)}, u32[]{:S(2)}, u32[]{:S(2)}) %all-to-all-start.1) | async-done | bytes 73760 | tf_op jit(solution)/shard_map/all_to_all | solution.py:629
  104.1 5.2 %collective-permute-start.10 = (f32[2,256,256]{2,1,0:T(8,128)}, f32[2,256,256]{2,1,0:T(8,128)S(1)}, u32[]{:S(2)}, u32[]{:S(2)}) collective-permute-start(f32[2,256,256]{2,1,0:T(8,128)} %collective-permute-done.8.below_any), channel_id=1, source_target_pairs={{1,0},{2,1},{3,2},{4,3},{5,4},{6,5},{7,6},{8,7},{9,8},{10,9},{11,1... | collective-permute-start | bytes 1572872 | tf_op jit(solution)/shard_map/ppermute | solution.py:616
  109.4 1.1 broadcast_in_dim.34
  110.5 12.6 %all-to-all-start.2 = ((f32[64,18,1,128]{3,2,1,0:T(1,128)}), f32[64,18,1,128]{3,2,1,0:T(1,128)S(1)}, u32[]{:S(2)}, u32[]{:S(2)}) async-start(f32[64,18,1,128]{3,2,1,0:T(1,128)} %broadcast_in_dim.34), calls=%async_computation.2 | async-start | bytes 1179648 | tf_op jit(solution)/shard_map/all_to_all | solution.py:629
  123.9 0.8 copy-done
  124.8 0.8 copy-done.1
  125.6 11.0 %all-to-all-done.2 = f32[64,18,1,128]{3,2,1,0:T(1,128)S(1)} async-done(((f32[64,18,1,128]{3,2,1,0:T(1,128)}), f32[64,18,1,128]{3,2,1,0:T(1,128)S(1)}, u32[]{:S(2)}, u32[]{:S(2)}) %all-to-all-start.2) | async-done | bytes 589856 | tf_op jit(solution)/shard_map/all_to_all | solution.py:629
  136.6 0.8 copy-done.3
  137.4 7.4 %curvature_frames.1 = (f32[2,256,256]{2,1,0:T(8,128)}, f32[2,256,256]{2,1,0:T(8,128)}, f32[1,128]{1,0:T(1,128)}) custom-call(s32[1,1,4,2]{3,2,1,0:T(4,128)} %copy.25.positions_ref, s32[1,32]{1,0:T(1,128)} %counts_ref.3, f32[1]{0:T(128)} %bitcast.12.prev_norm_ref, f32[2,256,256]{2,1,0:T(8,128)} %copy-done.5, f32[2,256,256]{2,1,0:T(8,128)} %collective-permute-done.8.below_any, ...), custom_call_target="tpu_custom_call" | custom-call | flops 5000000000 | bytes 10000000 | tf_op jit(solution)/shard_map/curvature_frames/pallas_call | solution.py:570
  145.5 12.3 %all_to_all.25 = f32[32,1,128]{2,1,0:T(1,128)S(1)} all-to-all(f32[32,1,128]{2,1,0:T(1,128)S(1)} %broadcast_in_dim.36), channel_id=1, replica_groups={{0,1,32,33,64,65,96,97,128,129,160,161,192,193,224,225,256,257,288,289,..., dimensions={0} | all-to-all | bytes 32768 | tf_op jit(solution)/shard_map/all_to_all | solution.py:629
  157.8 14.4 %all_to_all.26.gathered_any = f32[16,1,128]{2,1,0:T(1,128)} all-to-all(f32[16,1,128]{2,1,0:T(1,128)S(1)} %broadcast_in_dim.37), channel_id=1, replica_groups={{0,2,4,6,8,10,12,14,16,18,20,22,24,26,28,30},{1,3,5,7,9,11,13,15,17,19,..., dimensions={0} | all-to-all | bytes 16384 | tf_op jit(solution)/shard_map/all_to_all | solution.py:629
  172.2 3.0 %update.1 = (f32[2,256,256]{2,1,0:T(8,128)}, f32[2,256,256]{2,1,0:T(8,128)}, f32[1,1]{1,0:T(1,128)}, f32[1,1,4]{2,1,0:T(1,128)}) custom-call(f32[16,1,128]{2,1,0:T(1,128)} %all_to_all.26.gathered_any, f32[1,128]{1,0:T(1,128)} %get-tuple-element.47.sums_any, f32[2,256,256]{2,1,0:T(8,128)} %object_any.1, f32[2,256,256]{2,1,0:T(8,128)} %get-tuple-element.26.direction_any, ...), custom_call_target="tpu_custom_call" | custom-call | flops 1000000 | bytes 10000000 | tf_op jit(solution)/shard_map/update/pallas_call | solution.py:596
  (39 shorter events, 2.2 us)
Async XLA Ops:
  0.6 10.8 %collective-permute-start = (f32[2,256,256]{2,1,0:T(8,128)}, f32[2,256,256]{2,1,0:T(8,128)S(1)}, u32[]{:S(2)}, u32[]{:S(2)}) collective-permute-start(f32[2,256,256]{2,1,0:T(8,128)} %object_any.1), channel_id=1, source_target_pairs={{32,0},{64,32},{96,64},{128,96},{160,128},{192,160},{224,192},{256... | collective-permute-start | bytes 1572872 | tf_op jit(solution)/shard_map/ppermute | solution.py:616
  1.9 23.3 %collective-permute-start.1 = (f32[2,256,256]{2,1,0:T(8,128)}, f32[2,256,256]{2,1,0:T(8,128)S(1)}, u32[]{:S(2)}, u32[]{:S(2)}) collective-permute-start(f32[2,256,256]{2,1,0:T(8,128)} %object_any.1), channel_id=1, source_target_pairs={{1,0},{2,1},{3,2},{4,3},{5,4},{6,5},{7,6},{8,7},{9,8},{10,9},{11,1... | collective-permute-start | bytes 1572872 | tf_op jit(solution)/shard_map/ppermute | solution.py:616
  11.4 17.1 %copy-start.9 = (f32[2,256,256]{2,1,0:T(8,128)}, f32[2,256,256]{2,1,0:T(8,128)S(1)}, u32[]{:S(2)}) copy-start(f32[2,256,256]{2,1,0:T(8,128)S(1)} %collective-permute-done.below_any) | copy-start | bytes 1572868
  11.4 17.1 %collective-permute-start.2 = (f32[2,256,256]{2,1,0:T(8,128)S(1)}, f32[2,256,256]{2,1,0:T(8,128)S(1)}, u32[]{:S(2)}, u32[]{:S(2)}) collective-permute-start(f32[2,256,256]{2,1,0:T(8,128)S(1)} %collective-permute-done.below_any), channel_id=1, source_target_pairs={{1,0},{2,1},{3,2},{4,3},{5,4},{6,5},{7,6},{8,7},{9,8},{10,9},{11,1... | collective-permute-start | bytes 1572872 | tf_op jit(solution)/shard_map/ppermute | solution.py:616
  22.0 16.8 %collective-permute-start.4 = (f32[2,256,256]{2,1,0:T(8,128)}, f32[2,256,256]{2,1,0:T(8,128)S(1)}, u32[]{:S(2)}, u32[]{:S(2)}) collective-permute-start(f32[2,256,256]{2,1,0:T(8,128)} %prev_own_any.1), channel_id=1, source_target_pairs={{1,0},{2,1},{3,2},{4,3},{5,4},{6,5},{7,6},{8,7},{9,8},{10,9},{11,1... | collective-permute-start | bytes 1572872 | tf_op jit(solution)/shard_map/ppermute | solution.py:616
  24.0 15.1 %collective-permute-start.3 = (f32[2,256,256]{2,1,0:T(8,128)}, f32[2,256,256]{2,1,0:T(8,128)}, u32[]{:S(2)}, u32[]{:S(2)}) collective-permute-start(f32[2,256,256]{2,1,0:T(8,128)} %prev_own_any.1), channel_id=1, source_target_pairs={{32,0},{64,32},{96,64},{128,96},{160,128},{192,160},{224,192},{256... | collective-permute-start | bytes 1572872 | tf_op jit(solution)/shard_map/ppermute | solution.py:616
  25.3 3.3 %copy-start.10 = (f32[2,256,256]{2,1,0:T(8,128)}, f32[2,256,256]{2,1,0:T(8,128)S(1)}, u32[]{:S(2)}) copy-start(f32[2,256,256]{2,1,0:T(8,128)S(1)} %collective-permute-done.1.right_any) | copy-start | bytes 1572868
  28.6 0.8 copy-start.11
  38.8 19.8 %copy-start.7 = (f32[2,256,256]{2,1,0:T(8,128)}, f32[2,256,256]{2,1,0:T(8,128)S(1)}, u32[]{:S(2)}) copy-start(f32[2,256,256]{2,1,0:T(8,128)S(1)} %collective-permute-done.4.prev_right_any) | copy-start | bytes 1572868
  39.0 18.4 %collective-permute-start.5 = (f32[2,512,256]{2,1,0:T(8,128)}, f32[2,512,256]{2,1,0:T(8,128)S(1)}, u32[]{:S(2)}, u32[]{:S(2)}) collective-permute-start(f32[2,512,256]{2,1,0:T(8,128)} %get-tuple-element.34), channel_id=1, source_target_pairs={{0,1},{1,2},{2,3},{3,4},{4,5},{5,6},{6,7},{7,8},{8,9},{9,10},{10,1... | collective-permute-start | bytes 3145736 | tf_op jit(solution)/shard_map/ppermute | solution.py:616
  45.4 31.5 %all-to-all-start = ((f32[64,16,128]{2,1,0:T(8,128)}), f32[64,16,128]{2,1,0:T(8,128)S(1)}, u32[]{:S(2)}, u32[]{:S(2)}) async-start(f32[64,16,128]{2,1,0:T(8,128)} %bitcast.14), calls=%async_computation | async-start | bytes 1048576 | tf_op jit(solution)/shard_map/all_to_all | solution.py:629
  57.4 1.0 copy-start.2
  58.5 16.9 %copy-start.4 = (f32[2,256,256]{2,1,0:T(8,128)S(1)}, f32[2,256,256]{2,1,0:T(8,128)}, u32[]{:S(2)}) copy-start(f32[2,256,256]{2,1,0:T(8,128)} %prev_own_any.1) | copy-start | bytes 1572868
  58.5 16.9 %copy-start.6 = (f32[2,256,256]{2,1,0:T(8,128)S(1)}, f32[2,256,256]{2,1,0:T(8,128)}, u32[]{:S(2)}) copy-start(f32[2,256,256]{2,1,0:T(8,128)} %get-tuple-element.30) | copy-start | bytes 1572868
  58.7 16.7 %collective-permute-start.6 = (f32[2,256,256]{2,1,0:T(8,128)S(1)}, f32[2,256,256]{2,1,0:T(8,128)S(1)}, u32[]{:S(2)}, u32[]{:S(2)}) collective-permute-start(f32[2,256,256]{2,1,0:T(8,128)S(1)} %joined.3), channel_id=1, source_target_pairs={{0,32},{32,64},{64,96},{96,128},{128,160},{160,192},{192,224},{224... | collective-permute-start | bytes 1572872 | tf_op jit(solution)/shard_map/ppermute | solution.py:616
  63.6 11.9 %collective-permute-start.7 = (f32[2,256,256]{2,1,0:T(8,128)}, f32[2,256,256]{2,1,0:T(8,128)S(1)}, u32[]{:S(2)}, u32[]{:S(2)}) collective-permute-start(f32[2,256,256]{2,1,0:T(8,128)} %collective-permute-done.3.prev_below_any), channel_id=1, source_target_pairs={{1,0},{2,1},{3,2},{4,3},{5,4},{6,5},{7,6},{8,7},{9,8},{10,9},{11,1... | collective-permute-start | bytes 1572872 | tf_op jit(solution)/shard_map/ppermute | solution.py:616
  75.5 48.3 %copy-start.5 = (f32[2,256,256]{2,1,0:T(8,128)}, f32[2,256,256]{2,1,0:T(8,128)S(1)}, u32[]{:S(2)}) copy-start(f32[2,256,256]{2,1,0:T(8,128)S(1)} %get-tuple-element.38.own_any) | copy-start | bytes 1572868
  75.6 48.3 %copy-start.8 = (f32[2,256,256]{2,1,0:T(8,128)}, f32[2,256,256]{2,1,0:T(8,128)S(1)}, u32[]{:S(2)}) copy-start(f32[2,256,256]{2,1,0:T(8,128)S(1)} %collective-permute-done.7.prev_diag_any) | copy-start | bytes 1572868
  75.6 18.9 %collective-permute-start.8 = (f32[2,256,256]{2,1,0:T(8,128)S(1)}, f32[2,256,256]{2,1,0:T(8,128)}, u32[]{:S(2)}, u32[]{:S(2)}) collective-permute-start(f32[2,256,256]{2,1,0:T(8,128)S(1)} %get-tuple-element.38.own_any), channel_id=1, source_target_pairs={{32,0},{64,32},{96,64},{128,96},{160,128},{192,160},{224,192},{256... | collective-permute-start | bytes 1572872 | tf_op jit(solution)/shard_map/ppermute | solution.py:616
  77.6 26.5 %all-to-all-start.1 = ((f32[8,18,128]{2,1,0:T(8,128)}), f32[8,18,128]{2,1,0:T(8,128)S(1)}, u32[]{:S(2)}, u32[]{:S(2)}) async-start(f32[8,18,128]{2,1,0:T(8,128)} %broadcast_in_dim.16), calls=%async_computation.1 | async-start | bytes 196608 | tf_op jit(solution)/shard_map/all_to_all | solution.py:629
  91.3 32.5 %collective-permute-start.9 = (f32[2,256,256]{2,1,0:T(8,128)S(1)}, f32[2,256,256]{2,1,0:T(8,128)S(1)}, u32[]{:S(2)}, u32[]{:S(2)}) collective-permute-start(f32[2,256,256]{2,1,0:T(8,128)S(1)} %get-tuple-element.38.own_any), channel_id=1, source_target_pairs={{1,0},{2,1},{3,2},{4,3},{5,4},{6,5},{7,6},{8,7},{9,8},{10,9},{11,1... | collective-permute-start | bytes 1572872 | tf_op jit(solution)/shard_map/ppermute | solution.py:616
  104.1 20.5 %collective-permute-start.10 = (f32[2,256,256]{2,1,0:T(8,128)}, f32[2,256,256]{2,1,0:T(8,128)S(1)}, u32[]{:S(2)}, u32[]{:S(2)}) collective-permute-start(f32[2,256,256]{2,1,0:T(8,128)} %collective-permute-done.8.below_any), channel_id=1, source_target_pairs={{1,0},{2,1},{3,2},{4,3},{5,4},{6,5},{7,6},{8,7},{9,8},{10,9},{11,1... | collective-permute-start | bytes 1572872 | tf_op jit(solution)/shard_map/ppermute | solution.py:616
  110.5 26.1 %all-to-all-start.2 = ((f32[64,18,1,128]{3,2,1,0:T(1,128)}), f32[64,18,1,128]{3,2,1,0:T(1,128)S(1)}, u32[]{:S(2)}, u32[]{:S(2)}) async-start(f32[64,18,1,128]{3,2,1,0:T(1,128)} %broadcast_in_dim.34), calls=%async_computation.2 | async-start | bytes 1179648 | tf_op jit(solution)/shard_map/all_to_all | solution.py:629
  123.9 0.8 copy-start
  124.8 0.8 copy-start.1
  136.6 0.8 copy-start.3

commit v10 on v9

--- a/solution.py
+++ b/solution.py
@@ -155,18 +155,22 @@
 ):
     width = probe_ref.shape[-1]
     live = live_count(counts_ref)
-    *ready, left, measured, right = incoming(
-        [own_any, below_any, right_any, diag_any, probe_any]
+    probe, *ready, left, measured, right = incoming(
+        [probe_any, own_any, below_any, right_any, diag_any]
         + [left_any, measured_any.at[0, 0], right_table_any],
-        [tiles_ref.at[at] for at in range(4)] + [probe_ref, left_ref, measured_ref, right_ref],
+        [probe_ref] + [tiles_ref.at[at] for at in range(4)] + [left_ref, measured_ref, right_ref],
         in_sems,
     )
-    for arrival in ready:
-        arrival()
+    probe()
 
     def both(first):
         slots = (first, first + 1)
         spots = [corner(positions_ref, slot, width) for slot in slots]
+        for slot, (row, col) in zip(slots, spots):
+            for part in range(2):
+                moved_ref[slot, part] = rolled(probe_ref[part], row, col)
+        for arrival in ready:
+            arrival()
         waves = []
         for slot, (row, col) in zip(slots, spots):
             upper, nearer = masks(row, col, width)
@@ -174,7 +178,6 @@
                 patch_ref[slot, part] = wrapped(
                     *[tiles_ref[at, part] for at in range(4)], upper, nearer
                 )
-                moved_ref[slot, part] = rolled(probe_ref[part], row, col)
             patch_r, patch_i = patch_ref[slot, 0], patch_ref[slot, 1]
             probe_r, probe_i = moved_ref[slot, 0], moved_ref[slot, 1]
             kept = slot < live

time: 176 us -> 178 us (1.011)
    all_to_all x3, starting transfers between devices: 37.2 us -> 40.6 us  [exchanged(): lax.all_to_all(pieces, ('row', 'col'), 0, 0, axis_index_groups=groups)]
    ppermute x11, starting transfers between devices: 45.5 us -> 42.4 us  [passed_along(): return lax.ppermute(shard, axis, pairs)]
  transfers between devices with their start and end apart: 14 -> 14, of which waited for: 7 -> 6; matrix products, arithmetic and copies ran while one was open for 2% -> 2% of each run, Pallas kernels for 6% -> 6%
where the time goes in v10:
time: 178 us; the launch traced here: 177 us
  starting transfers between devices  83 us (47%)
  waiting for transfers between devices  36.6 us (21%)
  blocking collectives  27 us (15%)
  Pallas kernels  20.2 us (11%)
  local copies, waits for them, and re-layouts  8.04 us (5%)
    ppermute x11, starting transfers between devices, passed_along(): return lax.ppermute(shard, axis, pairs)  42.4 us
    all_to_all x3, starting transfers between devices, exchanged(): lax.all_to_all(pieces, ('row', 'col'), 0, 0, axis_index_groups=groups)  40.6 us
    all_to_all x2, blocking collectives, exchanged(): lax.all_to_all(pieces, ('row', 'col'), 0, 0, axis_index_groups=groups)  27 us
    all_to_all x3, waiting for transfers between devices, exchanged(): lax.all_to_all(pieces, ('row', 'col'), 0, 0, axis_index_groups=groups)  21.5 us
    ppermute x11, waiting for transfers between devices, passed_along(): return lax.ppermute(shard, axis, pairs)  15.1 us
    pallas_call x1, Pallas kernels, gradient_call(): pl.pallas_call(gradient_kernel, out_shape=(shaped(2, width, width),) * 2...  9.38 us
    pallas_call x1, Pallas kernels, curvature_call(): pl.pallas_call(functools.partial(curvature_kernel, probe_scale=scale, pie...  7.44 us
    unnamed x25, local copies, waits for them, and re-layouts  5.63 us
  transfers between devices with their start and end apart: 14, of which 6 were waited for; matrix products, arithmetic and copies ran while one was open for 2% of the time, Pallas kernels for 6%

profile of v10, /device:TPU:1, one launch (start us, length us, event | category | flops | bytes accessed | tf_op | source)
XLA Modules:
  0.0 176.9 jit_solution(591447800285979650)
XLA Ops:
  0.6 1.3 collective-permute-start
  1.9 8.8 %collective-permute-start.1 = (f32[2,256,256]{2,1,0:T(8,128)}, f32[2,256,256]{2,1,0:T(8,128)S(1)}, u32[]{:S(2)}, u32[]{:S(2)}) collective-permute-start(f32[2,256,256]{2,1,0:T(8,128)} %object_any.1), channel_id=1, source_target_pairs={{1,0},{2,1},{3,2},{4,3},{5,4},{6,5},{7,6},{8,7},{9,8},{10,9},{11,1... | collective-permute-start | bytes 1572872 | tf_op jit(solution)/shard_map/ppermute | solution.py:619
  10.7 0.7 collective-permute-done.below_any
  11.4 9.3 %collective-permute-start.2 = (f32[2,256,256]{2,1,0:T(8,128)S(1)}, f32[2,256,256]{2,1,0:T(8,128)S(1)}, u32[]{:S(2)}, u32[]{:S(2)}) collective-permute-start(f32[2,256,256]{2,1,0:T(8,128)S(1)} %collective-permute-done.below_any), channel_id=1, source_target_pairs={{1,0},{2,1},{3,2},{4,3},{5,4},{6,5},{7,6},{8,7},{9,8},{10,9},{11,1... | collective-permute-start | bytes 1572872 | tf_op jit(solution)/shard_map/ppermute | solution.py:619
  20.7 1.3 copy.25.positions_ref
  22.0 1.9 %collective-permute-start.4 = (f32[2,256,256]{2,1,0:T(8,128)}, f32[2,256,256]{2,1,0:T(8,128)S(1)}, u32[]{:S(2)}, u32[]{:S(2)}) collective-permute-start(f32[2,256,256]{2,1,0:T(8,128)} %prev_own_any.1), channel_id=1, source_target_pairs={{1,0},{2,1},{3,2},{4,3},{5,4},{6,5},{7,6},{8,7},{9,8},{10,9},{11,1... | collective-permute-start | bytes 1572872 | tf_op jit(solution)/shard_map/ppermute | solution.py:619
  24.0 1.3 collective-permute-start.3
  25.3 3.3 %collective-permute-done.2.diag_any = f32[2,256,256]{2,1,0:T(8,128)S(1)} collective-permute-done((f32[2,256,256]{2,1,0:T(8,128)S(1)}, f32[2,256,256]{2,1,0:T(8,128)S(1)}, u32[]{:S(2)}, u32[]{:S(2)}) %collective-permute-start.2) | collective-permute-done | bytes 524320 | tf_op jit(solution)/shard_map/ppermute | solution.py:619
  28.6 0.8 copy-done.11
  29.4 9.4 %gradient_frames.1 = (f32[2,256,256]{2,1,0:T(8,128)}, f32[2,256,256]{2,1,0:T(8,128)}, f32[2,512,256]{2,1,0:T(8,128)}, f32[1024,128]{1,0:T(8,128)}, f32[4,2,256,2...) custom-call(s32[1,1,4,2]{3,2,1,0:T(4,128)} %copy.25.positions_ref, s32[1,32]{1,0:T(1,128)} %counts_ref.3, ...), custom_call_target="tpu_custom_call" | custom-call | flops 10000000000 | bytes 10000000 | tf_op jit(solution)/shard_map/gradient_frames/pallas_call | solution.py:526
  39.0 4.0 %collective-permute-start.5 = (f32[2,512,256]{2,1,0:T(8,128)}, f32[2,512,256]{2,1,0:T(8,128)S(1)}, u32[]{:S(2)}, u32[]{:S(2)}) collective-permute-start(f32[2,512,256]{2,1,0:T(8,128)} %get-tuple-element.34), channel_id=1, source_target_pairs={{0,1},{1,2},{2,3},{3,4},{4,5},{5,6},{6,7},{7,8},{8,9},{9,10},{10,1... | collective-permute-start | bytes 3145736 | tf_op jit(solution)/shard_map/ppermute | solution.py:619
  43.0 13.7 %all-to-all-start = ((f32[64,16,128]{2,1,0:T(8,128)}), f32[64,16,128]{2,1,0:T(8,128)S(1)}, u32[]{:S(2)}, u32[]{:S(2)}) async-start(f32[64,16,128]{2,1,0:T(8,128)} %bitcast.14), calls=%async_computation | async-start | bytes 1048576 | tf_op jit(solution)/shard_map/all_to_all | solution.py:632
  56.8 1.0 copy-done.2
  58.0 5.0 %collective-permute-start.6 = (f32[2,256,256]{2,1,0:T(8,128)S(1)}, f32[2,256,256]{2,1,0:T(8,128)S(1)}, u32[]{:S(2)}, u32[]{:S(2)}) collective-permute-start(f32[2,256,256]{2,1,0:T(8,128)S(1)} %joined.3), channel_id=1, source_target_pairs={{0,32},{32,64},{64,96},{96,128},{128,160},{160,192},{192,224},{224... | collective-permute-start | bytes 1572872 | tf_op jit(solution)/shard_map/ppermute | solution.py:619
  63.1 1.9 %collective-permute-start.7 = (f32[2,256,256]{2,1,0:T(8,128)}, f32[2,256,256]{2,1,0:T(8,128)S(1)}, u32[]{:S(2)}, u32[]{:S(2)}) collective-permute-start(f32[2,256,256]{2,1,0:T(8,128)} %collective-permute-done.3.prev_below_any), channel_id=1, source_target_pairs={{1,0},{2,1},{3,2},{4,3},{5,4},{6,5},{7,6},{8,7},{9,8},{10,9},{11,1... | collective-permute-start | bytes 1572872 | tf_op jit(solution)/shard_map/ppermute | solution.py:619
  65.0 10.9 %collective-permute-done.6 = f32[2,256,256]{2,1,0:T(8,128)S(1)} collective-permute-done((f32[2,256,256]{2,1,0:T(8,128)S(1)}, f32[2,256,256]{2,1,0:T(8,128)S(1)}, u32[]{:S(2)}, u32[]{:S(2)}) %collective-permute-start.6) | collective-permute-done | bytes 524320 | tf_op jit(solution)/shard_map/ppermute | solution.py:619
  76.1 1.5 collective-permute-start.8
  77.7 0.6 broadcast_in_dim.16
  78.3 13.6 %all-to-all-start.1 = ((f32[8,18,128]{2,1,0:T(8,128)}), f32[8,18,128]{2,1,0:T(8,128)S(1)}, u32[]{:S(2)}, u32[]{:S(2)}) async-start(f32[8,18,128]{2,1,0:T(8,128)} %broadcast_in_dim.16), calls=%async_computation.1 | async-start | bytes 196608 | tf_op jit(solution)/shard_map/all_to_all | solution.py:632
  91.9 2.7 %collective-permute-start.9 = (f32[2,256,256]{2,1,0:T(8,128)S(1)}, f32[2,256,256]{2,1,0:T(8,128)S(1)}, u32[]{:S(2)}, u32[]{:S(2)}) collective-permute-start(f32[2,256,256]{2,1,0:T(8,128)S(1)} %get-tuple-element.38.own_any), channel_id=1, source_target_pairs={{1,0},{2,1},{3,2},{4,3},{5,4},{6,5},{7,6},{8,7},{9,8},{10,9},{11,1... | collective-permute-start | bytes 1572872 | tf_op jit(solution)/shard_map/ppermute | solution.py:619
  94.6 10.5 %all-to-all-done.1 = f32[8,18,128]{2,1,0:T(8,128)S(1)} async-done(((f32[8,18,128]{2,1,0:T(8,128)}), f32[8,18,128]{2,1,0:T(8,128)S(1)}, u32[]{:S(2)}, u32[]{:S(2)}) %all-to-all-start.1) | async-done | bytes 73760 | tf_op jit(solution)/shard_map/all_to_all | solution.py:632
  105.1 4.8 %collective-permute-start.10 = (f32[2,256,256]{2,1,0:T(8,128)}, f32[2,256,256]{2,1,0:T(8,128)S(1)}, u32[]{:S(2)}, u32[]{:S(2)}) collective-permute-start(f32[2,256,256]{2,1,0:T(8,128)} %collective-permute-done.8.below_any), channel_id=1, source_target_pairs={{1,0},{2,1},{3,2},{4,3},{5,4},{6,5},{7,6},{8,7},{9,8},{10,9},{11,1... | collective-permute-start | bytes 1572872 | tf_op jit(solution)/shard_map/ppermute | solution.py:619
  109.9 1.1 broadcast_in_dim.34
  111.0 13.2 %all-to-all-start.2 = ((f32[64,18,1,128]{3,2,1,0:T(1,128)}), f32[64,18,1,128]{3,2,1,0:T(1,128)S(1)}, u32[]{:S(2)}, u32[]{:S(2)}) async-start(f32[64,18,1,128]{3,2,1,0:T(1,128)} %broadcast_in_dim.34), calls=%async_computation.2 | async-start | bytes 1179648 | tf_op jit(solution)/shard_map/all_to_all | solution.py:632
  125.1 0.8 copy-done
  126.0 0.8 copy-done.1
  126.8 11.0 %all-to-all-done.2 = f32[64,18,1,128]{3,2,1,0:T(1,128)S(1)} async-done(((f32[64,18,1,128]{3,2,1,0:T(1,128)}), f32[64,18,1,128]{3,2,1,0:T(1,128)S(1)}, u32[]{:S(2)}, u32[]{:S(2)}) %all-to-all-start.2) | async-done | bytes 589856 | tf_op jit(solution)/shard_map/all_to_all | solution.py:632
  137.8 0.8 copy-done.3
  138.6 7.4 %curvature_frames.1 = (f32[2,256,256]{2,1,0:T(8,128)}, f32[2,256,256]{2,1,0:T(8,128)}, f32[1,128]{1,0:T(1,128)}) custom-call(s32[1,1,4,2]{3,2,1,0:T(4,128)} %copy.25.positions_ref, s32[1,32]{1,0:T(1,128)} %counts_ref.3, f32[1]{0:T(128)} %bitcast.12.prev_norm_ref, f32[2,256,256]{2,1,0:T(8,128)} %copy-done.5, f32[2,256,256]{2,1,0:T(8,128)} %collective-permute-done.8.below_any, ...), custom_call_target="tpu_custom_call" | custom-call | flops 5000000000 | bytes 10000000 | tf_op jit(solution)/shard_map/curvature_frames/pallas_call | solution.py:573
  146.7 12.5 %all_to_all.25 = f32[32,1,128]{2,1,0:T(1,128)S(1)} all-to-all(f32[32,1,128]{2,1,0:T(1,128)S(1)} %broadcast_in_dim.36), channel_id=1, replica_groups={{0,1,32,33,64,65,96,97,128,129,160,161,192,193,224,225,256,257,288,289,..., dimensions={0} | all-to-all | bytes 32768 | tf_op jit(solution)/shard_map/all_to_all | solution.py:632
  159.2 14.5 %all_to_all.26.gathered_any = f32[16,1,128]{2,1,0:T(1,128)} all-to-all(f32[16,1,128]{2,1,0:T(1,128)S(1)} %broadcast_in_dim.37), channel_id=1, replica_groups={{0,2,4,6,8,10,12,14,16,18,20,22,24,26,28,30},{1,3,5,7,9,11,13,15,17,19,..., dimensions={0} | all-to-all | bytes 16384 | tf_op jit(solution)/shard_map/all_to_all | solution.py:632
  173.7 3.0 %update.1 = (f32[2,256,256]{2,1,0:T(8,128)}, f32[2,256,256]{2,1,0:T(8,128)}, f32[1,1]{1,0:T(1,128)}, f32[1,1,4]{2,1,0:T(1,128)}) custom-call(f32[16,1,128]{2,1,0:T(1,128)} %all_to_all.26.gathered_any, f32[1,128]{1,0:T(1,128)} %get-tuple-element.47.sums_any, f32[2,256,256]{2,1,0:T(8,128)} %object_any.1, f32[2,256,256]{2,1,0:T(8,128)} %get-tuple-element.26.direction_any, ...), custom_call_target="tpu_custom_call" | custom-call | flops 1000000 | bytes 10000000 | tf_op jit(solution)/shard_map/update/pallas_call | solution.py:599
  (39 shorter events, 1.6 us)
Async XLA Ops:
  0.6 10.8 %collective-permute-start = (f32[2,256,256]{2,1,0:T(8,128)}, f32[2,256,256]{2,1,0:T(8,128)S(1)}, u32[]{:S(2)}, u32[]{:S(2)}) collective-permute-start(f32[2,256,256]{2,1,0:T(8,128)} %object_any.1), channel_id=1, source_target_pairs={{32,0},{64,32},{96,64},{128,96},{160,128},{192,160},{224,192},{256... | collective-permute-start | bytes 1572872 | tf_op jit(solution)/shard_map/ppermute | solution.py:619
  1.9 23.3 %collective-permute-start.1 = (f32[2,256,256]{2,1,0:T(8,128)}, f32[2,256,256]{2,1,0:T(8,128)S(1)}, u32[]{:S(2)}, u32[]{:S(2)}) collective-permute-start(f32[2,256,256]{2,1,0:T(8,128)} %object_any.1), channel_id=1, source_target_pairs={{1,0},{2,1},{3,2},{4,3},{5,4},{6,5},{7,6},{8,7},{9,8},{10,9},{11,1... | collective-permute-start | bytes 1572872 | tf_op jit(solution)/shard_map/ppermute | solution.py:619
  11.4 17.1 %copy-start.9 = (f32[2,256,256]{2,1,0:T(8,128)}, f32[2,256,256]{2,1,0:T(8,128)S(1)}, u32[]{:S(2)}) copy-start(f32[2,256,256]{2,1,0:T(8,128)S(1)} %collective-permute-done.below_any) | copy-start | bytes 1572868
  11.4 17.1 %collective-permute-start.2 = (f32[2,256,256]{2,1,0:T(8,128)S(1)}, f32[2,256,256]{2,1,0:T(8,128)S(1)}, u32[]{:S(2)}, u32[]{:S(2)}) collective-permute-start(f32[2,256,256]{2,1,0:T(8,128)S(1)} %collective-permute-done.below_any), channel_id=1, source_target_pairs={{1,0},{2,1},{3,2},{4,3},{5,4},{6,5},{7,6},{8,7},{9,8},{10,9},{11,1... | collective-permute-start | bytes 1572872 | tf_op jit(solution)/shard_map/ppermute | solution.py:619
  22.0 16.7 %collective-permute-start.4 = (f32[2,256,256]{2,1,0:T(8,128)}, f32[2,256,256]{2,1,0:T(8,128)S(1)}, u32[]{:S(2)}, u32[]{:S(2)}) collective-permute-start(f32[2,256,256]{2,1,0:T(8,128)} %prev_own_any.1), channel_id=1, source_target_pairs={{1,0},{2,1},{3,2},{4,3},{5,4},{6,5},{7,6},{8,7},{9,8},{10,9},{11,1... | collective-permute-start | bytes 1572872 | tf_op jit(solution)/shard_map/ppermute | solution.py:619
  24.0 15.1 %collective-permute-start.3 = (f32[2,256,256]{2,1,0:T(8,128)}, f32[2,256,256]{2,1,0:T(8,128)}, u32[]{:S(2)}, u32[]{:S(2)}) collective-permute-start(f32[2,256,256]{2,1,0:T(8,128)} %prev_own_any.1), channel_id=1, source_target_pairs={{32,0},{64,32},{96,64},{128,96},{160,128},{192,160},{224,192},{256... | collective-permute-start | bytes 1572872 | tf_op jit(solution)/shard_map/ppermute | solution.py:619
  25.3 3.3 %copy-start.10 = (f32[2,256,256]{2,1,0:T(8,128)}, f32[2,256,256]{2,1,0:T(8,128)S(1)}, u32[]{:S(2)}) copy-start(f32[2,256,256]{2,1,0:T(8,128)S(1)} %collective-permute-done.1.right_any) | copy-start | bytes 1572868
  28.6 0.8 copy-start.11
  38.8 19.2 %copy-start.7 = (f32[2,256,256]{2,1,0:T(8,128)}, f32[2,256,256]{2,1,0:T(8,128)S(1)}, u32[]{:S(2)}) copy-start(f32[2,256,256]{2,1,0:T(8,128)S(1)} %collective-permute-done.4.prev_right_any) | copy-start | bytes 1572868
  39.0 17.7 %collective-permute-start.5 = (f32[2,512,256]{2,1,0:T(8,128)}, f32[2,512,256]{2,1,0:T(8,128)S(1)}, u32[]{:S(2)}, u32[]{:S(2)}) collective-permute-start(f32[2,512,256]{2,1,0:T(8,128)} %get-tuple-element.34), channel_id=1, source_target_pairs={{0,1},{1,2},{2,3},{3,4},{4,5},{5,6},{6,7},{7,8},{8,9},{9,10},{10,1... | collective-permute-start | bytes 3145736 | tf_op jit(solution)/shard_map/ppermute | solution.py:619
  43.0 34.5 %all-to-all-start = ((f32[64,16,128]{2,1,0:T(8,128)}), f32[64,16,128]{2,1,0:T(8,128)S(1)}, u32[]{:S(2)}, u32[]{:S(2)}) async-start(f32[64,16,128]{2,1,0:T(8,128)} %bitcast.14), calls=%async_computation | async-start | bytes 1048576 | tf_op jit(solution)/shard_map/all_to_all | solution.py:632
  56.8 1.0 copy-start.2
  57.8 18.0 %copy-start.4 = (f32[2,256,256]{2,1,0:T(8,128)S(1)}, f32[2,256,256]{2,1,0:T(8,128)}, u32[]{:S(2)}) copy-start(f32[2,256,256]{2,1,0:T(8,128)} %prev_own_any.1) | copy-start | bytes 1572868
  57.8 18.0 %copy-start.6 = (f32[2,256,256]{2,1,0:T(8,128)S(1)}, f32[2,256,256]{2,1,0:T(8,128)}, u32[]{:S(2)}) copy-start(f32[2,256,256]{2,1,0:T(8,128)} %get-tuple-element.30) | copy-start | bytes 1572868
  58.0 17.8 %collective-permute-start.6 = (f32[2,256,256]{2,1,0:T(8,128)S(1)}, f32[2,256,256]{2,1,0:T(8,128)S(1)}, u32[]{:S(2)}, u32[]{:S(2)}) collective-permute-start(f32[2,256,256]{2,1,0:T(8,128)S(1)} %joined.3), channel_id=1, source_target_pairs={{0,32},{32,64},{64,96},{96,128},{128,160},{160,192},{192,224},{224... | collective-permute-start | bytes 1572872 | tf_op jit(solution)/shard_map/ppermute | solution.py:619
  63.1 13.0 %collective-permute-start.7 = (f32[2,256,256]{2,1,0:T(8,128)}, f32[2,256,256]{2,1,0:T(8,128)S(1)}, u32[]{:S(2)}, u32[]{:S(2)}) collective-permute-start(f32[2,256,256]{2,1,0:T(8,128)} %collective-permute-done.3.prev_below_any), channel_id=1, source_target_pairs={{1,0},{2,1},{3,2},{4,3},{5,4},{6,5},{7,6},{8,7},{9,8},{10,9},{11,1... | collective-permute-start | bytes 1572872 | tf_op jit(solution)/shard_map/ppermute | solution.py:619
  76.0 49.0 %copy-start.5 = (f32[2,256,256]{2,1,0:T(8,128)}, f32[2,256,256]{2,1,0:T(8,128)S(1)}, u32[]{:S(2)}) copy-start(f32[2,256,256]{2,1,0:T(8,128)S(1)} %get-tuple-element.38.own_any) | copy-start | bytes 1572868
  76.0 49.0 %copy-start.8 = (f32[2,256,256]{2,1,0:T(8,128)}, f32[2,256,256]{2,1,0:T(8,128)S(1)}, u32[]{:S(2)}) copy-start(f32[2,256,256]{2,1,0:T(8,128)S(1)} %collective-permute-done.7.prev_diag_any) | copy-start | bytes 1572868
  76.1 18.5 %collective-permute-start.8 = (f32[2,256,256]{2,1,0:T(8,128)S(1)}, f32[2,256,256]{2,1,0:T(8,128)}, u32[]{:S(2)}, u32[]{:S(2)}) collective-permute-start(f32[2,256,256]{2,1,0:T(8,128)S(1)} %get-tuple-element.38.own_any), channel_id=1, source_target_pairs={{32,0},{64,32},{96,64},{128,96},{160,128},{192,160},{224,192},{256... | collective-permute-start | bytes 1572872 | tf_op jit(solution)/shard_map/ppermute | solution.py:619
  78.3 26.8 %all-to-all-start.1 = ((f32[8,18,128]{2,1,0:T(8,128)}), f32[8,18,128]{2,1,0:T(8,128)S(1)}, u32[]{:S(2)}, u32[]{:S(2)}) async-start(f32[8,18,128]{2,1,0:T(8,128)} %broadcast_in_dim.16), calls=%async_computation.1 | async-start | bytes 196608 | tf_op jit(solution)/shard_map/all_to_all | solution.py:632
  91.9 33.1 %collective-permute-start.9 = (f32[2,256,256]{2,1,0:T(8,128)S(1)}, f32[2,256,256]{2,1,0:T(8,128)S(1)}, u32[]{:S(2)}, u32[]{:S(2)}) collective-permute-start(f32[2,256,256]{2,1,0:T(8,128)S(1)} %get-tuple-element.38.own_any), channel_id=1, source_target_pairs={{1,0},{2,1},{3,2},{4,3},{5,4},{6,5},{7,6},{8,7},{9,8},{10,9},{11,1... | collective-permute-start | bytes 1572872 | tf_op jit(solution)/shard_map/ppermute | solution.py:619
  105.1 20.8 %collective-permute-start.10 = (f32[2,256,256]{2,1,0:T(8,128)}, f32[2,256,256]{2,1,0:T(8,128)S(1)}, u32[]{:S(2)}, u32[]{:S(2)}) collective-permute-start(f32[2,256,256]{2,1,0:T(8,128)} %collective-permute-done.8.below_any), channel_id=1, source_target_pairs={{1,0},{2,1},{3,2},{4,3},{5,4},{6,5},{7,6},{8,7},{9,8},{10,9},{11,1... | collective-permute-start | bytes 1572872 | tf_op jit(solution)/shard_map/ppermute | solution.py:619
  111.0 26.7 %all-to-all-start.2 = ((f32[64,18,1,128]{3,2,1,0:T(1,128)}), f32[64,18,1,128]{3,2,1,0:T(1,128)S(1)}, u32[]{:S(2)}, u32[]{:S(2)}) async-start(f32[64,18,1,128]{3,2,1,0:T(1,128)} %broadcast_in_dim.34), calls=%async_computation.2 | async-start | bytes 1179648 | tf_op jit(solution)/shard_map/all_to_all | solution.py:632
  125.1 0.8 copy-start
  126.0 0.8 copy-start.1
  137.8 0.8 copy-start.3
